TPU v7x, 128 devices: a whole 4x4x4 slice. The times are simulated.
128 devices in a mesh: plane: 16 (over x, z), fourier: 8 (over y, core).
Axes of the slice: x: 4, y: 4, z: 4, core: 2. Of those that a mesh axis runs over, the one named last changes fastest.
Arguments:
- velocity: float32 [3, 128, 49, 128, 128], P(None, 'fourier', None, 'plane'), may hold values from -1.5 to 1.5
- metric: float32 [2, 128, 128], P(None, 'plane'), may hold values from 0.5 to 2
Outputs:
- pressure: float32 [128, 49, 128, 128], P('fourier', None, 'plane')
- residual: float32 [128, 49, 128, 128], P('fourier', None, 'plane')
All inputs are finite; a program needn't handle non-finite values.
Results may differ from a plain program's by a relative error of at most 0.00065.
Values sent between devices are 32-bit elements; how exact they have to be, the bound alone decides.
No kernel may reach another device: no remote copies, remote signals or barrier semaphores. Data moves between devices by JAX's collectives and lax.ppermute only.
A program may use at most 128 MiB of HBM per device.

v0:
```python
import jax
import jax.numpy as jnp
import numpy as np
from jax import lax
from jax.sharding import PartitionSpec as P

PENALTY = 10.0
BETA = 0.5
MASS_REF = 0.08
HIGHEST_PRECISION = lax.Precision.HIGHEST


def padded_2(value, sides, width):
    for axis, dim in sides:
        size, length = (lax.axis_size(axis), value.shape[dim])
        up = [(i, (i + 1) % size) for i in range(size - 1)]
        down = [(j, i) for i, j in up]
        last = lax.slice_in_dim(value, length - width, length, axis=dim)
        leading = lax.slice_in_dim(value, 0, width, axis=dim)
        before = lax.ppermute(last, axis, up)
        after = lax.ppermute(leading, axis, down)
        value = jnp.concatenate([before, value, after], axis=dim)
    return value


def node_tables():
    gll_nodes = np.array(
        [
            -1.0,
            -0.830223896278567,
            -0.4688487934707142,
            0.0,
            0.4688487934707142,
            0.830223896278567,
            1.0,
        ]
    )
    gll_weights = np.array(
        [
            1.0 / 21.0,
            0.2768260473615659,
            0.4317453812098627,
            0.4876190476190476,
            0.4317453812098627,
            0.2768260473615659,
            1.0 / 21.0,
        ]
    )
    identity = np.eye(7)
    differ = gll_nodes[:, None] - gll_nodes[None, :] + identity
    bary_weights = 1.0 / np.prod(differ, axis=1)
    off_diag = np.where(identity > 0.5, 0.0, bary_weights[None, :] / bary_weights[:, None] / differ)
    deriv_one = off_diag - identity * off_diag.sum(axis=1)[:, None]
    weight_diag = identity * gll_weights[None, :]
    stiff_one = deriv_one.T @ weight_diag @ deriv_one
    side_flag = np.where((np.arange(7) == 0) | (np.arange(7) == 6), 1.0, 0.0)
    rim_count = (side_flag[:, None] + side_flag[None, :]).reshape(49)
    stiff_x = np.kron(stiff_one, weight_diag)
    stiff_y = np.kron(weight_diag, stiff_one)
    system = jnp.asarray(stiff_x + stiff_y + PENALTY * np.eye(49) * rim_count[None, :], jnp.float32)
    lower = lax.linalg.cholesky(system)
    ident_big = jnp.eye(49, dtype=jnp.float32)
    half_solve = lax.linalg.triangular_solve(lower, ident_big, left_side=True, lower=True)
    block_inverse = lax.linalg.triangular_solve(
        lower, half_solve, left_side=True, lower=True, transpose_a=True
    )
    tables = (
        np.kron(deriv_one, identity),
        np.kron(identity, deriv_one),
        stiff_x,
        stiff_y,
        np.kron(gll_weights, gll_weights),
    )
    return tuple((jnp.asarray(table, jnp.float32) for table in tables)) + (block_inverse,)


def mode_tables(length):
    index = np.arange(length)
    wavenum = index // 2
    wavenum[1] = length // 2
    angles = 2.0 * np.pi * np.outer(index, wavenum) / length
    use_cos = (index % 2 == 0) | (index == 1)
    basis = np.where(use_cos[None, :], np.cos(angles), np.sin(angles))
    factor = np.full(length, 2.0 / length)
    factor[:2] = 1.0 / length
    forward = factor[:, None] * basis.T
    modal_diff = np.zeros((length, length))
    even = np.arange(2, length, 2)
    modal_diff[even, even + 1] = BETA * wavenum[even]
    modal_diff[even + 1, even] = -BETA * wavenum[even]
    plane_diff = basis @ modal_diff @ forward
    wave_sq = (BETA * wavenum) ** 2
    tables = (basis, forward, modal_diff, plane_diff, wave_sq)
    return tuple((jnp.asarray(table, jnp.float32) for table in tables))


def advection(velocity, scale_x, scale_y, basis, plane_diff, diff_x, diff_y):
    physical = jnp.einsum("qc,xcnij->xqnij", basis, velocity, precision=HIGHEST_PRECISION)
    along_z = jnp.einsum("qp,xpnij->xqnij", plane_diff, physical, precision=HIGHEST_PRECISION)
    along_x = jnp.einsum("mn,xqnij->xqmij", diff_x, physical, precision=HIGHEST_PRECISION) * scale_x
    along_y = jnp.einsum("mn,xqnij->xqmij", diff_y, physical, precision=HIGHEST_PRECISION) * scale_y
    return physical[0] * along_x + physical[1] * along_y + physical[2] * along_z


def apply_operator(field, west_row, east_row, scale_x, scale_y, wave_sq, stiff_x, stiff_y, masses):
    ratio = scale_x / scale_y
    stiffness = ratio * jnp.einsum("mn,cnij->cmij", stiff_x, field, precision=HIGHEST_PRECISION)
    stiffness = (
        stiffness + jnp.einsum("mn,cnij->cmij", stiff_y, field, precision=HIGHEST_PRECISION) / ratio
    )
    stiffness = (
        stiffness
        + wave_sq[:, None, None, None] * masses[None, :, None, None] / (scale_x * scale_y) * field
    )
    lattice = field.reshape(field.shape[0], 7, 7, field.shape[2], field.shape[3])
    jumps = jnp.zeros_like(lattice)
    jumps = jumps.at[:, 0].add(lattice[:, 0] - west_row).at[:, 6].add(lattice[:, 6] - east_row)
    south_row = jnp.pad(lattice[:, :, 6], ((0, 0), (0, 0), (0, 0), (1, 0)))[..., :-1]
    north_row = jnp.pad(lattice[:, :, 0], ((0, 0), (0, 0), (0, 0), (0, 1)))[..., 1:]
    jumps = (
        jumps.at[:, :, 0]
        .add(lattice[:, :, 0] - south_row)
        .at[:, :, 6]
        .add(lattice[:, :, 6] - north_row)
    )
    return stiffness + PENALTY * jumps.reshape(field.shape)


def precondition(resid, scale_x, scale_y, wave_sq, block_inverse):
    divisor = 0.5 * (scale_x / scale_y + scale_y / scale_x) + wave_sq[:, None, None] * MASS_REF / (
        scale_x * scale_y
    )
    return (
        jnp.einsum("mn,cnij->cmij", block_inverse, resid, precision=HIGHEST_PRECISION)
        / divisor[:, None]
    )


def inner(left, right):
    return jnp.sum(left * right, axis=(1, 2, 3))


def widen(vector):
    return vector[:, None, None, None]


def body(velocity, metric):
    diff_x, diff_y, stiff_x, stiff_y, masses, block_inverse = node_tables()
    modes_here = velocity.shape[1]
    rows_here = velocity.shape[3]
    basis, forward, modal_diff, plane_diff, wave_all = mode_tables(
        modes_here * lax.axis_size("fourier")
    )
    first_mode = lax.axis_index("fourier") * modes_here
    part_rows = rows_here // lax.axis_size("fourier")
    wave_sq = lax.dynamic_slice_in_dim(wave_all, first_mode, modes_here)
    scale_x = metric[0]
    scale_y = metric[1]
    gathered = lax.all_to_all(velocity, "fourier", split_axis=3, concat_axis=1, tiled=True)
    rows_metric = lax.dynamic_slice_in_dim(
        metric, lax.axis_index("fourier") * part_rows, part_rows, 1
    )
    advect = advection(gathered, rows_metric[0], rows_metric[1], basis, plane_diff, diff_x, diff_y)
    spectral = jnp.einsum("cq,xqnij->xcnij", forward, advect, precision=HIGHEST_PRECISION)
    returned = lax.all_to_all(spectral, "fourier", split_axis=1, concat_axis=3, tiled=True)
    local_diff = lax.dynamic_slice(modal_diff, (first_mode, first_mode), (modes_here, modes_here))
    part_x = jnp.einsum("mn,cnij->cmij", diff_x, returned[0], precision=HIGHEST_PRECISION)
    part_y = jnp.einsum("mn,cnij->cmij", diff_y, returned[1], precision=HIGHEST_PRECISION)
    part_z = jnp.einsum("cd,dnij->cnij", local_diff, returned[2], precision=HIGHEST_PRECISION)
    divergence = scale_x * part_x + scale_y * part_y + part_z
    source = -(masses[:, None, None] / (scale_x * scale_y)) * divergence

    def operate(field):
        rim_nodes = jnp.concatenate([field[:, 0:7], field[:, 42:49]], axis=1)
        padded = padded_2(rim_nodes, (("plane", 2),), 1)
        west_row = padded[:, 7:14, 0:rows_here]
        east_row = padded[:, 0:7, 2 : rows_here + 2]
        return apply_operator(
            field, west_row, east_row, scale_x, scale_y, wave_sq, stiff_x, stiff_y, masses
        )

    resid = source
    search_a = precondition(resid, scale_x, scale_y, wave_sq, block_inverse)
    image_a = operate(search_a)
    norm_a, along_a = lax.psum((inner(image_a, image_a), inner(resid, image_a)), "plane")
    step_a = along_a / norm_a
    pressure = widen(step_a) * search_a
    resid = resid - widen(step_a) * image_a
    search_b = precondition(resid, scale_x, scale_y, wave_sq, block_inverse)
    image_b = operate(search_b)
    margin_sum = lax.psum(inner(image_b, image_a), "plane")
    proj_coef = margin_sum / norm_a
    search_b = search_b - widen(proj_coef) * search_a
    image_b = image_b - widen(proj_coef) * image_a
    norm_b, along_b = lax.psum((inner(image_b, image_b), inner(resid, image_b)), "plane")
    step_b = along_b / norm_b
    pressure = pressure + widen(step_b) * search_b
    residual = resid - widen(step_b) * image_b
    return (pressure, residual)


def solution(mesh):
    in_specs = (P(None, "fourier", None, "plane", None), P(None, "plane", None))
    out_specs = (P("fourier", None, "plane", None), P("fourier", None, "plane", None))
    return jax.shard_map(body, mesh=mesh, in_specs=in_specs, out_specs=out_specs, check_vma=False)
```

profile of v0, /device:TPU:0, one launch (start us, length us, event | category | flops | bytes accessed | tf_op | source)
XLA Modules:
  0.0 625.8 jit_solution(17617862335093592062)
XLA Ops:
  0.6 9.3 %copy.150 = f32[3,16,49,8,128]{4,1,2,0,3:T(8,128)} copy(f32[3,16,49,8,128]{4,3,2,1,0:T(8,128)} %param.29) | data formatting | bytes 19267584 | tf_op args[0]
  15.2 107.9 %all-to-all-done = f32[3,16,49,8,128]{4,1,2,0,3:T(8,128)} async-done(((f32[3,16,49,8,128]{4,1,2,0,3:T(8,128)}), f32[3,16,49,8,128]{4,1,2,0,3:T(8,128)}, u32[]{:S(2)}, u32[]{:S(2)}) %all-to-all-start) | async-done | bytes 9633824 | tf_op jit(solution)/shard_map/all_to_all | solution.py:159
  128.1 9.6 %fusion.79 = f32[128,3,49,128]{3,0,2,1:T(8,128)S(1)} fusion(f32[128,128,1,1]{1,0,3,2:T(8,128)S(1)} %copy-done.13, f32[3,128,49,128]{3,1,2,0:T(8,128)S(1)} %bitcast.271), kind=kOutput, calls=%fused_computation.151 | convolution fusion | flops 3699376128 | bytes 19333120 | tf_op jit(solution)/shard_map/qc,xcnij->xqnij/dot_general | solution.py:98
  141.2 18.0 %fusion.70 = f32[3,49,128,128]{3,2,1,0:T(8,128)} fusion(f32[128,128,1,1]{1,0,3,2:T(8,128)S(1)} %copy-done.12, f32[128,3,49,128]{3,0,2,1:T(8,128)S(1)} %fusion.79), kind=kOutput, calls=%fused_computation.143 | convolution fusion | flops 3699376128 | bytes 19333120 | tf_op jit(solution)/shard_map/qp,xpnij->xqnij/dot_general | solution.py:99
  159.3 10.8 %copy.158 = f32[3,49,128,128]{2,1,3,0:T(8,128)} copy(f32[3,49,128,128]{3,2,1,0:T(8,128)} %fusion.70) | data formatting | bytes 19267584 | tf_op jit(solution)/shard_map/qp,xpnij->xqnij/dot_general | solution.py:99
  170.1 7.9 %slice_bitcast_fusion.7 = (f32[128,49,128]{2,0,1:T(8,128)}, f32[128,49,128]{2,0,1:T(8,128)}, f32[128,49,128]{2,0,1:T(8,128)S(1)}) fusion(f32[3,128,49,1,128]{4,1,2,0,3:T(8,128)} %bitcast.262), kind=kLoop, calls=%fused_computation.35 | loop fusion | bytes 19267584 | tf_op jit(solution)/shard_map/mul | solution.py:102
  178.0 5.7 copy.152
  191.2 22.9 %fusion = f32[3,128,128,49]{2,3,1,0:T(8,128)} fusion(f32[49,49,1,1]{1,0,3,2:T(8,128)S(1)} %copy-done.7, f32[3,128,49,128]{3,1,2,0:T(8,128)S(1)} %bitcast.265), kind=kOutput, calls=%fused_computation | convolution fusion | flops 1416167424 | bytes 19277188 | tf_op jit(solution)/shard_map/mn,xqnij->xqmij/dot_general | solution.py:101
  214.1 30.9 %fusion.5 = f32[3,128,49,128]{3,2,1,0:T(8,128)} fusion(f32[3,49,128,128]{2,1,3,0:T(8,128)} %copy.158, f32[3,128,128,49]{2,3,1,0:T(8,128)} %fusion, f32[128,49,128]{2,1,0:T(8,128)} %copy.156, f32[128]{0:T(128)S(1)} %get-tuple-element.144, f32[128,49,128]{2,1,0:T(8,128)} %copy.154, f32[128]{0:T(128)S(1)} %get-tuple-element.143, f32[128,49,128]{2,1,0:T(8,128)} %copy.152, ...), kind=kOutput, calls=%fused_computation.6 | convolution fusion | flops 1433026560 | bytes 48179588 | tf_op jit(solution)/shard_map/mn,xqnij->xqmij/dot_general | solution.py:100
  245.0 20.4 %fusion.25 = f32[3,128,49,1,128]{1,4,2,0,3:T(8,128)} fusion(f32[128,128,1,1]{1,0,3,2:T(8,128)S(1)} %copy-done.11, f32[3,128,49,128]{3,2,1,0:T(8,128)} %fusion.5), kind=kOutput, calls=%fused_computation.32 | convolution fusion | flops 3699376128 | bytes 19333120 | tf_op jit(solution)/shard_map/cq,xqnij->xcnij/dot_general | solution.py:164
  265.4 20.7 %copy.160 = f32[3,128,49,1,128]{4,3,2,0,1:T(1,128)} copy(f32[3,128,49,1,128]{1,4,2,0,3:T(8,128)} %fusion.25) | data formatting | bytes 19267584 | tf_op jit(solution)/shard_map/cq,xqnij->xcnij/transpose | solution.py:164
  286.2 5.6 all-to-all-start.1
  303.0 96.4 %all-to-all-done.1 = f32[3,128,49,1,128]{4,3,2,0,1:T(1,128)} async-done(((f32[3,128,49,1,128]{4,3,2,0,1:T(1,128)}), f32[3,128,49,1,128]{4,3,2,0,1:T(1,128)}, u32[]{:S(2)}, u32[]{:S(2)}) %all-to-all-start.1) | async-done | bytes 9633824 | tf_op jit(solution)/shard_map/all_to_all | solution.py:165
  399.3 8.8 %copy.161 = f32[3,128,49,1,128]{4,1,2,0,3:T(8,128)} copy(f32[3,128,49,1,128]{4,3,2,0,1:T(1,128)} %all-to-all-done.1) | data formatting | bytes 19267584 | tf_op jit(solution)/shard_map/all_to_all | solution.py:165
  408.1 9.4 %copy.301 = f32[3,8,16,49,1,128]{5,3,1,2,4,0:T(8,128)S(1)} copy(f32[3,8,16,49,1,128]{5,2,1,3,0,4:T(8,128)} %bitcast.270) | data formatting | bytes 19267584 | tf_op jit(solution)/shard_map/all_to_all | solution.py:165
  432.2 5.9 fusion.23
  445.4 5.5 fusion.15
  450.9 5.5 fusion.17
  461.6 39.6 %all-reduce.7 = (f32[16]{0:T(128)S(1)}, f32[16]{0:T(128)S(1)}) all-reduce(f32[16]{0:T(128)S(1)} %get-tuple-element.111, f32[16]{0:T(128)S(1)} %get-tuple-element.110), channel_id=1, replica_groups=mesh['plane'=16,'fourier'=8] {'plane'}, use_global_device_ids=true, to_apply=%region_3.4 | all-reduce | flops 32 | bytes 256 | tf_op jit(solution)/shard_map/psum | solution.py:185
  510.6 5.7 fusion.11
  516.4 5.5 fusion.13
  537.0 37.9 %psum.37 = f32[16]{0:T(128)S(1)} all-reduce(f32[16]{0:T(128)S(1)} %get-tuple-element.117), channel_id=1, replica_groups=mesh['plane'=16,'fourier'=8] {'plane'}, use_global_device_ids=true, to_apply=%region_7.8 | all-reduce | flops 16 | bytes 128 | tf_op jit(solution)/shard_map/psum | solution.py:191
  574.8 6.0 multiply_reduce_fusion
  580.9 35.4 %all-reduce.6 = (f32[16]{0:T(128)S(1)}, f32[16]{0:T(128)S(1)}) all-reduce(f32[16]{0:T(128)S(1)} %get-tuple-element.109, f32[16]{0:T(128)S(1)} %get-tuple-element.108), channel_id=1, replica_groups=mesh['plane'=16,'fourier'=8] {'plane'}, use_global_device_ids=true, to_apply=%region_9.10 | all-reduce | flops 32 | bytes 256 | tf_op jit(solution)/shard_map/psum | solution.py:195
  (107 shorter events, 92.8 us)
Async XLA Ops:
  9.9 5.2 copy-start.14
  9.9 113.2 %all-to-all-start = ((f32[3,16,49,8,128]{4,1,2,0,3:T(8,128)}), f32[3,16,49,8,128]{4,1,2,0,3:T(8,128)}, u32[]{:S(2)}, u32[]{:S(2)}) async-start(f32[3,16,49,8,128]{4,1,2,0,3:T(8,128)} %copy.150), calls=%async_computation | async-start | bytes 19267584 | tf_op jit(solution)/shard_map/all_to_all | solution.py:159
  123.1 5.0 copy-start.13
  128.1 13.2 %copy-start.12 = (f32[128,128,1,1]{1,0,3,2:T(8,128)S(1)}, f32[128,128,1,1]{1,0,3,2:T(8,128)}, u32[]{:S(2)}) copy-start(f32[128,128,1,1]{1,0,3,2:T(8,128)} %constant.290) | copy-start | bytes 196612
  170.1 21.1 %slice-start = ((s8[9633792]{0:T(1024)(128)(4,1)}), s8[4194304]{0:T(1024)(128)(4,1)S(1)}, s32[]{:S(2)}) async-start(s8[9633792]{0:T(1024)(128)(4,1)} %bitcast.263), calls=%async_computation.2 | async-start | bytes 8388608
  170.1 21.1 %slice-start.1 = ((s8[9633792]{0:T(1024)(128)(4,1)}), s8[4194304]{0:T(1024)(128)(4,1)S(1)}, s32[]{:S(2)}) async-start(s8[9633792]{0:T(1024)(128)(4,1)} %bitcast.263), calls=%async_computation.3 | async-start | bytes 8388608
  178.0 5.7 copy-start.6
  183.7 7.5 %slice-start.2 = ((s8[9633792]{0:T(1024)(128)(4,1)}), s8[1245184]{0:T(1024)(128)(4,1)S(1)}, s32[]{:S(2)}) async-start(s8[9633792]{0:T(1024)(128)(4,1)} %bitcast.263), calls=%async_computation.4 | async-start | bytes 2490368
  187.4 3.8 copy-start.7
  191.2 22.9 %copy-start.8 = (f32[49,49,1,1]{1,0,3,2:T(8,128)S(1)}, f32[49,49,1,1]{1,0,3,2:T(8,128)}, u32[]{:S(2)}) copy-start(f32[49,49,1,1]{1,0,3,2:T(8,128)} %constant.288) | copy-start | bytes 28816
  214.1 30.9 %copy-start.11 = (f32[128,128,1,1]{1,0,3,2:T(8,128)S(1)}, f32[128,128,1,1]{1,0,3,2:T(8,128)}, u32[]{:S(2)}) copy-start(f32[128,128,1,1]{1,0,3,2:T(8,128)} %constant.291) | copy-start | bytes 196612
  286.2 16.0 %copy-start.16 = (f32[128]{0:T(128)S(1)}, f32[128]{0:T(128)}, u32[]{:S(2)}) copy-start(f32[128]{0:T(128)} %constant.269.clone) | copy-start | bytes 1540
  286.2 16.5 %copy-start.15 = (f32[49]{0:T(128)S(1)}, f32[49]{0:T(128)}, u32[]{:S(2)}) copy-start(f32[49]{0:T(128)} %constant.264.clone) | copy-start | bytes 592
  286.2 113.2 %all-to-all-start.1 = ((f32[3,128,49,1,128]{4,3,2,0,1:T(1,128)}), f32[3,128,49,1,128]{4,3,2,0,1:T(1,128)}, u32[]{:S(2)}, u32[]{:S(2)}) async-start(f32[3,128,49,1,128]{4,3,2,0,1:T(1,128)} %copy.160), calls=%async_computation.1 | async-start | bytes 19267584 | tf_op jit(solution)/shard_map/all_to_all | solution.py:165
  438.1 19.7 %copy-start.2 = (f32[16,8,128,49]{2,3,1,0:T(8,128)}, f32[16,8,128,49]{2,3,1,0:T(8,128)S(1)}, u32[]{:S(2)}) copy-start(f32[16,8,128,49]{2,3,1,0:T(8,128)S(1)} %fusion.23) | copy-start | bytes 9633796
  438.7 6.7 %copy-start.10 = (f32[49,49,1,1]{1,0,3,2:T(8,128)S(1)}, f32[49,49,1,1]{1,0,3,2:T(8,128)}, u32[]{:S(2)}) copy-start(f32[49,49,1,1]{1,0,3,2:T(8,128)} %constant.293) | copy-start | bytes 28816
  439.5 17.4 %collective-permute-start.1 = (f32[16,14,1,128]{3,2,0,1:T(1,128)S(1)}, f32[16,14,1,128]{3,2,0,1:T(1,128)S(1)}, u32[]{:S(2)}, u32[]{:S(2)}) collective-permute-start(f32[16,14,1,128]{3,2,0,1:T(1,128)S(1)} %get-tuple-element.133), channel_id=1, source_target_pairs={{8,0},{16,8},{24,16},{32,24},{40,32},{48,40},{56,48},{64,56},{72,6... | collective-permute-start | bytes 344072 | tf_op jit(solution)/shard_map/ppermute | solution.py:21
  440.8 10.1 %copy-start.9 = (f32[49,49,1,1]{1,0,3,2:T(8,128)S(1)}, f32[49,49,1,1]{1,0,3,2:T(8,128)}, u32[]{:S(2)}) copy-start(f32[49,49,1,1]{1,0,3,2:T(8,128)} %constant.292) | copy-start | bytes 28816
  440.8 15.6 %collective-permute-start = (f32[16,14,1,128]{3,2,0,1:T(1,128)S(1)}, f32[16,14,1,128]{3,2,0,1:T(1,128)S(1)}, u32[]{:S(2)}, u32[]{:S(2)}) collective-permute-start(f32[16,14,1,128]{3,2,0,1:T(1,128)S(1)} %get-tuple-element.134), channel_id=1, source_target_pairs={{0,8},{8,16},{16,24},{24,32},{32,40},{40,48},{48,56},{56,64},{64,7... | collective-permute-start | bytes 344072 | tf_op jit(solution)/shard_map/ppermute | solution.py:20
  503.8 5.5 copy-start.3
  509.3 22.2 %copy-start.1 = (f32[16,8,128,49]{2,3,1,0:T(8,128)}, f32[16,8,128,49]{2,3,1,0:T(8,128)S(1)}, u32[]{:S(2)}) copy-start(f32[16,8,128,49]{2,3,1,0:T(8,128)S(1)} %fusion.21) | copy-start | bytes 9633796
  522.0 8.5 %collective-permute-start.3 = (f32[16,14,1,128]{3,2,0,1:T(1,128)S(1)}, f32[16,14,1,128]{3,2,0,1:T(1,128)S(1)}, u32[]{:S(2)}, u32[]{:S(2)}) collective-permute-start(f32[16,14,1,128]{3,2,0,1:T(1,128)S(1)} %get-tuple-element.131), channel_id=1, source_target_pairs={{8,0},{16,8},{24,16},{32,24},{40,32},{48,40},{56,48},{64,56},{72,6... | collective-permute-start | bytes 344072 | tf_op jit(solution)/shard_map/ppermute | solution.py:21
  523.3 6.9 %collective-permute-start.2 = (f32[16,14,1,128]{3,2,0,1:T(1,128)S(1)}, f32[16,14,1,128]{3,2,0,1:T(1,128)S(1)}, u32[]{:S(2)}, u32[]{:S(2)}) collective-permute-start(f32[16,14,1,128]{3,2,0,1:T(1,128)S(1)} %get-tuple-element.132), channel_id=1, source_target_pairs={{0,8},{8,16},{16,24},{24,32},{32,40},{40,48},{48,56},{56,64},{64,7... | collective-permute-start | bytes 344072 | tf_op jit(solution)/shard_map/ppermute | solution.py:20
  533.2 41.6 %copy-start.4 = (f32[16,49,8,128]{3,2,0,1:T(8,128)S(1)}, f32[16,49,8,128]{3,2,0,1:T(8,128)}, u32[]{:S(2)}) copy-start(f32[16,49,8,128]{3,2,0,1:T(8,128)} %copy-done.3) | copy-start | bytes 9633796
  (2 other events, 5.5 us)
where the time goes:
time: 636 us; the launch traced here: 626 us
  waiting for transfers between devices  207 us (33%)
  matrix products  148 us (23%)
  blocking collectives  113 us (18%)
  local copies, waits for them, and re-layouts  95.5 us (15%)
  other arithmetic  38.7 us (6%)
  starting transfers between devices  22.5 us (4%)
    all_to_all x1, waiting for transfers between devices, body(): lax.all_to_all(velocity, 'fourier', split_axis=3, concat_axis=1, tiled=True)  108 us
    all_to_all x1, waiting for transfers between devices, body(): lax.all_to_all(spectral, 'fourier', split_axis=1, concat_axis=3, tiled=True)  96.4 us
    psum x1, blocking collectives, body(): lax.psum((inner(image_a, image_a), inner(resid, image_a)), 'plane')  39.6 us
    psum x1, blocking collectives, body(): margin_sum = lax.psum(inner(image_b, image_a), 'plane')  37.9 us
    psum x1, blocking collectives, body(): lax.psum((inner(image_b, image_b), inner(resid, image_b)), 'plane')  35.4 us
    dot_general x1, matrix products, advection(): jnp.einsum('mn,xqnij->xqmij', diff_x, physical, precision=HIGHEST_PRECISION)  30.9 us
    dot_general x1, matrix products, advection(): jnp.einsum('mn,xqnij->xqmij', diff_y, physical, precision=HIGHEST_PRECISION)  22.9 us
    mul x4, local copies, waits for them, and re-layouts, advection(): return physical[0] * along_x + physical[1] * along_y + physical[2] * along_z  21 us
  transfers between devices with their start and end apart: 6, of which 3 were waited for; matrix products, arithmetic and copies ran while one was open for 4% of the time, Pallas kernels for 0%

commit v1 on v0

v1 whole, which is shorter than its diff:
```python
import functools

import jax
import jax.numpy as jnp
import numpy as np
from jax import lax
from jax.experimental import pallas as pl
from jax.experimental.pallas import tpu as pltpu
from jax.sharding import PartitionSpec as P

PENALTY = 10.0
BETA = 0.5
MASS_REF = 0.08
LANES = 128
F32 = jnp.float32
BF16 = jnp.bfloat16
MIB = 1 << 20


def node_tables():
    nodes = np.array(
        [
            -1.0,
            -0.830223896278567,
            -0.4688487934707142,
            0.0,
            0.4688487934707142,
            0.830223896278567,
            1.0,
        ]
    )
    weights = np.array(
        [
            1.0 / 21.0,
            0.2768260473615659,
            0.4317453812098627,
            0.4876190476190476,
            0.4317453812098627,
            0.2768260473615659,
            1.0 / 21.0,
        ]
    )
    identity = np.eye(7)
    differ = nodes[:, None] - nodes[None, :] + identity
    bary = 1.0 / np.prod(differ, axis=1)
    off_diag = np.where(identity > 0.5, 0.0, bary[None, :] / bary[:, None] / differ)
    deriv = off_diag - identity * off_diag.sum(axis=1)[:, None]
    weight_diag = identity * weights[None, :]
    stiff = deriv.T @ weight_diag @ deriv
    side = np.where((np.arange(7) == 0) | (np.arange(7) == 6), 1.0, 0.0)
    rim = (side[:, None] + side[None, :]).reshape(49)
    system = np.kron(stiff, weight_diag) + np.kron(weight_diag, stiff)
    system = system + PENALTY * np.eye(49) * rim[None, :]
    system = system.astype(np.float32).astype(np.float64)
    return weights, deriv, stiff, np.linalg.inv(system)


def mode_tables(length):
    index = np.arange(length)
    wavenum = index // 2
    wavenum[1] = length // 2
    angles = 2.0 * np.pi * np.outer(index, wavenum) / length
    use_cos = (index % 2 == 0) | (index == 1)
    basis = np.where(use_cos[None, :], np.cos(angles), np.sin(angles))
    factor = np.full(length, 2.0 / length)
    factor[:2] = 1.0 / length
    forward = factor[:, None] * basis.T
    modal_diff = np.zeros((length, length))
    even = np.arange(2, length, 2)
    modal_diff[even, even + 1] = BETA * wavenum[even]
    modal_diff[even + 1, even] = -BETA * wavenum[even]
    wave_sq = (BETA * wavenum) ** 2
    return basis, forward, modal_diff, wave_sq


WEIGHTS, DERIV, STIFF, BLOCK_INV = node_tables()

ANALYSIS = np.zeros((7, 7))
SYNTHESIS = np.zeros((7, 7))
for _k in range(3):
    ANALYSIS[_k, _k] = ANALYSIS[_k, 6 - _k] = 1.0
    ANALYSIS[4 + _k, _k] = 1.0
    ANALYSIS[4 + _k, 6 - _k] = -1.0
    SYNTHESIS[_k, _k] = SYNTHESIS[6 - _k, _k] = 1.0
    SYNTHESIS[_k, 4 + _k] = 1.0
    SYNTHESIS[6 - _k, 4 + _k] = -1.0
ANALYSIS[3, 3] = SYNTHESIS[3, 3] = 1.0


def parity_form(matrix):
    return np.linalg.inv(SYNTHESIS) @ matrix @ np.linalg.inv(ANALYSIS)


DERIV_P = parity_form(DERIV)
STIFF_P = parity_form(STIFF)
_S2 = np.kron(ANALYSIS, ANALYSIS)
_R2 = np.kron(SYNTHESIS, SYNTHESIS)
BLOCK_P = np.linalg.inv(_R2) @ BLOCK_INV @ np.linalg.inv(_S2)
BLOCK_P = BLOCK_P.reshape(7, 7, 7, 7)


def analyse(v):
    return [v[0] + v[6], v[1] + v[5], v[2] + v[4], v[3], v[0] - v[6], v[1] - v[5], v[2] - v[4]]


def synthesise(g):
    return [
        g[0] + g[4],
        g[1] + g[5],
        g[2] + g[6],
        g[3],
        g[2] - g[6],
        g[1] - g[5],
        g[0] - g[4],
    ]


def mat_rows(matrix, v):
    out = []
    for row in matrix:
        acc = None
        for coef, item in zip(row, v):
            if abs(coef) > 1e-11:
                term = item * np.float32(coef)
                acc = term if acc is None else acc + term
        out.append(acc)
    return out


def derive(v):
    g = analyse(v)
    even = mat_rows(DERIV_P[:4, 4:], g[4:])
    odd = mat_rows(DERIV_P[4:, :4], g[:4])
    out = [even[k] + odd[k] for k in range(3)]
    return out + [even[3]] + [even[k] - odd[k] for k in (2, 1, 0)]


def stiffen(v):
    g = analyse(v)
    return synthesise(mat_rows(STIFF_P[:4, :4], g[:4]) + mat_rows(STIFF_P[4:, 4:], g[4:]))


def symmetric_sector(table, x, size):
    pairs = [(i, j) for i in range(size) for j in range(i, size)]
    anti = [(i, j) for i in range(size) for j in range(i + 1, size)]
    plus = [x[i][j] if i == j else x[i][j] + x[j][i] for i, j in pairs]
    minus = [x[i][j] - x[j][i] for i, j in anti]

    def sym_row(i, j):
        return [0.5 * (table[i, j, k, l] + table[i, j, l, k]) for k, l in pairs]

    def anti_row(i, j):
        return [0.5 * (table[i, j, k, l] - table[i, j, l, k]) for k, l in anti]

    top = dict(zip(pairs, mat_rows([sym_row(i, j) for i, j in pairs], plus)))
    low = dict(zip(anti, mat_rows([anti_row(i, j) for i, j in anti], minus)))
    out = [[None] * size for _ in range(size)]
    for i, j in pairs:
        if i == j:
            out[i][j] = top[i, j]
        else:
            out[i][j] = top[i, j] + low[i, j]
            out[j][i] = top[i, j] - low[i, j]
    return out


def block_solve(v):
    part = [[None] * 7 for _ in range(7)]
    for b in range(7):
        column = analyse([v[7 * a + b] for a in range(7)])
        for k in range(7):
            part[k][b] = column[k]
    part = [analyse(part[k]) for k in range(7)]
    out = [[None] * 7 for _ in range(7)]
    ev, od = slice(0, 4), slice(4, 7)
    for rows, cols in ((ev, ev), (od, od), (ev, od), (od, ev)):
        ri, ci = range(7)[rows], range(7)[cols]
        x = [[part[i][j] for j in ci] for i in ri]
        table = BLOCK_P[rows, cols, rows, cols]
        if rows == cols:
            y = symmetric_sector(table, x, len(ri))
        else:
            n = len(ri) * len(ci)
            flat = mat_rows(table.reshape(n, n), [x[i][j] for i in range(len(ri)) for j in range(len(ci))])
            y = [flat[i * len(ci) : (i + 1) * len(ci)] for i in range(len(ri))]
        for i, row in zip(ri, y):
            for j, item in zip(ci, row):
                out[i][j] = item
    out = [synthesise(out[k]) for k in range(7)]
    res = [None] * 49
    for b in range(7):
        column = synthesise([out[k][b] for k in range(7)])
        for a in range(7):
            res[7 * a + b] = column[a]
    return res


def params(limit_mib, grid=None):
    semantics = None if grid is None else ("arbitrary",) * grid
    return pltpu.CompilerParams(vmem_limit_bytes=limit_mib * MIB, dimension_semantics=semantics)


def pack_kernel(in_ref, out_ref):
    def step(n, carry):
        for i in range(8):
            out_ref[i, 0, n] = in_ref[pl.ds(n * 8 + i, 8, stride=392), :]
        return carry

    lax.fori_loop(0, 49, step, 0, unroll=7)


def pack(velocity):
    flat = velocity.reshape(3 * 16 * 392, LANES)
    return pl.pallas_call(
        pack_kernel,
        grid=(3, 2),
        in_specs=[pl.BlockSpec((8 * 392, LANES), lambda x, h: (2 * x + h, 0))],
        out_specs=pl.BlockSpec((8, 1, 49, 8, LANES), lambda x, h: (0, x, 0, h, 0)),
        out_shape=jax.ShapeDtypeStruct((8, 3, 49, 16, LANES), F32),
        compiler_params=params(32, 2),
        name="pack",
    )(flat)


def forcing_kernel(in_ref, met_ref, wp_ref, wl_ref, fh_ref, fl_ref, out_ref, xb, u, z, adv, div):
    a = pl.program_id(0)
    sx = met_ref[0]
    sy = met_ref[1]
    for x in range(3):
        for b in range(7):
            block = in_ref[:, x, b].reshape(128, LANES)
            hi = block.astype(BF16)
            lo = (block - hi.astype(F32)).astype(BF16)
            xb[0:128, b * 128 : b * 128 + 128] = hi
            xb[128:256, b * 128 : b * 128 + 128] = lo
        both = jnp.dot(wp_ref[...], xb[...], preferred_element_type=F32)
        both = both + jnp.dot(wl_ref[...], xb[0:128], preferred_element_type=F32)
        u[x, a] = both[0:128]
        z[x] = both[128:256]

    def along_b(t, carry):
        q = pl.ds(pl.multiple_of(t * 8, 8), 8)
        lanes = [pl.ds(b * 128, 128) for b in range(7)]
        fields = [[u[i, a, q, s] for s in lanes] for i in range(3)]
        scaled = [item * sy for item in fields[1]]
        for i in range(3):
            slope = derive(fields[i])
            for b in range(7):
                adv[i, a, q, lanes[b]] = scaled[b] * slope[b] + fields[2][b] * z[i, q, lanes[b]]
        return carry

    lax.fori_loop(0, 16, along_b, 0)

    @pl.when(a == 6)
    def _():
        def along_a(t, carry):
            q = pl.ds(pl.multiple_of(t * 8, 8), 8)
            q2 = pl.ds(pl.multiple_of(t * 8 + 128, 8), 8)
            for b in range(7):
                s = pl.ds(b * 128, 128)
                first = [u[0, k, q, s] for k in range(7)]
                scaled = [item * sx for item in first]
                for i in range(3):
                    slope = derive(first if i == 0 else [u[i, k, q, s] for k in range(7)])
                    total = [scaled[k] * slope[k] + adv[i, k, q, s] for k in range(7)]
                    if i == 0:
                        total = [item * sx for item in derive(total)]
                    for k in range(7):
                        if i == 0:
                            div[k, q, s] = total[k]
                        elif i == 1:
                            adv[1, k, q, s] = total[k]
                        else:
                            div[k, q2, s] = total[k]
            for k in range(7):
                slope = derive([adv[1, k, q, pl.ds(b * 128, 128)] for b in range(7)])
                for b in range(7):
                    s = pl.ds(b * 128, 128)
                    div[k, q, s] = div[k, q, s] + sy * slope[b]
            return carry

        lax.fori_loop(0, 16, along_a, 0)
        area = -1.0 / (sx * sy)
        for k in range(7):
            block = div[k]
            hi = block.astype(BF16)
            lo = (block - hi.astype(F32)).astype(BF16)
            spec = jnp.dot(fh_ref[...], hi, preferred_element_type=F32)
            spec = spec + jnp.dot(fh_ref[...], lo, preferred_element_type=F32)
            spec = spec + jnp.dot(fl_ref[...], hi, preferred_element_type=F32)
            for b in range(7):
                scale = area * np.float32(WEIGHTS[k] * WEIGHTS[b])
                out_ref[:, 7 * k + b] = (spec[:, b * 128 : b * 128 + 128] * scale).reshape(8, 16, LANES)


def split_bf16(table):
    table = jnp.asarray(table, F32)
    hi = table.astype(BF16)
    return hi, (table - hi.astype(F32)).astype(BF16)


def forcing(gathered, met_row, basis, forward, modal_diff):
    both = np.concatenate([basis, basis @ modal_diff], axis=0)
    back = np.concatenate([forward, modal_diff @ forward], axis=1)
    wh, wl = split_bf16(both)
    fh, fl = split_bf16(back)
    wp = jnp.concatenate([wh, wh], axis=1)

    def whole(shape):
        return pl.BlockSpec(shape, lambda a: (0,) * len(shape))

    return pl.pallas_call(
        forcing_kernel,
        grid=(7,),
        in_specs=[
            pl.BlockSpec((8, 3, 7, 16, LANES), lambda a: (0, 0, a, 0, 0)),
            whole((2, 1, LANES)),
            whole((256, 256)),
            whole((256, 128)),
            whole((128, 256)),
            whole((128, 256)),
        ],
        out_specs=whole((8, 49, 16, LANES)),
        out_shape=jax.ShapeDtypeStruct((8, 49, 16, LANES), F32),
        scratch_shapes=[
            pltpu.VMEM((256, 896), BF16),
            pltpu.VMEM((3, 7, 128, 896), F32),
            pltpu.VMEM((3, 128, 896), F32),
            pltpu.VMEM((3, 7, 128, 896), F32),
            pltpu.VMEM((7, 256, 896), F32),
        ],
        compiler_params=params(56, 1),
        name="forcing",
    )(gathered, met_row, wp, wl, fh, fl)


def rows_of(c, n):
    return pl.ds(pl.multiple_of(c * 392 + n * 8, 8), 8)


def metric_values(met_ref):
    sx, sy = met_ref[0], met_ref[1]
    ratio = sx / sy
    back = sy / sx
    return ratio, back, 1.0 / (sx * sy)


def inverse_divisor(ratio, back, area, wave):
    return 1.0 / (0.5 * (ratio + back) + (wave * MASS_REF) * area)


def store_rims(field, c, east_ref, west_ref):
    for b in range(7):
        east_ref[pl.ds(c * 8 + b, 1), :] = field[42 + b][7:8]
        west_ref[pl.ds(c * 8 + b, 1), :] = field[b][0:1]


def apply_operator(v, c, wave, ratio, back, area, west_ref, east_ref):
    kind = [0, 1, 2, 3, 2, 1, 0]
    sub = lax.broadcasted_iota(jnp.int32, (8, LANES), 0)
    lane = lax.broadcasted_iota(jnp.int32, (8, LANES), 1)
    w = [np.float32(WEIGHTS[k]) for k in range(4)]
    ratio_w = [ratio * w[k] for k in range(4)]
    back_w = [back * w[k] for k in range(4)]
    mass = wave * area
    diag = {}
    for i in range(4):
        for j in range(i, 4):
            rim = PENALTY * ((i == 0) + (j == 0))
            diag[i, j] = mass * np.float32(WEIGHTS[i] * WEIGHTS[j]) + np.float32(rim)
    out = [None] * 49
    for b in range(7):
        column = stiffen([v[7 * a + b] for a in range(7)])
        for a in range(7):
            key = tuple(sorted((kind[a], kind[b])))
            out[7 * a + b] = column[a] * ratio_w[kind[b]] + v[7 * a + b] * diag[key]
    for a in range(7):
        line = stiffen([v[7 * a + b] for b in range(7)])
        for b in range(7):
            out[7 * a + b] = out[7 * a + b] + line[b] * back_w[kind[a]]
    ten = np.float32(PENALTY)
    for b in range(7):
        west = west_ref[pl.ds(c * 8 + b, 1), :]
        east = east_ref[pl.ds(c * 8 + b, 1), :]
        before = jnp.where(sub == 0, west, pltpu.roll(v[42 + b], 1, 0))
        after = jnp.where(sub == 7, east, pltpu.roll(v[b], 7, 0))
        out[b] = out[b] - ten * before
        out[42 + b] = out[42 + b] - ten * after
    for a in range(7):
        south = jnp.where(lane == 0, 0.0, pltpu.roll(v[7 * a + 6], 1, 1))
        north = jnp.where(lane == 127, 0.0, pltpu.roll(v[7 * a], 127, 1))
        out[7 * a] = out[7 * a] - ten * south
        out[7 * a + 6] = out[7 * a + 6] - ten * north
    return out


def first_kernel(wave_ref, recv_ref, met_ref, r_ref, p_ref, east_ref, west_ref):
    def unpack(n, carry):
        for i in range(8):
            r_ref[pl.ds(n * 8 + i, 16, stride=392), :] = recv_ref[i, n]
        return carry

    lax.fori_loop(0, 49, unpack, 0, unroll=7)
    east_ref[...] = jnp.zeros_like(east_ref)
    west_ref[...] = jnp.zeros_like(west_ref)
    ratio, back, area = metric_values(met_ref)

    def step(c, carry):
        inv = inverse_divisor(ratio, back, area, wave_ref[c])
        field = block_solve([r_ref[rows_of(c, n), :] for n in range(49)])
        field = [item * inv for item in field]
        for n in range(49):
            p_ref[rows_of(c, n), :] = field[n]
        store_rims(field, c, east_ref, west_ref)
        return carry

    lax.fori_loop(0, 16, step, 0)


def second_kernel(
    wave_ref, p_ref, met_ref, west_in, east_in, q_ref, s_ref, east_ref, west_ref
):
    east_ref[...] = jnp.zeros_like(east_ref)
    west_ref[...] = jnp.zeros_like(west_ref)
    ratio, back, area = metric_values(met_ref)

    def image(c, carry):
        v = [p_ref[rows_of(c, n), :] for n in range(49)]
        out = apply_operator(v, c, wave_ref[c], ratio, back, area, west_in, east_in)
        for n in range(49):
            q_ref[rows_of(c, n), :] = out[n]
        return carry

    lax.fori_loop(0, 16, image, 0)

    def search(c, carry):
        inv = inverse_divisor(ratio, back, area, wave_ref[c])
        field = block_solve([q_ref[rows_of(c, n), :] for n in range(49)])
        field = [item * inv for item in field]
        for n in range(49):
            s_ref[rows_of(c, n), :] = field[n]
        store_rims(field, c, east_ref, west_ref)
        return carry

    lax.fori_loop(0, 16, search, 0)


def third_kernel(
    wave_ref, r_ref, q_ref, s_ref, met_ref, west_in, east_in, t_ref, dots_ref, acc_ref
):
    ratio, back, area = metric_values(met_ref)

    def image(c, carry):
        v = [s_ref[rows_of(c, n), :] for n in range(49)]
        out = apply_operator(v, c, wave_ref[c], ratio, back, area, west_in, east_in)
        sums = [None] * 5
        for n in range(49):
            t_ref[rows_of(c, n), :] = out[n]
            q, r, t = q_ref[rows_of(c, n), :], r_ref[rows_of(c, n), :], out[n]
            for k, term in enumerate((q * q, r * q, t * q, t * t, r * t)):
                sums[k] = term if sums[k] is None else sums[k] + term
        for k in range(5):
            acc_ref[k, pl.ds(c, 1), :] = jnp.sum(sums[k], axis=0, keepdims=True)
        return carry

    lax.fori_loop(0, 16, image, 0)
    lane = lax.broadcasted_iota(jnp.int32, (16, LANES), 1)
    table = jnp.zeros((16, LANES), F32)
    for k in range(5):
        table = jnp.where(lane == k, jnp.sum(acc_ref[k], axis=1, keepdims=True), table)
    for d in range(16):
        dots_ref[d] = table


def last_kernel(dots_ref, r_ref, p_ref, q_ref, s_ref, t_ref, pres_ref, resid_ref, coef_ref):
    total = dots_ref[0]
    for d in range(1, 16):
        total = total + dots_ref[d]
    lane = lax.broadcasted_iota(jnp.int32, (16, LANES), 1)

    def pick(k):
        return jnp.sum(jnp.where(lane == k, total, 0.0), axis=1, keepdims=True)

    qq, rq, tq, tt, rt = [pick(k) for k in range(5)]
    alpha = rq / qq
    gamma = tq / qq
    lam = (rt - gamma * rq) / (tt - gamma * tq)
    coef_ref[0] = jnp.broadcast_to(alpha - lam * gamma, (16, LANES))
    coef_ref[1] = jnp.broadcast_to(lam, (16, LANES))

    def step(c, carry):
        first = coef_ref[0, pl.ds(c, 1), :]
        second = coef_ref[1, pl.ds(c, 1), :]
        for n in range(49):
            at = rows_of(c, n)
            pres_ref[at, :] = first * p_ref[at, :] + second * s_ref[at, :]
            resid_ref[at, :] = r_ref[at, :] - first * q_ref[at, :] - second * t_ref[at, :]
        return carry

    lax.fori_loop(0, 16, step, 0)


FIELD = (16 * 392, LANES)
RIM = (16 * 8, LANES)


def call(kernel, name, inputs, smem, outs, limit, scratch=()):
    specs = [
        pl.BlockSpec(memory_space=pltpu.SMEM if i in smem else pltpu.VMEM)
        for i in range(len(inputs))
    ]
    return pl.pallas_call(
        kernel,
        in_specs=specs,
        out_specs=tuple(pl.BlockSpec(memory_space=pltpu.VMEM) for _ in outs),
        out_shape=tuple(jax.ShapeDtypeStruct(s, F32) for s in outs),
        scratch_shapes=list(scratch),
        compiler_params=params(limit),
        name=name,
    )(*inputs)


def body(velocity, metric):
    modes_here = velocity.shape[1]
    basis, forward, modal_diff, wave_all = mode_tables(modes_here * lax.axis_size("fourier"))
    mine = lax.axis_index("fourier")
    wave = lax.dynamic_slice_in_dim(jnp.asarray(wave_all, F32), mine * modes_here, modes_here)
    met_row = lax.dynamic_slice_in_dim(metric, mine, 1, 1)

    packed = pack(velocity)
    gathered = lax.all_to_all(packed, "fourier", 0, 0, tiled=True)
    source = forcing(gathered, met_row, basis, forward, modal_diff)
    recv = lax.all_to_all(source, "fourier", 0, 0, tiled=True)

    size = lax.axis_size("plane")
    up = [(i, i + 1) for i in range(size - 1)]
    down = [(j, i) for i, j in up]

    def exchange(east, west):
        return lax.ppermute(east, "plane", up), lax.ppermute(west, "plane", down)

    r, p1, east, west = call(
        first_kernel, "first", (wave, recv, metric), (0,), (FIELD, FIELD, RIM, RIM), 40
    )
    west_in, east_in = exchange(east, west)
    q1, s, east, west = call(
        second_kernel,
        "second",
        (wave, p1, metric, west_in, east_in),
        (0,),
        (FIELD, FIELD, RIM, RIM),
        40,
    )
    west_in, east_in = exchange(east, west)
    t, dots = call(
        third_kernel,
        "third",
        (wave, r, q1, s, metric, west_in, east_in),
        (0,),
        (FIELD, (16, 16, LANES)),
        40,
        [pltpu.VMEM((5, 16, LANES), F32)],
    )
    dots = lax.all_to_all(dots, "plane", 0, 0, tiled=True)
    pressure, residual = call(
        last_kernel,
        "last",
        (dots, r, p1, q1, s, t),
        (),
        (FIELD, FIELD),
        40,
        [pltpu.VMEM((2, 16, LANES), F32)],
    )
    shape = velocity.shape[1:]
    return pressure.reshape(shape), residual.reshape(shape)


def solution(mesh):
    in_specs = (P(None, "fourier", None, "plane", None), P(None, "plane", None))
    out_specs = (P("fourier", None, "plane", None), P("fourier", None, "plane", None))
    return jax.shard_map(body, mesh=mesh, in_specs=in_specs, out_specs=out_specs, check_vma=False)
```

time: 636 us -> 247 us (0.39); the launches traced: 626 us -> 246 us
  matrix products: 148 us -> 0 us
  blocking collectives: 113 us -> 15.9 us
  local copies, waits for them, and re-layouts: 95.5 us -> 9.75 us
  waiting for transfers between devices: 207 us -> 156 us
  Pallas kernels: 0 us -> 44.5 us
  other arithmetic: 38.7 us -> 0 us
    dot_general x14 -> x0, matrix products: 148 us -> none  [the longest x1 30.9 us: advection(): jnp.einsum('mn,xqnij->xqmij', diff_x, physical, precision=HIGHEST_PRECISION)]
    psum x3 -> x0, blocking collectives: 113 us -> none  [the longest x1 39.6 us: body(): lax.psum((inner(image_a, image_a), inner(resid, image_a)), 'plane')]
    all_to_all x2, waiting for transfers between devices: 204 us -> 146 us  [the longest x1 107 us: body(): gathered = lax.all_to_all(packed, 'fourier', 0, 0, tiled=True)]
    pallas_call x0 -> x6, Pallas kernels: none -> 44.5 us  [the longest x1 21.7 us: forcing(): pl.pallas_call(forcing_kernel, grid=(7,), in_specs=[pl.BlockSpec((8, 3, 7...]
    all_to_all x3 -> x0, local copies, waits for them, and re-layouts: 23.1 us -> none  [the longest x2 18.2 us: body(): lax.all_to_all(spectral, 'fourier', split_axis=1, concat_axis=3, tiled=True)]
    mul x5 -> x0, local copies, waits for them, and re-layouts: 21 us -> none  [the longest x4 21 us: advection(): return physical[0] * along_x + physical[1] * along_y + physical[2] * along_z]
    transpose x1 -> x0, local copies, waits for them, and re-layouts: 20.7 us -> none  [body(): jnp.einsum('cq,xqnij->xcnij', forward, advect, precision=HIGHEST_PRECISION)]
    all_to_all x0 -> x1, blocking collectives: none -> 15.9 us  [body(): dots = lax.all_to_all(dots, 'plane', 0, 0, tiled=True)]
  transfers between devices with their start and end apart: 6 -> 6, of which waited for: 3 -> 6; matrix products, arithmetic and copies ran while one was open for 4% -> 0% of each run, Pallas kernels for 0% -> 0%
where the time goes in v1:
time: 247 us; the launch traced here: 246 us
  waiting for transfers between devices  156 us (63%)
  Pallas kernels  44.5 us (18%)
  starting transfers between devices  19.3 us (8%)
  blocking collectives  15.9 us (6%)
  local copies, waits for them, and re-layouts  9.75 us (4%)
    all_to_all x1, waiting for transfers between devices, body(): gathered = lax.all_to_all(packed, 'fourier', 0, 0, tiled=True)  107 us
    all_to_all x1, waiting for transfers between devices, body(): recv = lax.all_to_all(source, 'fourier', 0, 0, tiled=True)  39 us
    pallas_call x1, Pallas kernels, forcing(): pl.pallas_call(forcing_kernel, grid=(7,), in_specs=[pl.BlockSpec((8, 3, 7...  21.7 us
    pallas_call x4, Pallas kernels, call(): pl.pallas_call(kernel, in_specs=specs, out_specs=tuple((pl.BlockSpec(memo...  20.1 us
    all_to_all x1, blocking collectives, body(): dots = lax.all_to_all(dots, 'plane', 0, 0, tiled=True)  15.9 us
    ppermute x4, starting transfers between devices, exchange(): return (lax.ppermute(east, 'plane', up), lax.ppermute(west, 'plane', down))  10.3 us
    ppermute x4, waiting for transfers between devices, exchange(): return (lax.ppermute(east, 'plane', up), lax.ppermute(west, 'plane', down))  9.72 us
    unnamed x10, local copies, waits for them, and re-layouts  9.1 us
  transfers between devices with their start and end apart: 6, of which 6 were waited for; matrix products, arithmetic and copies ran while one was open for 0% of the time, Pallas kernels for 0%

profile of v1, /device:TPU:0, one launch (start us, length us, event | category | flops | bytes accessed | tf_op | source)
XLA Modules:
  0.0 246.3 jit_solution(18390783410902754866)
XLA Ops:
  0.6 3.8 %copy-done.1 = f32[3,16,49,8,128]{4,3,2,1,0:T(8,128)S(1)} copy-done((f32[3,16,49,8,128]{4,3,2,1,0:T(8,128)S(1)}, f32[3,16,49,8,128]{4,3,2,1,0:T(8,128)}, u32[]{:S(2)}) %copy-start.1) | copy-done | bytes 9633816
  4.4 2.8 %pack.1 = f32[8,3,49,16,128]{4,3,2,1,0:T(8,128)S(1)} custom-call(f32[18816,128]{1,0:T(8,128)S(1)} %bitcast.3), custom_call_target="tpu_custom_call" | custom-call | tf_op jit(solution)/shard_map/pack/pallas_call | solution.py:214
  7.2 3.7 %copy-done = f32[8,3,49,16,128]{4,3,2,1,0:T(8,128)} copy-done((f32[8,3,49,16,128]{4,3,2,1,0:T(8,128)}, f32[8,3,49,16,128]{4,3,2,1,0:T(8,128)S(1)}, u32[]{:S(2)}) %copy-start) | copy-done | bytes 9633816
  10.9 5.2 %all-to-all-start = ((f32[8,3,49,16,128]{4,3,2,1,0:T(8,128)}), f32[8,3,49,16,128]{4,3,2,1,0:T(8,128)}, u32[]{:S(2)}, u32[]{:S(2)}) async-start(f32[8,3,49,16,128]{4,3,2,1,0:T(8,128)} %copy-done), calls=%async_computation | async-start | bytes 19267584 | tf_op jit(solution)/shard_map/all_to_all | solution.py:531
  16.1 0.6 constant_dynamic-slice_fusion.met_ref
  16.7 107.4 %all-to-all-done.in_ref = f32[8,3,49,16,128]{4,3,2,1,0:T(8,128)} async-done(((f32[8,3,49,16,128]{4,3,2,1,0:T(8,128)}), f32[8,3,49,16,128]{4,3,2,1,0:T(8,128)}, u32[]{:S(2)}, u32[]{:S(2)}) %all-to-all-start) | async-done | bytes 9633824 | tf_op jit(solution)/shard_map/all_to_all | solution.py:531
  124.0 21.7 %forcing.1 = f32[8,49,16,128]{3,2,1,0:T(8,128)} custom-call(f32[8,3,49,16,128]{4,3,2,1,0:T(8,128)} %all-to-all-done.in_ref, f32[2,1,128]{2,1,0:T(1,128)} %constant_dynamic-slice_fusion.met_ref, bf16[256,256]{1,0:T(8,128)(2,1)} %constant.24.wp_ref, bf16[256,128]{1,0:T(8,128)(2,1)} %constant.27.wl_ref, bf16[128,256]{1,0:T(8,128)(2,1)} %constant.28.fh_ref, ...), custom_call_target="tpu_custom_call" | custom-call | tf_op jit(solution)/shard_map/forcing/pallas_call | solution.py:312
  145.7 3.8 %all-to-all-start.1 = ((f32[8,49,16,128]{3,2,1,0:T(8,128)}), f32[8,49,16,128]{3,2,1,0:T(8,128)S(1)}, u32[]{:S(2)}, u32[]{:S(2)}) async-start(f32[8,49,16,128]{3,2,1,0:T(8,128)} %forcing.1), calls=%async_computation.1 | async-start | bytes 6422528 | tf_op jit(solution)/shard_map/all_to_all | solution.py:533
  149.5 0.1 dynamic_slice.6.wave_ref
  149.6 39.0 %all-to-all-done.1.recv_ref = f32[8,49,16,128]{3,2,1,0:T(8,128)S(1)} async-done(((f32[8,49,16,128]{3,2,1,0:T(8,128)}), f32[8,49,16,128]{3,2,1,0:T(8,128)S(1)}, u32[]{:S(2)}, u32[]{:S(2)}) %all-to-all-start.1) | async-done | bytes 3211296 | tf_op jit(solution)/shard_map/all_to_all | solution.py:533
  188.6 3.8 %first.1 = (f32[6272,128]{1,0:T(8,128)S(1)}, f32[6272,128]{1,0:T(8,128)S(1)}, f32[128,128]{1,0:T(8,128)S(1)}, f32[128,128]{1,0:T(8,128)S(1)}) custom-call(f32[16]{0:T(128)S(1)} %dynamic_slice.6.wave_ref, f32[8,49,16,128]{3,2,1,0:T(8,128)S(1)} %all-to-all-done.1.recv_ref, f32[2,8,128]{2,1,0:T(8,128)S(1)} %copy-done.3), custom_call_target="tpu_custom_call" | custom-call | tf_op jit(solution)/shard_map/first/pallas_call | solution.py:512
  192.3 3.9 %collective-permute-start = (f32[128,128]{1,0:T(8,128)S(1)}, f32[128,128]{1,0:T(8,128)S(1)}, u32[]{:S(2)}, u32[]{:S(2)}) collective-permute-start(f32[128,128]{1,0:T(8,128)S(1)} %get-tuple-element.16), channel_id=1, source_target_pairs={{0,8},{8,16},{16,24},{24,32},{32,40},{40,48},{48,56},{56,64},{64,7... | collective-permute-start | bytes 196616 | tf_op jit(solution)/shard_map/ppermute | solution.py:540
  196.3 1.3 collective-permute-start.1
  197.6 0.6 collective-permute-done.west_in
  198.2 4.3 %collective-permute-done.1.east_in = f32[128,128]{1,0:T(8,128)S(1)} collective-permute-done((f32[128,128]{1,0:T(8,128)S(1)}, f32[128,128]{1,0:T(8,128)S(1)}, u32[]{:S(2)}, u32[]{:S(2)}) %collective-permute-start.1) | collective-permute-done | bytes 65568 | tf_op jit(solution)/shard_map/ppermute | solution.py:540
  202.4 6.1 %second.1 = (f32[6272,128]{1,0:T(8,128)S(1)}, f32[6272,128]{1,0:T(8,128)S(1)}, f32[128,128]{1,0:T(8,128)S(1)}, f32[128,128]{1,0:T(8,128)S(1)}) custom-call(f32[16]{0:T(128)S(1)} %dynamic_slice.6.wave_ref, f32[6272,128]{1,0:T(8,128)S(1)} %get-tuple-element.15.p_ref, f32[2,8,128]{2,1,0:T(8,128)S(1)} %copy-done.3, f32[128,128]{1,0:T(8,128)S(1)} %collective-permute-done.west_in, ...), custom_call_target="tpu_custom_call" | custom-call | tf_op jit(solution)/shard_map/second/pallas_call | solution.py:512
  208.6 3.8 %collective-permute-start.2 = (f32[128,128]{1,0:T(8,128)S(1)}, f32[128,128]{1,0:T(8,128)S(1)}, u32[]{:S(2)}, u32[]{:S(2)}) collective-permute-start(f32[128,128]{1,0:T(8,128)S(1)} %get-tuple-element.20), channel_id=1, source_target_pairs={{0,8},{8,16},{16,24},{24,32},{32,40},{40,48},{48,56},{56,64},{64,7... | collective-permute-start | bytes 196616 | tf_op jit(solution)/shard_map/ppermute | solution.py:540
  212.4 1.3 collective-permute-start.3
  213.7 0.6 collective-permute-done.2.west_in
  214.3 4.3 %collective-permute-done.3.east_in = f32[128,128]{1,0:T(8,128)S(1)} collective-permute-done((f32[128,128]{1,0:T(8,128)S(1)}, f32[128,128]{1,0:T(8,128)S(1)}, u32[]{:S(2)}, u32[]{:S(2)}) %collective-permute-start.3) | collective-permute-done | bytes 65568 | tf_op jit(solution)/shard_map/ppermute | solution.py:540
  218.6 4.6 %third.1 = (f32[6272,128]{1,0:T(8,128)S(1)}, f32[16,16,128]{2,1,0:T(8,128)S(1)}) custom-call(f32[16]{0:T(128)S(1)} %dynamic_slice.6.wave_ref, f32[6272,128]{1,0:T(8,128)S(1)} %get-tuple-element.14.r_ref, f32[6272,128]{1,0:T(8,128)S(1)} %get-tuple-element.18.q_ref, f32[6272,128]{1,0:T(8,128)S(1)} %get-tuple-element.19.s_ref, f32[2,8,128]{2,1,0:T(8,128)S(1)} %copy-done.3, ...), custom_call_target="tpu_custom_call" | custom-call | tf_op jit(solution)/shard_map/third/pallas_call | solution.py:512
  223.1 1.7 copy-done.2
  224.8 15.9 %all_to_all.15.dots_ref = f32[16,16,128]{2,1,0:T(8,128)S(1)} all-to-all(f32[16,16,128]{2,1,0:T(8,128)S(1)} %get-tuple-element.22), channel_id=1, replica_groups=mesh['plane'=16,'fourier'=8] {'plane'}, dimensions={0} | all-to-all | bytes 262144 | tf_op jit(solution)/shard_map/all_to_all | solution.py:564
  240.7 5.6 %last.1 = (f32[6272,128]{1,0:T(8,128)}, f32[6272,128]{1,0:T(8,128)}) custom-call(f32[16,16,128]{2,1,0:T(8,128)S(1)} %all_to_all.15.dots_ref, f32[6272,128]{1,0:T(8,128)S(1)} %get-tuple-element.14.r_ref, f32[6272,128]{1,0:T(8,128)S(1)} %get-tuple-element.15.p_ref, f32[6272,128]{1,0:T(8,128)S(1)} %get-tuple-element.18.q_ref, ...), custom_call_target="tpu_custom_call" | custom-call | tf_op jit(solution)/shard_map/last/pallas_call | solution.py:512
  (7 shorter events, 0.0 us)
Async XLA Ops:
  0.6 3.8 %copy-start.1 = (f32[3,16,49,8,128]{4,3,2,1,0:T(8,128)S(1)}, f32[3,16,49,8,128]{4,3,2,1,0:T(8,128)}, u32[]{:S(2)}) copy-start(f32[3,16,49,8,128]{4,3,2,1,0:T(8,128)} %param.5) | copy-start | bytes 28901380
  7.2 3.7 %copy-start = (f32[8,3,49,16,128]{4,3,2,1,0:T(8,128)}, f32[8,3,49,16,128]{4,3,2,1,0:T(8,128)S(1)}, u32[]{:S(2)}) copy-start(f32[8,3,49,16,128]{4,3,2,1,0:T(8,128)S(1)} %pack.1) | copy-start | bytes 28901380
  10.9 5.2 %copy-start.3 = (f32[2,8,128]{2,1,0:T(8,128)S(1)}, f32[2,8,128]{2,1,0:T(8,128)}, u32[]{:S(2)}) copy-start(f32[2,8,128]{2,1,0:T(8,128)} %met_ref.5) | copy-start | bytes 24580
  10.9 113.2 %all-to-all-start = ((f32[8,3,49,16,128]{4,3,2,1,0:T(8,128)}), f32[8,3,49,16,128]{4,3,2,1,0:T(8,128)}, u32[]{:S(2)}, u32[]{:S(2)}) async-start(f32[8,3,49,16,128]{4,3,2,1,0:T(8,128)} %copy-done), calls=%async_computation | async-start | bytes 19267584 | tf_op jit(solution)/shard_map/all_to_all | solution.py:531
  145.7 3.8 %copy-start.4 = (f32[128]{0:T(128)S(1)}, f32[128]{0:T(128)}, u32[]{:S(2)}) copy-start(f32[128]{0:T(128)} %constant.18.clone) | copy-start | bytes 1540
  145.7 42.8 %all-to-all-start.1 = ((f32[8,49,16,128]{3,2,1,0:T(8,128)}), f32[8,49,16,128]{3,2,1,0:T(8,128)S(1)}, u32[]{:S(2)}, u32[]{:S(2)}) async-start(f32[8,49,16,128]{3,2,1,0:T(8,128)} %forcing.1), calls=%async_computation.1 | async-start | bytes 6422528 | tf_op jit(solution)/shard_map/all_to_all | solution.py:533
  192.3 5.8 %collective-permute-start = (f32[128,128]{1,0:T(8,128)S(1)}, f32[128,128]{1,0:T(8,128)S(1)}, u32[]{:S(2)}, u32[]{:S(2)}) collective-permute-start(f32[128,128]{1,0:T(8,128)S(1)} %get-tuple-element.16), channel_id=1, source_target_pairs={{0,8},{8,16},{16,24},{24,32},{32,40},{40,48},{48,56},{56,64},{64,7... | collective-permute-start | bytes 196616 | tf_op jit(solution)/shard_map/ppermute | solution.py:540
  196.3 6.2 %collective-permute-start.1 = (f32[128,128]{1,0:T(8,128)S(1)}, f32[128,128]{1,0:T(8,128)S(1)}, u32[]{:S(2)}, u32[]{:S(2)}) collective-permute-start(f32[128,128]{1,0:T(8,128)S(1)} %get-tuple-element.17), channel_id=1, source_target_pairs={{8,0},{16,8},{24,16},{32,24},{40,32},{48,40},{56,48},{64,56},{72,6... | collective-permute-start | bytes 196616 | tf_op jit(solution)/shard_map/ppermute | solution.py:540
  208.6 5.7 %collective-permute-start.2 = (f32[128,128]{1,0:T(8,128)S(1)}, f32[128,128]{1,0:T(8,128)S(1)}, u32[]{:S(2)}, u32[]{:S(2)}) collective-permute-start(f32[128,128]{1,0:T(8,128)S(1)} %get-tuple-element.20), channel_id=1, source_target_pairs={{0,8},{8,16},{16,24},{24,32},{32,40},{40,48},{48,56},{56,64},{64,7... | collective-permute-start | bytes 196616 | tf_op jit(solution)/shard_map/ppermute | solution.py:540
  212.4 6.2 %collective-permute-start.3 = (f32[128,128]{1,0:T(8,128)S(1)}, f32[128,128]{1,0:T(8,128)S(1)}, u32[]{:S(2)}, u32[]{:S(2)}) collective-permute-start(f32[128,128]{1,0:T(8,128)S(1)} %get-tuple-element.21), channel_id=1, source_target_pairs={{8,0},{16,8},{24,16},{32,24},{40,32},{48,40},{56,48},{64,56},{72,6... | collective-permute-start | bytes 196616 | tf_op jit(solution)/shard_map/ppermute | solution.py:540
  223.1 1.7 copy-start.2

commit v2 on v1

--- a/solution.py
+++ b/solution.py
@@ -1,7 +1,6 @@
-import functools
-
 import jax
 import jax.numpy as jnp
+import ml_dtypes
 import numpy as np
 from jax import lax
 from jax.experimental import pallas as pl
@@ -15,6 +14,7 @@
 F32 = jnp.float32
 BF16 = jnp.bfloat16
 MIB = 1 << 20
+FULL = 60
 
 
 def node_tables():
@@ -200,138 +200,215 @@
     return pltpu.CompilerParams(vmem_limit_bytes=limit_mib * MIB, dimension_semantics=semantics)
 
 
-def pack_kernel(in_ref, out_ref):
+STEPS = ((0, 0), (1, 0), (3, 0), (2, 0), (1, 1), (3, 1), (2, 1), (0, 1))
+
+
+def partner(me, d, flip):
+    core = me % 2
+    return ((me // 2 + d) % 4) * 2 + (core + flip - 2 * core * flip)
+
+
+def permute(value, step):
+    d, flip = STEPS[step]
+    return lax.ppermute(value, "fourier", [(i, partner(i, d, flip)) for i in range(8)])
+
+
+def target(me, step):
+    return partner(me, *STEPS[step])
+
+
+def origin(me, step):
+    d, flip = STEPS[step]
+    return partner(me, (4 - d) % 4, flip)
+
+
+def pack_kernel(me_ref, in_ref, *out_refs):
+    me = me_ref[0]
+    rows = [target(me, s) for s in range(8)]
+
     def step(n, carry):
-        for i in range(8):
-            out_ref[i, 0, n] = in_ref[pl.ds(n * 8 + i, 8, stride=392), :]
+        for s in range(8):
+            out_refs[s][n] = in_ref[pl.ds(n * 8 + rows[s], 8, stride=392), :]
         return carry
 
     lax.fori_loop(0, 49, step, 0, unroll=7)
 
 
-def pack(velocity):
-    flat = velocity.reshape(3 * 16 * 392, LANES)
+def pack(me, flat, x):
     return pl.pallas_call(
         pack_kernel,
-        grid=(3, 2),
-        in_specs=[pl.BlockSpec((8 * 392, LANES), lambda x, h: (2 * x + h, 0))],
-        out_specs=pl.BlockSpec((8, 1, 49, 8, LANES), lambda x, h: (0, x, 0, h, 0)),
-        out_shape=jax.ShapeDtypeStruct((8, 3, 49, 16, LANES), F32),
-        compiler_params=params(32, 2),
+        grid=(2,),
+        in_specs=[
+            pl.BlockSpec(memory_space=pltpu.SMEM),
+            pl.BlockSpec((8 * 392, LANES), lambda h: (2 * x + h, 0)),
+        ],
+        out_specs=[pl.BlockSpec((49, 8, LANES), lambda h: (0, h, 0)) for _ in range(8)],
+        out_shape=[pltpu.HBM((49, 16, LANES), F32) for _ in range(8)],
+        compiler_params=params(FULL, 1),
         name="pack",
-    )(flat)
-
-
-def forcing_kernel(in_ref, met_ref, wp_ref, wl_ref, fh_ref, fl_ref, out_ref, xb, u, z, adv, div):
-    a = pl.program_id(0)
+    )(me, flat)
+
+
+def transform(me, block_of, w_ref, xb):
+    for s in range(8):
+        at = pl.multiple_of(origin(me, s) * 16, 16)
+        for b in range(7):
+            block = block_of(s, b)
+            hi = block.astype(BF16)
+            lo = (block - hi.astype(F32)).astype(BF16)
+            lanes = pl.ds(b * 128, 128)
+            xb[pl.ds(at, 16), lanes] = hi
+            xb[pl.ds(at + 128, 16), lanes] = lo
+            xb[pl.ds(at + 256, 16), lanes] = hi
+    return jnp.dot(w_ref[...], xb[...], preferred_element_type=F32)
+
+
+def row_copies(sources, a, slots, sems):
+    slot = a % 2
+    return [
+        pltpu.make_async_copy(ref.at[pl.ds(7 * a, 7)], slots.at[slot, i], sems.at[slot, i])
+        for i, ref in enumerate(sources)
+    ]
+
+
+def stream_rows(sources, slots, sems, work):
+    for copy in row_copies(sources, 0, slots, sems):
+        copy.start()
+
+    def step(a, carry):
+        @pl.when(a < 6)
+        def _():
+            for copy in row_copies(sources, a + 1, slots, sems):
+                copy.start()
+
+        for copy in row_copies(sources, a, slots, sems):
+            copy.wait()
+        work(a)
+        return carry
+
+    lax.fori_loop(0, 7, step, 0)
+
+
+BLOCK = [pl.ds(b * 128, 128) for b in range(7)]
+
+
+def q_rows(t, offset=0):
+    return pl.ds(pl.multiple_of(t * 8 + offset, 8), 8)
+
+
+def early_kernel(*refs):
+    me_ref, sources = refs[0], refs[1:17]
+    met_ref, w_ref = refs[17:19]
+    u, v, zu, zv, adv0, adv1, xb, slots, sems = refs[19:]
+    me = me_ref[0]
     sx = met_ref[0]
     sy = met_ref[1]
-    for x in range(3):
+
+    def node_row(a):
+        for x, (field, slope) in enumerate(((u, zu), (v, zv))):
+            both = transform(me, lambda s, b: slots[a % 2, 8 * x + s, b], w_ref, xb)
+            field[a] = both[0:128]
+            slope[a] = both[128:256]
+
+        def along_b(t, carry):
+            q = q_rows(t)
+            first = [u[a, q, s] for s in BLOCK]
+            second = [v[a, q, s] for s in BLOCK]
+            scaled = [item * sy for item in second]
+            for field, out in ((first, adv0), (second, adv1)):
+                slope = derive(field)
+                for b in range(7):
+                    out[a, q, BLOCK[b]] = scaled[b] * slope[b]
+            return carry
+
+        lax.fori_loop(0, 16, along_b, 0)
+
+    stream_rows(sources, slots, sems, node_row)
+
+    def along_a(t, carry):
+        q = q_rows(t)
+        for s in BLOCK:
+            first = [u[k, q, s] for k in range(7)]
+            second = [v[k, q, s] for k in range(7)]
+            scaled = [item * sx for item in first]
+            for field, out in ((first, adv0), (second, adv1)):
+                slope = derive(field)
+                for k in range(7):
+                    out[k, q, s] = out[k, q, s] + scaled[k] * slope[k]
+        return carry
+
+    lax.fori_loop(0, 16, along_a, 0)
+
+
+def late_kernel(*refs):
+    me_ref, sources = refs[0], refs[1:9]
+    u, v, zu, zv, adv0, adv1 = refs[9:15]
+    met_ref, w_ref, f_ref = refs[15:18]
+    outs = refs[18:26]
+    xb, w, zw, sum0, div, forward, db = refs[26:]
+    me = me_ref[0]
+    sx = met_ref[0]
+    sy = met_ref[1]
+    for s in range(8):
+        at = pl.ds(pl.multiple_of(target(me, s) * 16, 16), 16)
+        forward[s * 16 : s * 16 + 16] = f_ref[at]
+
+    def node_row(a, carry):
+        both = transform(me, lambda s, b: sources[s][7 * a + b], w_ref, xb)
+        w[a] = both[0:128]
+        zw[...] = both[128:256]
+
+        def along_b(t, carry):
+            q = q_rows(t)
+            q2 = q_rows(t, 128)
+            third = [w[a, q, s] for s in BLOCK]
+            slope = derive(third)
+            line = []
+            for b, s in enumerate(BLOCK):
+                sum0[a, q, s] = adv0[a, q, s] + third[b] * zu[a, q, s]
+                line.append(adv1[a, q, s] + third[b] * zv[a, q, s])
+                div[a, q2, s] = (v[a, q, s] * sy) * slope[b] + third[b] * zw[q, s]
+            slope = derive(line)
+            for b, s in enumerate(BLOCK):
+                div[a, q, s] = sy * slope[b]
+            return carry
+
+        lax.fori_loop(0, 16, along_b, 0)
+        return carry
+
+    lax.fori_loop(0, 7, node_row, 0)
+
+    def along_a(t, carry):
+        q = q_rows(t)
+        q2 = q_rows(t, 128)
+        for s in BLOCK:
+            slope = derive([w[k, q, s] for k in range(7)])
+            for k in range(7):
+                div[k, q2, s] = div[k, q2, s] + (u[k, q, s] * sx) * slope[k]
+            slope = derive([sum0[k, q, s] for k in range(7)])
+            for k in range(7):
+                div[k, q, s] = div[k, q, s] + sx * slope[k]
+        return carry
+
+    lax.fori_loop(0, 16, along_a, 0)
+    area = -1.0 / (sx * sy)
+    for k in range(7):
+        block = div[k]
+        hi = block.astype(BF16)
+        db[0:256] = hi
+        db[256:512] = (block - hi.astype(F32)).astype(BF16)
+        db[512:768] = hi
+        spec = jnp.dot(forward[...], db[...], preferred_element_type=F32)
         for b in range(7):
-            block = in_ref[:, x, b].reshape(128, LANES)
-            hi = block.astype(BF16)
-            lo = (block - hi.astype(F32)).astype(BF16)
-            xb[0:128, b * 128 : b * 128 + 128] = hi
-            xb[128:256, b * 128 : b * 128 + 128] = lo
-        both = jnp.dot(wp_ref[...], xb[...], preferred_element_type=F32)
-        both = both + jnp.dot(wl_ref[...], xb[0:128], preferred_element_type=F32)
-        u[x, a] = both[0:128]
-        z[x] = both[128:256]
-
-    def along_b(t, carry):
-        q = pl.ds(pl.multiple_of(t * 8, 8), 8)
-        lanes = [pl.ds(b * 128, 128) for b in range(7)]
-        fields = [[u[i, a, q, s] for s in lanes] for i in range(3)]
-        scaled = [item * sy for item in fields[1]]
-        for i in range(3):
-            slope = derive(fields[i])
-            for b in range(7):
-                adv[i, a, q, lanes[b]] = scaled[b] * slope[b] + fields[2][b] * z[i, q, lanes[b]]
-        return carry
-
-    lax.fori_loop(0, 16, along_b, 0)
-
-    @pl.when(a == 6)
-    def _():
-        def along_a(t, carry):
-            q = pl.ds(pl.multiple_of(t * 8, 8), 8)
-            q2 = pl.ds(pl.multiple_of(t * 8 + 128, 8), 8)
-            for b in range(7):
-                s = pl.ds(b * 128, 128)
-                first = [u[0, k, q, s] for k in range(7)]
-                scaled = [item * sx for item in first]
-                for i in range(3):
-                    slope = derive(first if i == 0 else [u[i, k, q, s] for k in range(7)])
-                    total = [scaled[k] * slope[k] + adv[i, k, q, s] for k in range(7)]
-                    if i == 0:
-                        total = [item * sx for item in derive(total)]
-                    for k in range(7):
-                        if i == 0:
-                            div[k, q, s] = total[k]
-                        elif i == 1:
-                            adv[1, k, q, s] = total[k]
-                        else:
-                            div[k, q2, s] = total[k]
-            for k in range(7):
-                slope = derive([adv[1, k, q, pl.ds(b * 128, 128)] for b in range(7)])
-                for b in range(7):
-                    s = pl.ds(b * 128, 128)
-                    div[k, q, s] = div[k, q, s] + sy * slope[b]
-            return carry
-
-        lax.fori_loop(0, 16, along_a, 0)
-        area = -1.0 / (sx * sy)
-        for k in range(7):
-            block = div[k]
-            hi = block.astype(BF16)
-            lo = (block - hi.astype(F32)).astype(BF16)
-            spec = jnp.dot(fh_ref[...], hi, preferred_element_type=F32)
-            spec = spec + jnp.dot(fh_ref[...], lo, preferred_element_type=F32)
-            spec = spec + jnp.dot(fl_ref[...], hi, preferred_element_type=F32)
-            for b in range(7):
-                scale = area * np.float32(WEIGHTS[k] * WEIGHTS[b])
-                out_ref[:, 7 * k + b] = (spec[:, b * 128 : b * 128 + 128] * scale).reshape(8, 16, LANES)
+            scale = area * np.float32(WEIGHTS[k] * WEIGHTS[b])
+            for s in range(8):
+                outs[s][7 * k + b] = spec[s * 16 : s * 16 + 16, b * 128 : b * 128 + 128] * scale
 
 
 def split_bf16(table):
-    table = jnp.asarray(table, F32)
-    hi = table.astype(BF16)
-    return hi, (table - hi.astype(F32)).astype(BF16)
-
-
-def forcing(gathered, met_row, basis, forward, modal_diff):
-    both = np.concatenate([basis, basis @ modal_diff], axis=0)
-    back = np.concatenate([forward, modal_diff @ forward], axis=1)
-    wh, wl = split_bf16(both)
-    fh, fl = split_bf16(back)
-    wp = jnp.concatenate([wh, wh], axis=1)
-
-    def whole(shape):
-        return pl.BlockSpec(shape, lambda a: (0,) * len(shape))
-
-    return pl.pallas_call(
-        forcing_kernel,
-        grid=(7,),
-        in_specs=[
-            pl.BlockSpec((8, 3, 7, 16, LANES), lambda a: (0, 0, a, 0, 0)),
-            whole((2, 1, LANES)),
-            whole((256, 256)),
-            whole((256, 128)),
-            whole((128, 256)),
-            whole((128, 256)),
-        ],
-        out_specs=whole((8, 49, 16, LANES)),
-        out_shape=jax.ShapeDtypeStruct((8, 49, 16, LANES), F32),
-        scratch_shapes=[
-            pltpu.VMEM((256, 896), BF16),
-            pltpu.VMEM((3, 7, 128, 896), F32),
-            pltpu.VMEM((3, 128, 896), F32),
-            pltpu.VMEM((3, 7, 128, 896), F32),
-            pltpu.VMEM((7, 256, 896), F32),
-        ],
-        compiler_params=params(56, 1),
-        name="forcing",
-    )(gathered, met_row, wp, wl, fh, fl)
+    table = table.astype(np.float32)
+    hi = table.astype(ml_dtypes.bfloat16)
+    return hi, (table - hi.astype(np.float32)).astype(ml_dtypes.bfloat16)
 
 
 def rows_of(c, n):
@@ -355,7 +432,7 @@
         west_ref[pl.ds(c * 8 + b, 1), :] = field[b][0:1]
 
 
-def apply_operator(v, c, wave, ratio, back, area, west_ref, east_ref):
+def apply_operator(v, wave, ratio, back, area):
     kind = [0, 1, 2, 3, 2, 1, 0]
     sub = lax.broadcasted_iota(jnp.int32, (8, LANES), 0)
     lane = lax.broadcasted_iota(jnp.int32, (8, LANES), 1)
@@ -380,10 +457,8 @@
             out[7 * a + b] = out[7 * a + b] + line[b] * back_w[kind[a]]
     ten = np.float32(PENALTY)
     for b in range(7):
-        west = west_ref[pl.ds(c * 8 + b, 1), :]
-        east = east_ref[pl.ds(c * 8 + b, 1), :]
-        before = jnp.where(sub == 0, west, pltpu.roll(v[42 + b], 1, 0))
-        after = jnp.where(sub == 7, east, pltpu.roll(v[b], 7, 0))
+        before = jnp.where(sub == 0, 0.0, pltpu.roll(v[42 + b], 1, 0))
+        after = jnp.where(sub == 7, 0.0, pltpu.roll(v[b], 7, 0))
         out[b] = out[b] - ten * before
         out[42 + b] = out[42 + b] - ten * after
     for a in range(7):
@@ -394,10 +469,13 @@
     return out
 
 
-def first_kernel(wave_ref, recv_ref, met_ref, r_ref, p_ref, east_ref, west_ref):
+def first_kernel(me_ref, wave_ref, *refs):
+    recv, (met_ref, r_ref, p_ref, east_ref, west_ref) = refs[:8], refs[8:]
+    rows = [origin(me_ref[0], s) for s in range(8)]
+
     def unpack(n, carry):
-        for i in range(8):
-            r_ref[pl.ds(n * 8 + i, 16, stride=392), :] = recv_ref[i, n]
+        for s in range(8):
+            r_ref[pl.ds(n * 8 + rows[s], 16, stride=392), :] = recv[s][n]
         return carry
 
     lax.fori_loop(0, 49, unpack, 0, unroll=7)
@@ -417,25 +495,41 @@
     lax.fori_loop(0, 16, step, 0)
 
 
+def rim_fix(value, kind, c, b, edge_ref):
+    sub = lax.broadcasted_iota(jnp.int32, (8, LANES), 0)
+    row = 0 if kind == "west" else 7
+    return jnp.where(sub == row, value - np.float32(PENALTY) * edge_ref[pl.ds(c * 8 + b, 1), :], value)
+
+
+def local_image_kernel(wave_ref, p_ref, met_ref, q_ref):
+    ratio, back, area = metric_values(met_ref)
+
+    def image(c, carry):
+        v = [p_ref[rows_of(c, n), :] for n in range(49)]
+        out = apply_operator(v, wave_ref[c], ratio, back, area)
+        for n in range(49):
+            q_ref[rows_of(c, n), :] = out[n]
+        return carry
+
+    lax.fori_loop(0, 16, image, 0)
+
+
 def second_kernel(
-    wave_ref, p_ref, met_ref, west_in, east_in, q_ref, s_ref, east_ref, west_ref
+    wave_ref, local_ref, met_ref, west_in, east_in, q_ref, s_ref, east_ref, west_ref
 ):
     east_ref[...] = jnp.zeros_like(east_ref)
     west_ref[...] = jnp.zeros_like(west_ref)
     ratio, back, area = metric_values(met_ref)
 
-    def image(c, carry):
-        v = [p_ref[rows_of(c, n), :] for n in range(49)]
-        out = apply_operator(v, c, wave_ref[c], ratio, back, area, west_in, east_in)
-        for n in range(49):
-            q_ref[rows_of(c, n), :] = out[n]
-        return carry
-
-    lax.fori_loop(0, 16, image, 0)
-
     def search(c, carry):
         inv = inverse_divisor(ratio, back, area, wave_ref[c])
-        field = block_solve([q_ref[rows_of(c, n), :] for n in range(49)])
+        field = [local_ref[rows_of(c, n), :] for n in range(49)]
+        for b in range(7):
+            field[b] = rim_fix(field[b], "west", c, b, west_in)
+            field[42 + b] = rim_fix(field[42 + b], "east", c, b, east_in)
+        for n in range(49):
+            q_ref[rows_of(c, n), :] = field[n]
+        field = block_solve(field)
         field = [item * inv for item in field]
         for n in range(49):
             s_ref[rows_of(c, n), :] = field[n]
@@ -445,14 +539,12 @@
     lax.fori_loop(0, 16, search, 0)
 
 
-def third_kernel(
-    wave_ref, r_ref, q_ref, s_ref, met_ref, west_in, east_in, t_ref, dots_ref, acc_ref
-):
+def third_kernel(wave_ref, r_ref, q_ref, s_ref, met_ref, t_ref, acc_ref):
     ratio, back, area = metric_values(met_ref)
 
     def image(c, carry):
         v = [s_ref[rows_of(c, n), :] for n in range(49)]
-        out = apply_operator(v, c, wave_ref[c], ratio, back, area, west_in, east_in)
+        out = apply_operator(v, wave_ref[c], ratio, back, area)
         sums = [None] * 5
         for n in range(49):
             t_ref[rows_of(c, n), :] = out[n]
@@ -464,15 +556,40 @@
         return carry
 
     lax.fori_loop(0, 16, image, 0)
+
+
+def product_kernel(r_ref, q_ref, t_ref, acc_ref, west_in, east_in, dots_ref, add_ref, table_ref, sem):
+    def step(c, carry):
+        tq = jnp.zeros((1, LANES), F32)
+        tt, rt = tq, tq
+        for b in range(7):
+            for n, row, edge_ref in ((b, 0, west_in), (42 + b, 7, east_in)):
+                at = pl.ds(c * 392 + n * 8 + row, 1)
+                change = -np.float32(PENALTY) * edge_ref[pl.ds(c * 8 + b, 1), :]
+                tq = tq + change * q_ref[at, :]
+                rt = rt + change * r_ref[at, :]
+                tt = tt + change * (2.0 * t_ref[at, :] + change)
+        for k, item in enumerate((tq, tt, rt)):
+            add_ref[k, pl.ds(c, 1), :] = item
+        return carry
+
+    lax.fori_loop(0, 16, step, 0)
     lane = lax.broadcasted_iota(jnp.int32, (16, LANES), 1)
     table = jnp.zeros((16, LANES), F32)
     for k in range(5):
-        table = jnp.where(lane == k, jnp.sum(acc_ref[k], axis=1, keepdims=True), table)
+        total = acc_ref[k] if k < 2 else acc_ref[k] + add_ref[k - 2]
+        table = jnp.where(lane == k, jnp.sum(total, axis=1, keepdims=True), table)
     for d in range(16):
-        dots_ref[d] = table
-
-
-def last_kernel(dots_ref, r_ref, p_ref, q_ref, s_ref, t_ref, pres_ref, resid_ref, coef_ref):
+        table_ref[d] = table
+    copy = pltpu.make_async_copy(table_ref, dots_ref, sem)
+    copy.start()
+    copy.wait()
+
+
+def last_kernel(
+    dots_ref, r_ref, p_ref, q_ref, s_ref, t_ref, west_in, east_in,
+    pres_ref, resid_ref, coef_ref, pres_buf, resid_buf, sems,
+):
     total = dots_ref[0]
     for d in range(1, 16):
         total = total + dots_ref[d]
@@ -488,34 +605,61 @@
     coef_ref[0] = jnp.broadcast_to(alpha - lam * gamma, (16, LANES))
     coef_ref[1] = jnp.broadcast_to(lam, (16, LANES))
 
+    def copies(c):
+        at = pl.ds(pl.multiple_of(c * 392, 8), 392)
+        return (
+            pltpu.make_async_copy(pres_buf.at[at, :], pres_ref.at[at, :], sems.at[0, c]),
+            pltpu.make_async_copy(resid_buf.at[at, :], resid_ref.at[at, :], sems.at[1, c]),
+        )
+
     def step(c, carry):
         first = coef_ref[0, pl.ds(c, 1), :]
         second = coef_ref[1, pl.ds(c, 1), :]
         for n in range(49):
             at = rows_of(c, n)
-            pres_ref[at, :] = first * p_ref[at, :] + second * s_ref[at, :]
-            resid_ref[at, :] = r_ref[at, :] - first * q_ref[at, :] - second * t_ref[at, :]
+            t = t_ref[at, :]
+            if n < 7:
+                t = rim_fix(t, "west", c, n, west_in)
+            if n >= 42:
+                t = rim_fix(t, "east", c, n - 42, east_in)
+            pres_buf[at, :] = first * p_ref[at, :] + second * s_ref[at, :]
+            resid_buf[at, :] = r_ref[at, :] - first * q_ref[at, :] - second * t
+        for copy in copies(c):
+            copy.start()
         return carry
 
     lax.fori_loop(0, 16, step, 0)
+
+    def finish(c, carry):
+        for copy in copies(c):
+            copy.wait()
+        return carry
+
+    lax.fori_loop(0, 16, finish, 0)
 
 
 FIELD = (16 * 392, LANES)
 RIM = (16 * 8, LANES)
 
 
-def call(kernel, name, inputs, smem, outs, limit, scratch=()):
+def call(kernel, name, inputs, outs, limit, scratch=(), smem=(), any_in=(), hbm=(), cost=None):
     specs = [
-        pl.BlockSpec(memory_space=pltpu.SMEM if i in smem else pltpu.VMEM)
+        pl.BlockSpec(
+            memory_space=pltpu.SMEM if i in smem else pl.ANY if i in any_in else pltpu.VMEM
+        )
         for i in range(len(inputs))
+    ]
+    out_specs = [
+        pl.BlockSpec(memory_space=pltpu.HBM if i in hbm else pltpu.VMEM) for i in range(len(outs))
     ]
     return pl.pallas_call(
         kernel,
         in_specs=specs,
-        out_specs=tuple(pl.BlockSpec(memory_space=pltpu.VMEM) for _ in outs),
-        out_shape=tuple(jax.ShapeDtypeStruct(s, F32) for s in outs),
+        out_specs=out_specs,
+        out_shape=[jax.ShapeDtypeStruct(s, F32) for s in outs],
         scratch_shapes=list(scratch),
         compiler_params=params(limit),
+        cost_estimate=cost and pl.CostEstimate(flops=0, bytes_accessed=cost, transcendentals=0),
         name=name,
     )(*inputs)
 
@@ -524,13 +668,58 @@
     modes_here = velocity.shape[1]
     basis, forward, modal_diff, wave_all = mode_tables(modes_here * lax.axis_size("fourier"))
     mine = lax.axis_index("fourier")
+    me = mine.astype(jnp.int32).reshape(1)
     wave = lax.dynamic_slice_in_dim(jnp.asarray(wave_all, F32), mine * modes_here, modes_here)
     met_row = lax.dynamic_slice_in_dim(metric, mine, 1, 1)
-
-    packed = pack(velocity)
-    gathered = lax.all_to_all(packed, "fourier", 0, 0, tiled=True)
-    source = forcing(gathered, met_row, basis, forward, modal_diff)
-    recv = lax.all_to_all(source, "fourier", 0, 0, tiled=True)
+    hi, lo = split_bf16(np.concatenate([basis, basis @ modal_diff], axis=0))
+    to_planes = jnp.asarray(np.concatenate([hi, hi, lo], axis=1))
+    hi, lo = split_bf16(np.concatenate([forward, modal_diff @ forward], axis=1))
+    to_modes = jnp.asarray(np.concatenate([hi, hi, lo], axis=1))
+
+    flat = pltpu.with_memory_space_constraint(velocity.reshape(3 * 16 * 392, LANES), pltpu.HBM)
+    gathered = []
+    for x in range(3):
+        packed = pack(me, flat, x)
+        blocks = [packed[0]] + [permute(packed[s], s) for s in range(1, 8)]
+        if x < 2:
+            blocks = [pltpu.with_memory_space_constraint(item, pltpu.HBM) for item in blocks]
+        gathered.append(blocks)
+
+    plane_field = (7, 128, 896)
+    early = call(
+        early_kernel,
+        "early",
+        (me, *gathered[0], *gathered[1], met_row, to_planes),
+        [plane_field] * 6,
+        8,
+        [
+            pltpu.VMEM((384, 896), BF16),
+            pltpu.VMEM((2, 16, 7, 16, LANES), F32),
+            pltpu.SemaphoreType.DMA((2, 16)),
+        ],
+        smem=(0,),
+        any_in=range(1, 17),
+        cost=40 * MIB,
+    )
+    source = call(
+        late_kernel,
+        "late",
+        (me, *gathered[2], *early, met_row, to_planes, to_modes),
+        [(49, 16, LANES)] * 8,
+        22,
+        [
+            pltpu.VMEM((384, 896), BF16),
+            pltpu.VMEM(plane_field, F32),
+            pltpu.VMEM((128, 896), F32),
+            pltpu.VMEM(plane_field, F32),
+            pltpu.VMEM((7, 256, 896), F32),
+            pltpu.VMEM((128, 768), BF16),
+            pltpu.VMEM((768, 896), BF16),
+        ],
+        smem=(0,),
+        cost=40 * MIB,
+    )
+    recv = [source[0]] + [permute(source[s], s) for s in range(1, 8)]
 
     size = lax.axis_size("plane")
     up = [(i, i + 1) for i in range(size - 1)]
@@ -540,36 +729,62 @@
         return lax.ppermute(east, "plane", up), lax.ppermute(west, "plane", down)
 
     r, p1, east, west = call(
-        first_kernel, "first", (wave, recv, metric), (0,), (FIELD, FIELD, RIM, RIM), 40
+        first_kernel,
+        "first",
+        (me, wave, *recv, metric),
+        [FIELD, FIELD, RIM, RIM],
+        24,
+        smem=(0, 1),
     )
     west_in, east_in = exchange(east, west)
+    (local,) = call(
+        local_image_kernel, "local_image", (wave, p1, metric), [FIELD], 16, smem=(0,), cost=8 * MIB
+    )
     q1, s, east, west = call(
         second_kernel,
         "second",
-        (wave, p1, metric, west_in, east_in),
-        (0,),
-        (FIELD, FIELD, RIM, RIM),
-        40,
+        (wave, local, metric, west_in, east_in),
+        [FIELD, FIELD, RIM, RIM],
+        16,
+        smem=(0,),
     )
     west_in, east_in = exchange(east, west)
-    t, dots = call(
+    t, acc = call(
         third_kernel,
         "third",
-        (wave, r, q1, s, metric, west_in, east_in),
-        (0,),
-        (FIELD, (16, 16, LANES)),
-        40,
-        [pltpu.VMEM((5, 16, LANES), F32)],
+        (wave, r, q1, s, metric),
+        [FIELD, (5, 16, LANES)],
+        16,
+        smem=(0,),
+        cost=12 * MIB,
+    )
+    (dots,) = call(
+        product_kernel,
+        "products",
+        (r, q1, t, acc, west_in, east_in),
+        [(16, 16, LANES)],
+        16,
+        [
+            pltpu.VMEM((3, 16, LANES), F32),
+            pltpu.VMEM((16, 16, LANES), F32),
+            pltpu.SemaphoreType.DMA,
+        ],
+        hbm=(0,),
     )
     dots = lax.all_to_all(dots, "plane", 0, 0, tiled=True)
     pressure, residual = call(
         last_kernel,
         "last",
-        (dots, r, p1, q1, s, t),
-        (),
-        (FIELD, FIELD),
-        40,
-        [pltpu.VMEM((2, 16, LANES), F32)],
+        (dots, r, p1, q1, s, t, west_in, east_in),
+        [FIELD, FIELD],
+        24,
+        [
+            pltpu.VMEM((2, 16, LANES), F32),
+            pltpu.VMEM(FIELD, F32),
+            pltpu.VMEM(FIELD, F32),
+            pltpu.SemaphoreType.DMA((2, 16)),
+        ],
+        hbm=(0, 1),
     )
     shape = velocity.shape[1:]
     return pressure.reshape(shape), residual.reshape(shape)

time: 247 us -> 214 us (0.87)
  waiting for transfers between devices: 156 us -> 97 us
  starting transfers between devices: 19.3 us -> 41.7 us
  Pallas kernels: 44.5 us -> 56.1 us
  local copies, waits for them, and re-layouts: 9.75 us -> 0.17 us
    all_to_all x2 -> x0, waiting for transfers between devices: 146 us -> none  [the longest x1 107 us: body(): gathered = lax.all_to_all(packed, 'fourier', 0, 0, tiled=True)]
    ppermute x0 -> x28, waiting for transfers between devices: none -> 95.2 us  [permute(): lax.ppermute(value, 'fourier', [(i, partner(i, d, flip)) for i in range(8)])]
    ppermute x0 -> x28, starting transfers between devices: none -> 31.4 us  [permute(): lax.ppermute(value, 'fourier', [(i, partner(i, d, flip)) for i in range(8)])]
    pallas_call x6 -> x11, Pallas kernels: 44.5 us -> 56.1 us  [the longest x8 45 us: call(): pl.pallas_call(kernel, in_specs=specs, out_specs=out_specs, out_shape=[ja...]
    unnamed x10 -> x36, local copies, waits for them, and re-layouts: 9.1 us -> 0.08 us
    all_to_all x2 -> x0, starting transfers between devices: 9.02 us -> none  [the longest x1 5.23 us: body(): gathered = lax.all_to_all(packed, 'fourier', 0, 0, tiled=True)]
    ppermute x4, waiting for transfers between devices: 9.72 us -> 1.8 us  [exchange(): return (lax.ppermute(east, 'plane', up), lax.ppermute(west, 'plane', down))]
  transfers between devices with their start and end apart: 6 -> 32, of which waited for: 6 -> 20; matrix products, arithmetic and copies ran while one was open for 0% -> 0% of each run, Pallas kernels for 0% -> 13%
where the time goes in v2:
time: 214 us; the launch traced here: 213 us
  waiting for transfers between devices  97 us (45%)
  Pallas kernels  56.1 us (26%)
  starting transfers between devices  41.7 us (19%)
  blocking collectives  17.1 us (8%)
    ppermute x28, waiting for transfers between devices, permute(): lax.ppermute(value, 'fourier', [(i, partner(i, d, flip)) for i in range(8)])  95.2 us
    pallas_call x8, Pallas kernels, call(): pl.pallas_call(kernel, in_specs=specs, out_specs=out_specs, out_shape=[ja...  45 us
    ppermute x28, starting transfers between devices, permute(): lax.ppermute(value, 'fourier', [(i, partner(i, d, flip)) for i in range(8)])  31.4 us
    all_to_all x1, blocking collectives, body(): dots = lax.all_to_all(dots, 'plane', 0, 0, tiled=True)  17.1 us
    pallas_call x3, Pallas kernels, pack(): pl.pallas_call(pack_kernel, grid=(2,), in_specs=[pl.BlockSpec(memory_spac...  11.1 us
    ppermute x4, starting transfers between devices, exchange(): return (lax.ppermute(east, 'plane', up), lax.ppermute(west, 'plane', down))  10.2 us
  transfers between devices with their start and end apart: 32, of which 20 were waited for; matrix products, arithmetic and copies ran while one was open for 0% of the time, Pallas kernels for 13%

profile of v2, /device:TPU:0, one launch (start us, length us, event | category | flops | bytes accessed | tf_op | source)
XLA Modules:
  0.0 213.2 jit_solution(234917257694941095)
XLA Ops:
  0.6 3.6 %pack.4 = (f32[49,16,128]{2,1,0:T(8,128)}, f32[49,16,128]{2,1,0:T(8,128)}, f32[49,16,128]{2,1,0:T(8,128)}, f32[49,16,128]{2,1,0:T(8,128)}, f32[49,16,128]{2,1,0:...) custom-call(s32[1]{0:T(128)} %bitcast.me_ref.refs_0_, f32[18816,128]{1,0:T(8,128)} %bitcast.4), custom_call_target="tpu_custom_call" | custom-call | tf_op jit(solution)/shard_map/pack/pallas_call | solution.py:238
  9.4 3.7 %pack.5 = (f32[49,16,128]{2,1,0:T(8,128)}, f32[49,16,128]{2,1,0:T(8,128)}, f32[49,16,128]{2,1,0:T(8,128)}, f32[49,16,128]{2,1,0:T(8,128)}, f32[49,16,128]{2,1,0:...) custom-call(s32[1]{0:T(128)} %bitcast.me_ref.refs_0_, f32[18816,128]{1,0:T(8,128)} %bitcast.5), custom_call_target="tpu_custom_call" | custom-call | tf_op jit(solution)/shard_map/pack/pallas_call | solution.py:238
  19.1 6.1 %collective-permute-done.11.refs_6_ = f32[49,16,128]{2,1,0:T(8,128)S(1)} collective-permute-done((f32[49,16,128]{2,1,0:T(8,128)}, f32[49,16,128]{2,1,0:T(8,128)S(1)}, u32[]{:S(2)}, u32[]{:S(2)}) %collective-permute-start.11) | collective-permute-done | bytes 401440 | tf_op jit(solution)/shard_map/ppermute | solution.py:213
  30.2 5.0 %collective-permute-done.14.refs_10_ = f32[49,16,128]{2,1,0:T(8,128)S(1)} collective-permute-done((f32[49,16,128]{2,1,0:T(8,128)}, f32[49,16,128]{2,1,0:T(8,128)S(1)}, u32[]{:S(2)}, u32[]{:S(2)}) %collective-permute-start.14) | collective-permute-done | bytes 401440 | tf_op jit(solution)/shard_map/ppermute | solution.py:213
  36.3 6.1 %collective-permute-done.15.refs_11_ = f32[49,16,128]{2,1,0:T(8,128)S(1)} collective-permute-done((f32[49,16,128]{2,1,0:T(8,128)}, f32[49,16,128]{2,1,0:T(8,128)S(1)}, u32[]{:S(2)}, u32[]{:S(2)}) %collective-permute-start.15) | collective-permute-done | bytes 401440 | tf_op jit(solution)/shard_map/ppermute | solution.py:213
  42.5 3.8 %pack.3 = (f32[49,16,128]{2,1,0:T(8,128)}, f32[49,16,128]{2,1,0:T(8,128)}, f32[49,16,128]{2,1,0:T(8,128)}, f32[49,16,128]{2,1,0:T(8,128)}, f32[49,16,128]{2,1,0:...) custom-call(s32[1]{0:T(128)} %bitcast.me_ref.refs_0_, f32[18816,128]{1,0:T(8,128)} %bitcast.6), custom_call_target="tpu_custom_call" | custom-call | tf_op jit(solution)/shard_map/pack/pallas_call | solution.py:238
  53.6 5.9 %collective-permute-done.18.refs_14_ = f32[49,16,128]{2,1,0:T(8,128)S(1)} collective-permute-done((f32[49,16,128]{2,1,0:T(8,128)}, f32[49,16,128]{2,1,0:T(8,128)S(1)}, u32[]{:S(2)}, u32[]{:S(2)}) %collective-permute-start.18) | collective-permute-done | bytes 401440 | tf_op jit(solution)/shard_map/ppermute | solution.py:213
  65.1 4.1 %collective-permute-done.7.refs_2_ = f32[49,16,128]{2,1,0:T(8,128)S(1)} collective-permute-done((f32[49,16,128]{2,1,0:T(8,128)S(1)}, f32[49,16,128]{2,1,0:T(8,128)S(1)}, u32[]{:S(2)}, u32[]{:S(2)}) %collective-permute-start.7) | collective-permute-done | bytes 401440 | tf_op jit(solution)/shard_map/ppermute | solution.py:213
  70.9 5.8 %collective-permute-done.8.refs_3_ = f32[49,16,128]{2,1,0:T(8,128)S(1)} collective-permute-done((f32[49,16,128]{2,1,0:T(8,128)}, f32[49,16,128]{2,1,0:T(8,128)S(1)}, u32[]{:S(2)}, u32[]{:S(2)}) %collective-permute-start.8) | collective-permute-done | bytes 401440 | tf_op jit(solution)/shard_map/ppermute | solution.py:213
  80.5 5.9 %collective-permute-done.refs_2_ = f32[49,16,128]{2,1,0:T(8,128)S(1)} collective-permute-done((f32[49,16,128]{2,1,0:T(8,128)}, f32[49,16,128]{2,1,0:T(8,128)S(1)}, u32[]{:S(2)}, u32[]{:S(2)}) %collective-permute-start) | collective-permute-done | bytes 401440 | tf_op jit(solution)/shard_map/ppermute | solution.py:213
  87.8 6.0 %collective-permute-done.1.refs_3_ = f32[49,16,128]{2,1,0:T(8,128)S(1)} collective-permute-done((f32[49,16,128]{2,1,0:T(8,128)}, f32[49,16,128]{2,1,0:T(8,128)S(1)}, u32[]{:S(2)}, u32[]{:S(2)}) %collective-permute-start.1) | collective-permute-done | bytes 401440 | tf_op jit(solution)/shard_map/ppermute | solution.py:213
  93.9 12.5 %early.1 = (f32[7,128,896]{2,1,0:T(8,128)S(1)}, f32[7,128,896]{2,1,0:T(8,128)S(1)}, f32[7,128,896]{2,1,0:T(8,128)S(1)}, f32[7,128,896]{2,1,0:T(8,128)S(1)}, f32[...) custom-call(s32[1]{0:T(128)} %bitcast.me_ref.refs_0_, f32[49,16,128]{2,1,0:T(8,128)} %get-tuple-element.60.refs_1_, ...), custom_call_target="tpu_custom_call" | custom-call | bytes 41943040 | tf_op jit(solution)/shard_map/early/pallas_call | solution.py:655
  106.4 7.0 %collective-permute-done.5.refs_7_ = f32[49,16,128]{2,1,0:T(8,128)S(1)} collective-permute-done((f32[49,16,128]{2,1,0:T(8,128)}, f32[49,16,128]{2,1,0:T(8,128)S(1)}, u32[]{:S(2)}, u32[]{:S(2)}) %collective-permute-start.5) | collective-permute-done | bytes 401440 | tf_op jit(solution)/shard_map/ppermute | solution.py:213
  113.4 13.6 %late.1 = (f32[49,16,128]{2,1,0:T(8,128)S(1)}, f32[49,16,128]{2,1,0:T(8,128)S(1)}, f32[49,16,128]{2,1,0:T(8,128)S(1)}, f32[49,16,128]{2,1,0:T(8,128)}, f32[49,16...) custom-call(s32[1]{0:T(128)} %bitcast.me_ref.refs_0_, ...), custom_call_target="tpu_custom_call" | custom-call | bytes 41943040 | tf_op jit(solution)/shard_map/late/pallas_call | solution.py:655
  133.2 15.8 %collective-permute-done.21.refs_1_ = f32[49,16,128]{2,1,0:T(8,128)S(1)} collective-permute-done((f32[49,16,128]{2,1,0:T(8,128)S(1)}, f32[49,16,128]{2,1,0:T(8,128)S(1)}, u32[]{:S(2)}, u32[]{:S(2)}) %collective-permute-start.21) | collective-permute-done | bytes 401440 | tf_op jit(solution)/shard_map/ppermute | solution.py:213
  149.1 6.8 %collective-permute-done.24.refs_4_ = f32[49,16,128]{2,1,0:T(8,128)S(1)} collective-permute-done((f32[49,16,128]{2,1,0:T(8,128)}, f32[49,16,128]{2,1,0:T(8,128)S(1)}, u32[]{:S(2)}, u32[]{:S(2)}) %collective-permute-start.24) | collective-permute-done | bytes 401440 | tf_op jit(solution)/shard_map/ppermute | solution.py:213
  155.9 8.8 %collective-permute-done.25.refs_5_ = f32[49,16,128]{2,1,0:T(8,128)S(1)} collective-permute-done((f32[49,16,128]{2,1,0:T(8,128)}, f32[49,16,128]{2,1,0:T(8,128)S(1)}, u32[]{:S(2)}, u32[]{:S(2)}) %collective-permute-start.25) | collective-permute-done | bytes 401440 | tf_op jit(solution)/shard_map/ppermute | solution.py:213
  164.8 3.8 %first.1 = (f32[6272,128]{1,0:T(8,128)S(1)}, f32[6272,128]{1,0:T(8,128)S(1)}, f32[128,128]{1,0:T(8,128)S(1)}, f32[128,128]{1,0:T(8,128)S(1)}) custom-call(s32[1]{0:T(128)} %bitcast.me_ref.refs_0_, f32[16]{0:T(128)S(1)} %dynamic_slice.6.wave_ref, f32[49,16,128]{2,1,0:T(8,128)S(1)} %get-tuple-element.82.refs_0_, ...), custom_call_target="tpu_custom_call" | custom-call | tf_op jit(solution)/shard_map/first/pallas_call | solution.py:655
  168.7 3.8 %collective-permute-start.28 = (f32[128,128]{1,0:T(8,128)S(1)}, f32[128,128]{1,0:T(8,128)S(1)}, u32[]{:S(2)}, u32[]{:S(2)}) collective-permute-start(f32[128,128]{1,0:T(8,128)S(1)} %get-tuple-element.92), channel_id=1, source_target_pairs={{0,8},{8,16},{16,24},{24,32},{32,40},{40,48},{48,56},{56,64},{64,7... | collective-permute-start | bytes 196616 | tf_op jit(solution)/shard_map/ppermute | solution.py:729
  173.8 3.4 %local_image.1.local_ref = f32[6272,128]{1,0:T(8,128)S(1)} custom-call(f32[16]{0:T(128)S(1)} %dynamic_slice.6.wave_ref, f32[6272,128]{1,0:T(8,128)S(1)} %get-tuple-element.91.p_ref, f32[2,8,128]{2,1,0:T(8,128)S(1)} %copy-done.3), custom_call_target="tpu_custom_call" | custom-call | bytes 8388608 | tf_op jit(solution)/shard_map/local_image/pallas_call | solution.py:655
  178.7 3.4 %second.1 = (f32[6272,128]{1,0:T(8,128)S(1)}, f32[6272,128]{1,0:T(8,128)S(1)}, f32[128,128]{1,0:T(8,128)S(1)}, f32[128,128]{1,0:T(8,128)S(1)}) custom-call(f32[16]{0:T(128)S(1)} %dynamic_slice.6.wave_ref, f32[6272,128]{1,0:T(8,128)S(1)} %local_image.1.local_ref, f32[2,8,128]{2,1,0:T(8,128)S(1)} %copy-done.3, f32[128,128]{1,0:T(8,128)S(1)} %collective-permute-done.28.west_in, ...), custom_call_target="tpu_custom_call" | custom-call | tf_op jit(solution)/shard_map/second/pallas_call | solution.py:655
  182.1 3.8 %collective-permute-start.30 = (f32[128,128]{1,0:T(8,128)S(1)}, f32[128,128]{1,0:T(8,128)S(1)}, u32[]{:S(2)}, u32[]{:S(2)}) collective-permute-start(f32[128,128]{1,0:T(8,128)S(1)} %get-tuple-element.98), channel_id=1, source_target_pairs={{0,8},{8,16},{16,24},{24,32},{32,40},{40,48},{48,56},{56,64},{64,7... | collective-permute-start | bytes 196616 | tf_op jit(solution)/shard_map/ppermute | solution.py:729
  187.2 4.5 %third.1 = (f32[6272,128]{1,0:T(8,128)S(1)}, f32[5,16,128]{2,1,0:T(8,128)S(1)}) custom-call(f32[16]{0:T(128)S(1)} %dynamic_slice.6.wave_ref, f32[6272,128]{1,0:T(8,128)S(1)} %get-tuple-element.90.r_ref, f32[6272,128]{1,0:T(8,128)S(1)} %get-tuple-element.94.q_ref, f32[6272,128]{1,0:T(8,128)S(1)} %get-tuple-element.95.s_ref, f32[2,8,128]{2,1,0:T(8,128)S(1)} %copy-done.3), custom_call_target="tpu_custom_call" | custom-call | bytes 12582912 | tf_op jit(solution)/shard_map/third/pallas_call | solution.py:655
  192.8 17.1 %all_to_all.5.dots_ref = f32[16,16,128]{2,1,0:T(8,128)S(1)} all-to-all(f32[16,16,128]{2,1,0:T(8,128)S(1)} %products.1), channel_id=1, replica_groups=mesh['plane'=16,'fourier'=8] {'plane'}, dimensions={0} | all-to-all | bytes 262144 | tf_op jit(solution)/shard_map/all_to_all | solution.py:774
  (90 shorter events, 51.7 us)
Async XLA Ops:
  5.3 19.9 %collective-permute-start.11 = (f32[49,16,128]{2,1,0:T(8,128)}, f32[49,16,128]{2,1,0:T(8,128)S(1)}, u32[]{:S(2)}, u32[]{:S(2)}) collective-permute-start(f32[49,16,128]{2,1,0:T(8,128)} %get-tuple-element.65), channel_id=1, source_target_pairs={{0,7},{1,6},{2,1},{3,0},{4,3},{5,2},{6,5},{7,4},{8,15},{9,14},{10,... | collective-permute-start | bytes 1204232 | tf_op jit(solution)/shard_map/ppermute | solution.py:213
  7.2 20.1 %collective-permute-start.12 = (f32[49,16,128]{2,1,0:T(8,128)}, f32[49,16,128]{2,1,0:T(8,128)S(1)}, u32[]{:S(2)}, u32[]{:S(2)}) collective-permute-start(f32[49,16,128]{2,1,0:T(8,128)} %get-tuple-element.66), channel_id=1, source_target_pairs={{0,5},{1,4},{2,7},{3,6},{4,1},{5,0},{6,3},{7,2},{8,13},{9,12},{10,... | collective-permute-start | bytes 1204232 | tf_op jit(solution)/shard_map/ppermute | solution.py:213
  8.7 20.6 %collective-permute-start.13 = (f32[49,16,128]{2,1,0:T(8,128)}, f32[49,16,128]{2,1,0:T(8,128)S(1)}, u32[]{:S(2)}, u32[]{:S(2)}) collective-permute-start(f32[49,16,128]{2,1,0:T(8,128)} %get-tuple-element.67), channel_id=1, source_target_pairs={{0,1},{1,0},{2,3},{3,2},{4,5},{5,4},{6,7},{7,6},{8,9},{9,8},{10,11... | collective-permute-start | bytes 1204232 | tf_op jit(solution)/shard_map/ppermute | solution.py:213
  13.1 22.2 %collective-permute-start.14 = (f32[49,16,128]{2,1,0:T(8,128)}, f32[49,16,128]{2,1,0:T(8,128)S(1)}, u32[]{:S(2)}, u32[]{:S(2)}) collective-permute-start(f32[49,16,128]{2,1,0:T(8,128)} %get-tuple-element.69), channel_id=1, source_target_pairs={{0,2},{1,3},{2,4},{3,5},{4,6},{5,7},{6,0},{7,1},{8,10},{9,11},{10,... | collective-permute-start | bytes 1204232 | tf_op jit(solution)/shard_map/ppermute | solution.py:213
  16.9 25.5 %collective-permute-start.15 = (f32[49,16,128]{2,1,0:T(8,128)}, f32[49,16,128]{2,1,0:T(8,128)S(1)}, u32[]{:S(2)}, u32[]{:S(2)}) collective-permute-start(f32[49,16,128]{2,1,0:T(8,128)} %get-tuple-element.70), channel_id=1, source_target_pairs={{0,6},{1,7},{2,0},{3,1},{4,2},{5,3},{6,4},{7,5},{8,14},{9,15},{10,... | collective-permute-start | bytes 1204232 | tf_op jit(solution)/shard_map/ppermute | solution.py:213
  25.2 21.2 %collective-permute-start.16 = (f32[49,16,128]{2,1,0:T(8,128)}, f32[49,16,128]{2,1,0:T(8,128)S(1)}, u32[]{:S(2)}, u32[]{:S(2)}) collective-permute-start(f32[49,16,128]{2,1,0:T(8,128)} %get-tuple-element.71), channel_id=1, source_target_pairs={{0,4},{1,5},{2,6},{3,7},{4,0},{5,1},{6,2},{7,3},{8,12},{9,13},{10,... | collective-permute-start | bytes 1204232 | tf_op jit(solution)/shard_map/ppermute | solution.py:213
  27.3 23.6 %collective-permute-start.17 = (f32[49,16,128]{2,1,0:T(8,128)}, f32[49,16,128]{2,1,0:T(8,128)S(1)}, u32[]{:S(2)}, u32[]{:S(2)}) collective-permute-start(f32[49,16,128]{2,1,0:T(8,128)} %get-tuple-element.72), channel_id=1, source_target_pairs={{0,3},{1,2},{2,5},{3,4},{4,7},{5,6},{6,1},{7,0},{8,11},{9,10},{10,... | collective-permute-start | bytes 1204232 | tf_op jit(solution)/shard_map/ppermute | solution.py:213
  29.3 30.2 %collective-permute-start.18 = (f32[49,16,128]{2,1,0:T(8,128)}, f32[49,16,128]{2,1,0:T(8,128)S(1)}, u32[]{:S(2)}, u32[]{:S(2)}) collective-permute-start(f32[49,16,128]{2,1,0:T(8,128)} %get-tuple-element.73), channel_id=1, source_target_pairs={{0,7},{1,6},{2,1},{3,0},{4,3},{5,2},{6,5},{7,4},{8,15},{9,14},{10,... | collective-permute-start | bytes 1204232 | tf_op jit(solution)/shard_map/ppermute | solution.py:213
  35.2 26.6 %collective-permute-start.19 = (f32[49,16,128]{2,1,0:T(8,128)}, f32[49,16,128]{2,1,0:T(8,128)}, u32[]{:S(2)}, u32[]{:S(2)}) collective-permute-start(f32[49,16,128]{2,1,0:T(8,128)} %get-tuple-element.74), channel_id=1, source_target_pairs={{0,5},{1,4},{2,7},{3,6},{4,1},{5,0},{6,3},{7,2},{8,13},{9,12},{10,... | collective-permute-start | bytes 1204232 | tf_op jit(solution)/shard_map/ppermute | solution.py:213
  42.4 22.4 %collective-permute-start.20 = (f32[49,16,128]{2,1,0:T(8,128)}, f32[49,16,128]{2,1,0:T(8,128)}, u32[]{:S(2)}, u32[]{:S(2)}) collective-permute-start(f32[49,16,128]{2,1,0:T(8,128)} %get-tuple-element.75), channel_id=1, source_target_pairs={{0,1},{1,0},{2,3},{3,2},{4,5},{5,4},{6,7},{7,6},{8,9},{9,8},{10,11... | collective-permute-start | bytes 1204232 | tf_op jit(solution)/shard_map/ppermute | solution.py:213
  46.4 22.8 %collective-permute-start.7 = (f32[49,16,128]{2,1,0:T(8,128)S(1)}, f32[49,16,128]{2,1,0:T(8,128)S(1)}, u32[]{:S(2)}, u32[]{:S(2)}) collective-permute-start(f32[49,16,128]{2,1,0:T(8,128)S(1)} %copy-done.16), channel_id=1, source_target_pairs={{0,2},{1,3},{2,4},{3,5},{4,6},{5,7},{6,0},{7,1},{8,10},{9,11},{10,... | collective-permute-start | bytes 1204232 | tf_op jit(solution)/shard_map/ppermute | solution.py:213
  50.9 25.8 %collective-permute-start.8 = (f32[49,16,128]{2,1,0:T(8,128)}, f32[49,16,128]{2,1,0:T(8,128)S(1)}, u32[]{:S(2)}, u32[]{:S(2)}) collective-permute-start(f32[49,16,128]{2,1,0:T(8,128)} %get-tuple-element.62), channel_id=1, source_target_pairs={{0,6},{1,7},{2,0},{3,1},{4,2},{5,3},{6,4},{7,5},{8,14},{9,15},{10,... | collective-permute-start | bytes 1204232 | tf_op jit(solution)/shard_map/ppermute | solution.py:213
  59.5 19.5 %collective-permute-start.9 = (f32[49,16,128]{2,1,0:T(8,128)}, f32[49,16,128]{2,1,0:T(8,128)S(1)}, u32[]{:S(2)}, u32[]{:S(2)}) collective-permute-start(f32[49,16,128]{2,1,0:T(8,128)} %get-tuple-element.63), channel_id=1, source_target_pairs={{0,4},{1,5},{2,6},{3,7},{4,0},{5,1},{6,2},{7,3},{8,12},{9,13},{10,... | collective-permute-start | bytes 1204232 | tf_op jit(solution)/shard_map/ppermute | solution.py:213
  61.9 24.6 %collective-permute-start = (f32[49,16,128]{2,1,0:T(8,128)}, f32[49,16,128]{2,1,0:T(8,128)S(1)}, u32[]{:S(2)}, u32[]{:S(2)}) collective-permute-start(f32[49,16,128]{2,1,0:T(8,128)} %get-tuple-element.53), channel_id=1, source_target_pairs={{0,2},{1,3},{2,4},{3,5},{4,6},{5,7},{6,0},{7,1},{8,10},{9,11},{10,... | collective-permute-start | bytes 1204232 | tf_op jit(solution)/shard_map/ppermute | solution.py:213
  64.8 29.0 %collective-permute-start.1 = (f32[49,16,128]{2,1,0:T(8,128)}, f32[49,16,128]{2,1,0:T(8,128)S(1)}, u32[]{:S(2)}, u32[]{:S(2)}) collective-permute-start(f32[49,16,128]{2,1,0:T(8,128)} %get-tuple-element.54), channel_id=1, source_target_pairs={{0,6},{1,7},{2,0},{3,1},{4,2},{5,3},{6,4},{7,5},{8,14},{9,15},{10,... | collective-permute-start | bytes 1204232 | tf_op jit(solution)/shard_map/ppermute | solution.py:213
  69.2 37.2 %collective-permute-start.2 = (f32[49,16,128]{2,1,0:T(8,128)}, f32[49,16,128]{2,1,0:T(8,128)S(1)}, u32[]{:S(2)}, u32[]{:S(2)}) collective-permute-start(f32[49,16,128]{2,1,0:T(8,128)} %get-tuple-element.55), channel_id=1, source_target_pairs={{0,4},{1,5},{2,6},{3,7},{4,0},{5,1},{6,2},{7,3},{8,12},{9,13},{10,... | collective-permute-start | bytes 1204232 | tf_op jit(solution)/shard_map/ppermute | solution.py:213
  76.7 29.7 %collective-permute-start.3 = (f32[49,16,128]{2,1,0:T(8,128)}, f32[49,16,128]{2,1,0:T(8,128)S(1)}, u32[]{:S(2)}, u32[]{:S(2)}) collective-permute-start(f32[49,16,128]{2,1,0:T(8,128)} %get-tuple-element.56), channel_id=1, source_target_pairs={{0,3},{1,2},{2,5},{3,4},{4,7},{5,6},{6,1},{7,0},{8,11},{9,10},{10,... | collective-permute-start | bytes 1204232 | tf_op jit(solution)/shard_map/ppermute | solution.py:213
  79.0 27.4 %collective-permute-start.4 = (f32[49,16,128]{2,1,0:T(8,128)}, f32[49,16,128]{2,1,0:T(8,128)S(1)}, u32[]{:S(2)}, u32[]{:S(2)}) collective-permute-start(f32[49,16,128]{2,1,0:T(8,128)} %get-tuple-element.57), channel_id=1, source_target_pairs={{0,7},{1,6},{2,1},{3,0},{4,3},{5,2},{6,5},{7,4},{8,15},{9,14},{10,... | collective-permute-start | bytes 1204232 | tf_op jit(solution)/shard_map/ppermute | solution.py:213
  86.4 27.0 %collective-permute-start.5 = (f32[49,16,128]{2,1,0:T(8,128)}, f32[49,16,128]{2,1,0:T(8,128)S(1)}, u32[]{:S(2)}, u32[]{:S(2)}) collective-permute-start(f32[49,16,128]{2,1,0:T(8,128)} %get-tuple-element.58), channel_id=1, source_target_pairs={{0,5},{1,4},{2,7},{3,6},{4,1},{5,0},{6,3},{7,2},{8,13},{9,12},{10,... | collective-permute-start | bytes 1204232 | tf_op jit(solution)/shard_map/ppermute | solution.py:213
  93.9 19.5 %collective-permute-start.6 = (f32[49,16,128]{2,1,0:T(8,128)}, f32[49,16,128]{2,1,0:T(8,128)S(1)}, u32[]{:S(2)}, u32[]{:S(2)}) collective-permute-start(f32[49,16,128]{2,1,0:T(8,128)} %get-tuple-element.59), channel_id=1, source_target_pairs={{0,1},{1,0},{2,3},{3,2},{4,5},{5,4},{6,7},{7,6},{8,9},{9,8},{10,11... | collective-permute-start | bytes 1204232 | tf_op jit(solution)/shard_map/ppermute | solution.py:213
  127.0 22.0 %collective-permute-start.21 = (f32[49,16,128]{2,1,0:T(8,128)S(1)}, f32[49,16,128]{2,1,0:T(8,128)S(1)}, u32[]{:S(2)}, u32[]{:S(2)}) collective-permute-start(f32[49,16,128]{2,1,0:T(8,128)S(1)} %get-tuple-element.83), channel_id=1, source_target_pairs={{0,2},{1,3},{2,4},{3,5},{4,6},{5,7},{6,0},{7,1},{8,10},{9,11},{10,... | collective-permute-start | bytes 1204232 | tf_op jit(solution)/shard_map/ppermute | solution.py:213
  127.9 21.1 %collective-permute-start.22 = (f32[49,16,128]{2,1,0:T(8,128)S(1)}, f32[49,16,128]{2,1,0:T(8,128)S(1)}, u32[]{:S(2)}, u32[]{:S(2)}) collective-permute-start(f32[49,16,128]{2,1,0:T(8,128)S(1)} %get-tuple-element.84), channel_id=1, source_target_pairs={{0,6},{1,7},{2,0},{3,1},{4,2},{5,3},{6,4},{7,5},{8,14},{9,15},{10,... | collective-permute-start | bytes 1204232 | tf_op jit(solution)/shard_map/ppermute | solution.py:213
  130.3 25.7 %collective-permute-start.24 = (f32[49,16,128]{2,1,0:T(8,128)}, f32[49,16,128]{2,1,0:T(8,128)S(1)}, u32[]{:S(2)}, u32[]{:S(2)}) collective-permute-start(f32[49,16,128]{2,1,0:T(8,128)} %get-tuple-element.86), channel_id=1, source_target_pairs={{0,3},{1,2},{2,5},{3,4},{4,7},{5,6},{6,1},{7,0},{8,11},{9,10},{10,... | collective-permute-start | bytes 1204232 | tf_op jit(solution)/shard_map/ppermute | solution.py:213
  130.3 34.4 %collective-permute-start.25 = (f32[49,16,128]{2,1,0:T(8,128)}, f32[49,16,128]{2,1,0:T(8,128)S(1)}, u32[]{:S(2)}, u32[]{:S(2)}) collective-permute-start(f32[49,16,128]{2,1,0:T(8,128)} %get-tuple-element.87), channel_id=1, source_target_pairs={{0,7},{1,6},{2,1},{3,0},{4,3},{5,2},{6,5},{7,4},{8,15},{9,14},{10,... | collective-permute-start | bytes 1204232 | tf_op jit(solution)/shard_map/ppermute | solution.py:213
  (26 other events, 515.1 us)

commit v3 on v2

--- a/solution.py
+++ b/solution.py
@@ -203,6 +203,9 @@
 STEPS = ((0, 0), (1, 0), (3, 0), (2, 0), (1, 1), (3, 1), (2, 1), (0, 1))
 
 
+PAIRS = tuple((STEPS.index((d, 0)), STEPS.index((d, 1))) for d in range(4))
+
+
 def partner(me, d, flip):
     core = me % 2
     return ((me // 2 + d) % 4) * 2 + (core + flip - 2 * core * flip)
@@ -222,51 +225,58 @@
     return partner(me, (4 - d) % 4, flip)
 
 
-def pack_kernel(me_ref, in_ref, *out_refs):
+def pack_kernel(me_ref, block_ref, *out_refs):
     me = me_ref[0]
+    in_ref = block_ref.reshape(8 * 392, LANES)
     rows = [target(me, s) for s in range(8)]
 
     def step(n, carry):
         for s in range(8):
-            out_refs[s][n] = in_ref[pl.ds(n * 8 + rows[s], 8, stride=392), :]
+            out_refs[s][0, n] = in_ref[pl.ds(n * 8 + rows[s], 8, stride=392), :]
         return carry
 
     lax.fori_loop(0, 49, step, 0, unroll=7)
 
 
-def pack(me, flat, x):
+def pack(me, split, x):
     return pl.pallas_call(
         pack_kernel,
         grid=(2,),
         in_specs=[
             pl.BlockSpec(memory_space=pltpu.SMEM),
-            pl.BlockSpec((8 * 392, LANES), lambda h: (2 * x + h, 0)),
+            pl.BlockSpec((1, 4, 1, 2, 392, LANES), lambda p: (x, 0, p, 0, 0, 0)),
         ],
-        out_specs=[pl.BlockSpec((49, 8, LANES), lambda h: (0, h, 0)) for _ in range(8)],
-        out_shape=[pltpu.HBM((49, 16, LANES), F32) for _ in range(8)],
+        out_specs=[pl.BlockSpec((1, 49, 8, LANES), lambda p: (p, 0, 0, 0)) for _ in range(8)],
+        out_shape=[pltpu.HBM((2, 49, 8, LANES), F32) for _ in range(8)],
         compiler_params=params(FULL, 1),
         name="pack",
-    )(me, flat)
-
-
-def transform(me, block_of, w_ref, xb):
-    for s in range(8):
-        at = pl.multiple_of(origin(me, s) * 16, 16)
+    )(me, split)
+
+
+def transform(me, block_of, w_ref, xb, field, slope):
+    core = me % 2
+    for first, second in PAIRS:
+        at = pl.multiple_of((origin(me, first) // 2) * 16, 16)
         for b in range(7):
-            block = block_of(s, b)
-            hi = block.astype(BF16)
-            lo = (block - hi.astype(F32)).astype(BF16)
             lanes = pl.ds(b * 128, 128)
-            xb[pl.ds(at, 16), lanes] = hi
-            xb[pl.ds(at + 128, 16), lanes] = lo
-            xb[pl.ds(at + 256, 16), lanes] = hi
-    return jnp.dot(w_ref[...], xb[...], preferred_element_type=F32)
+            for p in range(2):
+                block = jnp.concatenate([block_of(first, p, b), block_of(second, p, b)], axis=0)
+                hi = block.astype(BF16)
+                xb[pl.ds(at + 192 * p, 16), lanes] = hi
+                xb[pl.ds(at + 192 * p + 64, 16), lanes] = (block - hi.astype(F32)).astype(BF16)
+                xb[pl.ds(at + 192 * p + 128, 16), lanes] = hi
+    even = jnp.dot(w_ref[core, 0], xb[0:192], preferred_element_type=F32)
+    odd = jnp.dot(w_ref[core, 1], xb[192:384], preferred_element_type=F32)
+    field[0:64] = even[0:64] + odd[0:64]
+    field[64:128] = even[0:64] - odd[0:64]
+    slope[0:64] = even[64:128] + odd[64:128]
+    slope[64:128] = even[64:128] - odd[64:128]
 
 
 def row_copies(sources, a, slots, sems):
     slot = a % 2
     return [
-        pltpu.make_async_copy(ref.at[pl.ds(7 * a, 7)], slots.at[slot, i], sems.at[slot, i])
+        pltpu.make_async_copy(ref.at[:, pl.ds(7 * a, 7)], slots.at[slot, i], sems.at[slot, i])
         for i, ref in enumerate(sources)
     ]
 
@@ -306,19 +316,22 @@
 
     def node_row(a):
         for x, (field, slope) in enumerate(((u, zu), (v, zv))):
-            both = transform(me, lambda s, b: slots[a % 2, 8 * x + s, b], w_ref, xb)
-            field[a] = both[0:128]
-            slope[a] = both[128:256]
+            transform(
+                me, lambda s, p, b: slots[a % 2, 8 * x + s, p, b], w_ref, xb, field.at[a], slope.at[a]
+            )
 
         def along_b(t, carry):
             q = q_rows(t)
             first = [u[a, q, s] for s in BLOCK]
             second = [v[a, q, s] for s in BLOCK]
             scaled = [item * sy for item in second]
-            for field, out in ((first, adv0), (second, adv1)):
+            for field, out, scale in ((first, adv0, sx), (second, adv1, sy)):
                 slope = derive(field)
                 for b in range(7):
-                    out[a, q, BLOCK[b]] = scaled[b] * slope[b]
+                    out[a, q, BLOCK[b]] = (scaled[b] * slope[b]) * scale
+            for s in BLOCK:
+                zu[a, q, s] = zu[a, q, s] * sx
+                zv[a, q, s] = zv[a, q, s] * sy
             return carry
 
         lax.fori_loop(0, 16, along_b, 0)
@@ -331,10 +344,13 @@
             first = [u[k, q, s] for k in range(7)]
             second = [v[k, q, s] for k in range(7)]
             scaled = [item * sx for item in first]
-            for field, out in ((first, adv0), (second, adv1)):
+            for field, out, scale in ((first, adv0, sx), (second, adv1, sy)):
                 slope = derive(field)
                 for k in range(7):
-                    out[k, q, s] = out[k, q, s] + scaled[k] * slope[k]
+                    out[k, q, s] = out[k, q, s] + (scaled[k] * slope[k]) * scale
+            for k in range(7):
+                u[k, q, s] = scaled[k]
+                v[k, q, s] = second[k] * sy
         return carry
 
     lax.fori_loop(0, 16, along_a, 0)
@@ -349,14 +365,14 @@
     me = me_ref[0]
     sx = met_ref[0]
     sy = met_ref[1]
-    for s in range(8):
-        at = pl.ds(pl.multiple_of(target(me, s) * 16, 16), 16)
-        forward[s * 16 : s * 16 + 16] = f_ref[at]
+    for d, (first, _) in enumerate(PAIRS):
+        at = pl.ds(pl.multiple_of((target(me, first) // 2) * 16, 16), 16)
+        for p in range(2):
+            forward[p, d * 16 : d * 16 + 16] = f_ref[me % 2, p, 0, at]
+            forward[p, 64 + d * 16 : 80 + d * 16] = f_ref[me % 2, p, 1, at]
 
     def node_row(a, carry):
-        both = transform(me, lambda s, b: sources[s][7 * a + b], w_ref, xb)
-        w[a] = both[0:128]
-        zw[...] = both[128:256]
+        transform(me, lambda s, p, b: sources[s][p, 7 * a + b], w_ref, xb, w.at[a], zw)
 
         def along_b(t, carry):
             q = q_rows(t)
@@ -367,13 +383,13 @@
             for b, s in enumerate(BLOCK):
                 sum0[a, q, s] = adv0[a, q, s] + third[b] * zu[a, q, s]
                 line.append(adv1[a, q, s] + third[b] * zv[a, q, s])
-                div[a, q2, s] = (v[a, q, s] * sy) * slope[b] + third[b] * zw[q, s]
+                div[a, q2, s] = v[a, q, s] * slope[b] + third[b] * zw[q, s]
             slope = derive(line)
             for b, s in enumerate(BLOCK):
-                div[a, q, s] = sy * slope[b]
+                div[a, q, s] = slope[b]
             return carry
 
-        lax.fori_loop(0, 16, along_b, 0)
+        lax.fori_loop(0, 16, along_b, 0, unroll=4)
         return carry
 
     lax.fori_loop(0, 7, node_row, 0)
@@ -384,25 +400,58 @@
         for s in BLOCK:
             slope = derive([w[k, q, s] for k in range(7)])
             for k in range(7):
-                div[k, q2, s] = div[k, q2, s] + (u[k, q, s] * sx) * slope[k]
+                div[k, q2, s] = div[k, q2, s] + u[k, q, s] * slope[k]
             slope = derive([sum0[k, q, s] for k in range(7)])
             for k in range(7):
-                div[k, q, s] = div[k, q, s] + sx * slope[k]
-        return carry
-
-    lax.fori_loop(0, 16, along_a, 0)
+                div[k, q, s] = div[k, q, s] + slope[k]
+        return carry
+
+    lax.fori_loop(0, 16, along_a, 0, unroll=2)
     area = -1.0 / (sx * sy)
     for k in range(7):
-        block = div[k]
-        hi = block.astype(BF16)
-        db[0:256] = hi
-        db[256:512] = (block - hi.astype(F32)).astype(BF16)
-        db[512:768] = hi
-        spec = jnp.dot(forward[...], db[...], preferred_element_type=F32)
-        for b in range(7):
-            scale = area * np.float32(WEIGHTS[k] * WEIGHTS[b])
-            for s in range(8):
-                outs[s][7 * k + b] = spec[s * 16 : s * 16 + 16, b * 128 : b * 128 + 128] * scale
+        for p in range(2):
+            for i in range(2):
+                one, two = div[k, 128 * i : 128 * i + 64], div[k, 128 * i + 64 : 128 * i + 128]
+                block = one + two if p == 0 else one - two
+                hi = block.astype(BF16)
+                db[k % 2, p, 64 * i : 64 * i + 64] = hi
+                db[k % 2, p, 128 + 64 * i : 192 + 64 * i] = (block - hi.astype(F32)).astype(BF16)
+        for p in range(2):
+            both = jnp.dot(forward[p], db[k % 2, p], preferred_element_type=F32)
+            spec = both[0:64] + both[64:128]
+            for b in range(7):
+                scale = area * np.float32(WEIGHTS[k] * WEIGHTS[b])
+                for d, pair in enumerate(PAIRS):
+                    for flip, s in enumerate(pair):
+                        low = 16 * d + 8 * flip
+                        value = spec[low : low + 8, b * 128 : b * 128 + 128] * scale
+                        outs[s][7 * k + b, 8 * p : 8 * p + 8] = value
+
+
+def parity_columns(core, parity):
+    return [
+        16 * (2 * y + (core + flip) % 2) + 4 * g + 2 * parity + r
+        for y in range(4)
+        for flip in range(2)
+        for g in range(4)
+        for r in range(2)
+    ]
+
+
+def wave_tables(basis, forward, modal_diff):
+    planes, modes = [], []
+    for core in range(2):
+        for parity in range(2):
+            c = parity_columns(core, parity)
+            hi, lo = split_bf16(np.concatenate([basis[:64, c], (basis @ modal_diff)[:64, c]]))
+            planes.append(np.concatenate([hi, hi, lo], axis=1))
+            back = np.concatenate([forward[c, :64], (modal_diff @ forward)[c, :64]], axis=1)
+            hi, lo = split_bf16(back)
+            modes.append(np.stack([np.concatenate([hi, hi], 1), np.concatenate([lo, 0 * lo], 1)]))
+    return (
+        jnp.asarray(np.stack(planes).reshape(2, 2, 128, 192)),
+        jnp.asarray(np.stack(modes).reshape(2, 2, 2, 64, 256)),
+    )
 
 
 def split_bf16(table):
@@ -606,10 +655,12 @@
     coef_ref[1] = jnp.broadcast_to(lam, (16, LANES))
 
     def copies(c):
+        mode = 4 * ((c // 2) % 4) + 2 * (c // 8) + c % 2
         at = pl.ds(pl.multiple_of(c * 392, 8), 392)
+        to = pl.ds(pl.multiple_of(mode * 392, 8), 392)
         return (
-            pltpu.make_async_copy(pres_buf.at[at, :], pres_ref.at[at, :], sems.at[0, c]),
-            pltpu.make_async_copy(resid_buf.at[at, :], resid_ref.at[at, :], sems.at[1, c]),
+            pltpu.make_async_copy(pres_buf.at[at, :], pres_ref.at[to, :], sems.at[0, c]),
+            pltpu.make_async_copy(resid_buf.at[at, :], resid_ref.at[to, :], sems.at[1, c]),
         )
 
     def step(c, carry):
@@ -669,17 +720,17 @@
     basis, forward, modal_diff, wave_all = mode_tables(modes_here * lax.axis_size("fourier"))
     mine = lax.axis_index("fourier")
     me = mine.astype(jnp.int32).reshape(1)
+    wave_all = wave_all.reshape(-1, 4, 2, 2).transpose(0, 2, 1, 3).reshape(-1)
     wave = lax.dynamic_slice_in_dim(jnp.asarray(wave_all, F32), mine * modes_here, modes_here)
     met_row = lax.dynamic_slice_in_dim(metric, mine, 1, 1)
-    hi, lo = split_bf16(np.concatenate([basis, basis @ modal_diff], axis=0))
-    to_planes = jnp.asarray(np.concatenate([hi, hi, lo], axis=1))
-    hi, lo = split_bf16(np.concatenate([forward, modal_diff @ forward], axis=1))
-    to_modes = jnp.asarray(np.concatenate([hi, hi, lo], axis=1))
-
-    flat = pltpu.with_memory_space_constraint(velocity.reshape(3 * 16 * 392, LANES), pltpu.HBM)
+    to_planes, to_modes = wave_tables(basis, forward, modal_diff)
+
+    split = pltpu.with_memory_space_constraint(
+        velocity.reshape(3, 4, 2, 2, 392, LANES), pltpu.HBM
+    )
     gathered = []
     for x in range(3):
-        packed = pack(me, flat, x)
+        packed = pack(me, split, x)
         blocks = [packed[0]] + [permute(packed[s], s) for s in range(1, 8)]
         if x < 2:
             blocks = [pltpu.with_memory_space_constraint(item, pltpu.HBM) for item in blocks]
@@ -694,7 +745,7 @@
         8,
         [
             pltpu.VMEM((384, 896), BF16),
-            pltpu.VMEM((2, 16, 7, 16, LANES), F32),
+            pltpu.VMEM((2, 16, 2, 7, 8, LANES), F32),
             pltpu.SemaphoreType.DMA((2, 16)),
         ],
         smem=(0,),
@@ -713,8 +764,8 @@
             pltpu.VMEM((128, 896), F32),
             pltpu.VMEM(plane_field, F32),
             pltpu.VMEM((7, 256, 896), F32),
-            pltpu.VMEM((128, 768), BF16),
-            pltpu.VMEM((768, 896), BF16),
+            pltpu.VMEM((2, 128, 256), BF16),
+            pltpu.VMEM((2, 2, 256, 896), BF16),
         ],
         smem=(0,),
         cost=40 * MIB,

time: 214 us -> 212 us (level)
  Pallas kernels: 56.1 us -> 53.3 us
    pallas_call x8, Pallas kernels: 45 us -> 42.4 us  [call(): pl.pallas_call(kernel, in_specs=specs, out_specs=out_specs, out_shape=[ja...]
  transfers between devices with their start and end apart: 32 -> 32, of which waited for: 20 -> 19; matrix products, arithmetic and copies ran while one was open for 0% -> 0% of each run, Pallas kernels for 13% -> 13%
where the time goes in v3:
time: 212 us; the launch traced here: 211 us
  waiting for transfers between devices  97.7 us (46%)
  Pallas kernels  53.3 us (25%)
  starting transfers between devices  41.6 us (20%)
  blocking collectives  17.1 us (8%)
    ppermute x28, waiting for transfers between devices, permute(): lax.ppermute(value, 'fourier', [(i, partner(i, d, flip)) for i in range(8)])  95.9 us
    pallas_call x8, Pallas kernels, call(): pl.pallas_call(kernel, in_specs=specs, out_specs=out_specs, out_shape=[ja...  42.4 us
    ppermute x28, starting transfers between devices, permute(): lax.ppermute(value, 'fourier', [(i, partner(i, d, flip)) for i in range(8)])  31.4 us
    all_to_all x1, blocking collectives, body(): dots = lax.all_to_all(dots, 'plane', 0, 0, tiled=True)  17.1 us
    pallas_call x3, Pallas kernels, pack(): pl.pallas_call(pack_kernel, grid=(2,), in_specs=[pl.BlockSpec(memory_spac...  10.9 us
    ppermute x4, starting transfers between devices, exchange(): return (lax.ppermute(east, 'plane', up), lax.ppermute(west, 'plane', down))  10.3 us
  transfers between devices with their start and end apart: 32, of which 19 were waited for; matrix products, arithmetic and copies ran while one was open for 0% of the time, Pallas kernels for 13%

profile of v3, /device:TPU:0, one launch (start us, length us, event | category | flops | bytes accessed | tf_op | source)
XLA Modules:
  0.0 211.0 jit_solution(10687848960815836934)
XLA Ops:
  0.6 3.6 %pack.4 = (f32[2,49,8,128]{3,2,1,0:T(8,128)}, f32[2,49,8,128]{3,2,1,0:T(8,128)}, f32[2,49,8,128]{3,2,1,0:T(8,128)}, f32[2,49,8,128]{3,2,1,0:T(8,128)}, f32[2,49,...) custom-call(s32[1]{0:T(128)} %bitcast.me_ref.refs_0_, ...), custom_call_target="tpu_custom_call" | custom-call | tf_op jit(solution)/shard_map/pack/pallas_call | solution.py:242
  9.3 3.6 %pack.5 = (f32[2,49,8,128]{3,2,1,0:T(8,128)}, f32[2,49,8,128]{3,2,1,0:T(8,128)}, f32[2,49,8,128]{3,2,1,0:T(8,128)}, f32[2,49,8,128]{3,2,1,0:T(8,128)}, f32[2,49,...) custom-call(s32[1]{0:T(128)} %bitcast.me_ref.refs_0_, ...), custom_call_target="tpu_custom_call" | custom-call | tf_op jit(solution)/shard_map/pack/pallas_call | solution.py:242
  19.1 6.1 %collective-permute-done.11.refs_6_ = f32[2,49,8,128]{3,2,1,0:T(8,128)S(1)} collective-permute-done((f32[2,49,8,128]{3,2,1,0:T(8,128)}, f32[2,49,8,128]{3,2,1,0:T(8,128)S(1)}, u32[]{:S(2)}, u32[]{:S(2)}) %collective-permute-start.11) | collective-permute-done | bytes 401440 | tf_op jit(solution)/shard_map/ppermute | solution.py:216
  30.2 5.0 %collective-permute-done.14.refs_10_ = f32[2,49,8,128]{3,2,1,0:T(8,128)S(1)} collective-permute-done((f32[2,49,8,128]{3,2,1,0:T(8,128)}, f32[2,49,8,128]{3,2,1,0:T(8,128)S(1)}, u32[]{:S(2)}, u32[]{:S(2)}) %collective-permute-start.14) | collective-permute-done | bytes 401440 | tf_op jit(solution)/shard_map/ppermute | solution.py:216
  36.2 6.1 %collective-permute-done.15.refs_11_ = f32[2,49,8,128]{3,2,1,0:T(8,128)S(1)} collective-permute-done((f32[2,49,8,128]{3,2,1,0:T(8,128)}, f32[2,49,8,128]{3,2,1,0:T(8,128)S(1)}, u32[]{:S(2)}, u32[]{:S(2)}) %collective-permute-start.15) | collective-permute-done | bytes 401440 | tf_op jit(solution)/shard_map/ppermute | solution.py:216
  42.5 3.7 %pack.3 = (f32[2,49,8,128]{3,2,1,0:T(8,128)}, f32[2,49,8,128]{3,2,1,0:T(8,128)}, f32[2,49,8,128]{3,2,1,0:T(8,128)}, f32[2,49,8,128]{3,2,1,0:T(8,128)}, f32[2,49,...) custom-call(s32[1]{0:T(128)} %bitcast.me_ref.refs_0_, ...), custom_call_target="tpu_custom_call" | custom-call | tf_op jit(solution)/shard_map/pack/pallas_call | solution.py:242
  53.6 5.9 %collective-permute-done.18.refs_14_ = f32[2,49,8,128]{3,2,1,0:T(8,128)S(1)} collective-permute-done((f32[2,49,8,128]{3,2,1,0:T(8,128)}, f32[2,49,8,128]{3,2,1,0:T(8,128)S(1)}, u32[]{:S(2)}, u32[]{:S(2)}) %collective-permute-start.18) | collective-permute-done | bytes 401440 | tf_op jit(solution)/shard_map/ppermute | solution.py:216
  65.0 4.3 %collective-permute-done.7.refs_2_ = f32[2,49,8,128]{3,2,1,0:T(8,128)S(1)} collective-permute-done((f32[2,49,8,128]{3,2,1,0:T(8,128)}, f32[2,49,8,128]{3,2,1,0:T(8,128)S(1)}, u32[]{:S(2)}, u32[]{:S(2)}) %collective-permute-start.7) | collective-permute-done | bytes 401440 | tf_op jit(solution)/shard_map/ppermute | solution.py:216
  70.9 5.7 %collective-permute-done.8.refs_3_ = f32[2,49,8,128]{3,2,1,0:T(8,128)S(1)} collective-permute-done((f32[2,49,8,128]{3,2,1,0:T(8,128)}, f32[2,49,8,128]{3,2,1,0:T(8,128)S(1)}, u32[]{:S(2)}, u32[]{:S(2)}) %collective-permute-start.8) | collective-permute-done | bytes 401440 | tf_op jit(solution)/shard_map/ppermute | solution.py:216
  80.4 6.0 %collective-permute-done.refs_2_ = f32[2,49,8,128]{3,2,1,0:T(8,128)S(1)} collective-permute-done((f32[2,49,8,128]{3,2,1,0:T(8,128)}, f32[2,49,8,128]{3,2,1,0:T(8,128)S(1)}, u32[]{:S(2)}, u32[]{:S(2)}) %collective-permute-start) | collective-permute-done | bytes 401440 | tf_op jit(solution)/shard_map/ppermute | solution.py:216
  87.8 6.0 %collective-permute-done.1.refs_3_ = f32[2,49,8,128]{3,2,1,0:T(8,128)S(1)} collective-permute-done((f32[2,49,8,128]{3,2,1,0:T(8,128)}, f32[2,49,8,128]{3,2,1,0:T(8,128)S(1)}, u32[]{:S(2)}, u32[]{:S(2)}) %collective-permute-start.1) | collective-permute-done | bytes 401440 | tf_op jit(solution)/shard_map/ppermute | solution.py:216
  93.9 12.1 %early.1 = (f32[7,128,896]{2,1,0:T(8,128)S(1)}, f32[7,128,896]{2,1,0:T(8,128)S(1)}, f32[7,128,896]{2,1,0:T(8,128)S(1)}, f32[7,128,896]{2,1,0:T(8,128)S(1)}, f32[...) custom-call(s32[1]{0:T(128)} %bitcast.me_ref.refs_0_, f32[2,49,8,128]{3,2,1,0:T(8,128)} %get-tuple-element.60.refs_1_, ...), custom_call_target="tpu_custom_call" | custom-call | bytes 41943040 | tf_op jit(solution)/shard_map/early/pallas_call | solution.py:706
  106.0 7.4 %collective-permute-done.5.refs_7_ = f32[2,49,8,128]{3,2,1,0:T(8,128)S(1)} collective-permute-done((f32[2,49,8,128]{3,2,1,0:T(8,128)}, f32[2,49,8,128]{3,2,1,0:T(8,128)S(1)}, u32[]{:S(2)}, u32[]{:S(2)}) %collective-permute-start.5) | collective-permute-done | bytes 401440 | tf_op jit(solution)/shard_map/ppermute | solution.py:216
  113.4 11.4 %late.1 = (f32[49,16,128]{2,1,0:T(8,128)S(1)}, f32[49,16,128]{2,1,0:T(8,128)S(1)}, f32[49,16,128]{2,1,0:T(8,128)S(1)}, f32[49,16,128]{2,1,0:T(8,128)}, f32[49,16...) custom-call(s32[1]{0:T(128)} %bitcast.me_ref.refs_0_, ...), custom_call_target="tpu_custom_call" | custom-call | bytes 41943040 | tf_op jit(solution)/shard_map/late/pallas_call | solution.py:706
  131.0 15.7 %collective-permute-done.21.refs_1_ = f32[49,16,128]{2,1,0:T(8,128)S(1)} collective-permute-done((f32[49,16,128]{2,1,0:T(8,128)S(1)}, f32[49,16,128]{2,1,0:T(8,128)S(1)}, u32[]{:S(2)}, u32[]{:S(2)}) %collective-permute-start.21) | collective-permute-done | bytes 401440 | tf_op jit(solution)/shard_map/ppermute | solution.py:216
  146.9 7.0 %collective-permute-done.24.refs_4_ = f32[49,16,128]{2,1,0:T(8,128)S(1)} collective-permute-done((f32[49,16,128]{2,1,0:T(8,128)}, f32[49,16,128]{2,1,0:T(8,128)S(1)}, u32[]{:S(2)}, u32[]{:S(2)}) %collective-permute-start.24) | collective-permute-done | bytes 401440 | tf_op jit(solution)/shard_map/ppermute | solution.py:216
  153.8 8.7 %collective-permute-done.25.refs_5_ = f32[49,16,128]{2,1,0:T(8,128)S(1)} collective-permute-done((f32[49,16,128]{2,1,0:T(8,128)}, f32[49,16,128]{2,1,0:T(8,128)S(1)}, u32[]{:S(2)}, u32[]{:S(2)}) %collective-permute-start.25) | collective-permute-done | bytes 401440 | tf_op jit(solution)/shard_map/ppermute | solution.py:216
  162.6 3.8 %first.1 = (f32[6272,128]{1,0:T(8,128)S(1)}, f32[6272,128]{1,0:T(8,128)S(1)}, f32[128,128]{1,0:T(8,128)S(1)}, f32[128,128]{1,0:T(8,128)S(1)}) custom-call(s32[1]{0:T(128)} %bitcast.me_ref.refs_0_, f32[16]{0:T(128)S(1)} %dynamic_slice.6.wave_ref, f32[49,16,128]{2,1,0:T(8,128)S(1)} %get-tuple-element.82.refs_0_, ...), custom_call_target="tpu_custom_call" | custom-call | tf_op jit(solution)/shard_map/first/pallas_call | solution.py:706
  166.4 3.9 %collective-permute-start.28 = (f32[128,128]{1,0:T(8,128)S(1)}, f32[128,128]{1,0:T(8,128)S(1)}, u32[]{:S(2)}, u32[]{:S(2)}) collective-permute-start(f32[128,128]{1,0:T(8,128)S(1)} %get-tuple-element.92), channel_id=1, source_target_pairs={{0,8},{8,16},{16,24},{24,32},{32,40},{40,48},{48,56},{56,64},{64,7... | collective-permute-start | bytes 196616 | tf_op jit(solution)/shard_map/ppermute | solution.py:780
  171.7 3.4 %local_image.1.local_ref = f32[6272,128]{1,0:T(8,128)S(1)} custom-call(f32[16]{0:T(128)S(1)} %dynamic_slice.6.wave_ref, f32[6272,128]{1,0:T(8,128)S(1)} %get-tuple-element.91.p_ref, f32[2,8,128]{2,1,0:T(8,128)S(1)} %copy-done.3), custom_call_target="tpu_custom_call" | custom-call | bytes 8388608 | tf_op jit(solution)/shard_map/local_image/pallas_call | solution.py:706
  176.5 3.4 %second.1 = (f32[6272,128]{1,0:T(8,128)S(1)}, f32[6272,128]{1,0:T(8,128)S(1)}, f32[128,128]{1,0:T(8,128)S(1)}, f32[128,128]{1,0:T(8,128)S(1)}) custom-call(f32[16]{0:T(128)S(1)} %dynamic_slice.6.wave_ref, f32[6272,128]{1,0:T(8,128)S(1)} %local_image.1.local_ref, f32[2,8,128]{2,1,0:T(8,128)S(1)} %copy-done.3, f32[128,128]{1,0:T(8,128)S(1)} %collective-permute-done.28.west_in, ...), custom_call_target="tpu_custom_call" | custom-call | tf_op jit(solution)/shard_map/second/pallas_call | solution.py:706
  180.0 3.8 %collective-permute-start.30 = (f32[128,128]{1,0:T(8,128)S(1)}, f32[128,128]{1,0:T(8,128)S(1)}, u32[]{:S(2)}, u32[]{:S(2)}) collective-permute-start(f32[128,128]{1,0:T(8,128)S(1)} %get-tuple-element.98), channel_id=1, source_target_pairs={{0,8},{8,16},{16,24},{24,32},{32,40},{40,48},{48,56},{56,64},{64,7... | collective-permute-start | bytes 196616 | tf_op jit(solution)/shard_map/ppermute | solution.py:780
  185.0 4.5 %third.1 = (f32[6272,128]{1,0:T(8,128)S(1)}, f32[5,16,128]{2,1,0:T(8,128)S(1)}) custom-call(f32[16]{0:T(128)S(1)} %dynamic_slice.6.wave_ref, f32[6272,128]{1,0:T(8,128)S(1)} %get-tuple-element.90.r_ref, f32[6272,128]{1,0:T(8,128)S(1)} %get-tuple-element.94.q_ref, f32[6272,128]{1,0:T(8,128)S(1)} %get-tuple-element.95.s_ref, f32[2,8,128]{2,1,0:T(8,128)S(1)} %copy-done.3), custom_call_target="tpu_custom_call" | custom-call | bytes 12582912 | tf_op jit(solution)/shard_map/third/pallas_call | solution.py:706
  190.6 17.1 %all_to_all.5.dots_ref = f32[16,16,128]{2,1,0:T(8,128)S(1)} all-to-all(f32[16,16,128]{2,1,0:T(8,128)S(1)} %products.1), channel_id=1, replica_groups=mesh['plane'=16,'fourier'=8] {'plane'}, dimensions={0} | all-to-all | bytes 262144 | tf_op jit(solution)/shard_map/all_to_all | solution.py:825
  (90 shorter events, 51.5 us)
Async XLA Ops:
  5.3 19.9 %collective-permute-start.11 = (f32[2,49,8,128]{3,2,1,0:T(8,128)}, f32[2,49,8,128]{3,2,1,0:T(8,128)S(1)}, u32[]{:S(2)}, u32[]{:S(2)}) collective-permute-start(f32[2,49,8,128]{3,2,1,0:T(8,128)} %get-tuple-element.65), channel_id=1, source_target_pairs={{0,7},{1,6},{2,1},{3,0},{4,3},{5,2},{6,5},{7,4},{8,15},{9,14},{10,... | collective-permute-start | bytes 1204232 | tf_op jit(solution)/shard_map/ppermute | solution.py:216
  7.2 20.1 %collective-permute-start.12 = (f32[2,49,8,128]{3,2,1,0:T(8,128)}, f32[2,49,8,128]{3,2,1,0:T(8,128)S(1)}, u32[]{:S(2)}, u32[]{:S(2)}) collective-permute-start(f32[2,49,8,128]{3,2,1,0:T(8,128)} %get-tuple-element.66), channel_id=1, source_target_pairs={{0,5},{1,4},{2,7},{3,6},{4,1},{5,0},{6,3},{7,2},{8,13},{9,12},{10,... | collective-permute-start | bytes 1204232 | tf_op jit(solution)/shard_map/ppermute | solution.py:216
  8.7 20.6 %collective-permute-start.13 = (f32[2,49,8,128]{3,2,1,0:T(8,128)}, f32[2,49,8,128]{3,2,1,0:T(8,128)S(1)}, u32[]{:S(2)}, u32[]{:S(2)}) collective-permute-start(f32[2,49,8,128]{3,2,1,0:T(8,128)} %get-tuple-element.67), channel_id=1, source_target_pairs={{0,1},{1,0},{2,3},{3,2},{4,5},{5,4},{6,7},{7,6},{8,9},{9,8},{10,11... | collective-permute-start | bytes 1204232 | tf_op jit(solution)/shard_map/ppermute | solution.py:216
  13.0 22.2 %collective-permute-start.14 = (f32[2,49,8,128]{3,2,1,0:T(8,128)}, f32[2,49,8,128]{3,2,1,0:T(8,128)S(1)}, u32[]{:S(2)}, u32[]{:S(2)}) collective-permute-start(f32[2,49,8,128]{3,2,1,0:T(8,128)} %get-tuple-element.69), channel_id=1, source_target_pairs={{0,2},{1,3},{2,4},{3,5},{4,6},{5,7},{6,0},{7,1},{8,10},{9,11},{10,... | collective-permute-start | bytes 1204232 | tf_op jit(solution)/shard_map/ppermute | solution.py:216
  16.9 25.5 %collective-permute-start.15 = (f32[2,49,8,128]{3,2,1,0:T(8,128)}, f32[2,49,8,128]{3,2,1,0:T(8,128)S(1)}, u32[]{:S(2)}, u32[]{:S(2)}) collective-permute-start(f32[2,49,8,128]{3,2,1,0:T(8,128)} %get-tuple-element.70), channel_id=1, source_target_pairs={{0,6},{1,7},{2,0},{3,1},{4,2},{5,3},{6,4},{7,5},{8,14},{9,15},{10,... | collective-permute-start | bytes 1204232 | tf_op jit(solution)/shard_map/ppermute | solution.py:216
  25.2 21.0 %collective-permute-start.16 = (f32[2,49,8,128]{3,2,1,0:T(8,128)}, f32[2,49,8,128]{3,2,1,0:T(8,128)S(1)}, u32[]{:S(2)}, u32[]{:S(2)}) collective-permute-start(f32[2,49,8,128]{3,2,1,0:T(8,128)} %get-tuple-element.71), channel_id=1, source_target_pairs={{0,4},{1,5},{2,6},{3,7},{4,0},{5,1},{6,2},{7,3},{8,12},{9,13},{10,... | collective-permute-start | bytes 1204232 | tf_op jit(solution)/shard_map/ppermute | solution.py:216
  27.2 23.6 %collective-permute-start.17 = (f32[2,49,8,128]{3,2,1,0:T(8,128)}, f32[2,49,8,128]{3,2,1,0:T(8,128)S(1)}, u32[]{:S(2)}, u32[]{:S(2)}) collective-permute-start(f32[2,49,8,128]{3,2,1,0:T(8,128)} %get-tuple-element.72), channel_id=1, source_target_pairs={{0,3},{1,2},{2,5},{3,4},{4,7},{5,6},{6,1},{7,0},{8,11},{9,10},{10,... | collective-permute-start | bytes 1204232 | tf_op jit(solution)/shard_map/ppermute | solution.py:216
  29.3 30.2 %collective-permute-start.18 = (f32[2,49,8,128]{3,2,1,0:T(8,128)}, f32[2,49,8,128]{3,2,1,0:T(8,128)S(1)}, u32[]{:S(2)}, u32[]{:S(2)}) collective-permute-start(f32[2,49,8,128]{3,2,1,0:T(8,128)} %get-tuple-element.73), channel_id=1, source_target_pairs={{0,7},{1,6},{2,1},{3,0},{4,3},{5,2},{6,5},{7,4},{8,15},{9,14},{10,... | collective-permute-start | bytes 1204232 | tf_op jit(solution)/shard_map/ppermute | solution.py:216
  35.2 26.5 %collective-permute-start.19 = (f32[2,49,8,128]{3,2,1,0:T(8,128)}, f32[2,49,8,128]{3,2,1,0:T(8,128)S(1)}, u32[]{:S(2)}, u32[]{:S(2)}) collective-permute-start(f32[2,49,8,128]{3,2,1,0:T(8,128)} %get-tuple-element.74), channel_id=1, source_target_pairs={{0,5},{1,4},{2,7},{3,6},{4,1},{5,0},{6,3},{7,2},{8,13},{9,12},{10,... | collective-permute-start | bytes 1204232 | tf_op jit(solution)/shard_map/ppermute | solution.py:216
  42.4 22.3 %collective-permute-start.20 = (f32[2,49,8,128]{3,2,1,0:T(8,128)}, f32[2,49,8,128]{3,2,1,0:T(8,128)}, u32[]{:S(2)}, u32[]{:S(2)}) collective-permute-start(f32[2,49,8,128]{3,2,1,0:T(8,128)} %get-tuple-element.75), channel_id=1, source_target_pairs={{0,1},{1,0},{2,3},{3,2},{4,5},{5,4},{6,7},{7,6},{8,9},{9,8},{10,11... | collective-permute-start | bytes 1204232 | tf_op jit(solution)/shard_map/ppermute | solution.py:216
  46.2 23.1 %collective-permute-start.7 = (f32[2,49,8,128]{3,2,1,0:T(8,128)}, f32[2,49,8,128]{3,2,1,0:T(8,128)S(1)}, u32[]{:S(2)}, u32[]{:S(2)}) collective-permute-start(f32[2,49,8,128]{3,2,1,0:T(8,128)} %get-tuple-element.61), channel_id=1, source_target_pairs={{0,2},{1,3},{2,4},{3,5},{4,6},{5,7},{6,0},{7,1},{8,10},{9,11},{10,... | collective-permute-start | bytes 1204232 | tf_op jit(solution)/shard_map/ppermute | solution.py:216
  50.9 25.8 %collective-permute-start.8 = (f32[2,49,8,128]{3,2,1,0:T(8,128)}, f32[2,49,8,128]{3,2,1,0:T(8,128)S(1)}, u32[]{:S(2)}, u32[]{:S(2)}) collective-permute-start(f32[2,49,8,128]{3,2,1,0:T(8,128)} %get-tuple-element.62), channel_id=1, source_target_pairs={{0,6},{1,7},{2,0},{3,1},{4,2},{5,3},{6,4},{7,5},{8,14},{9,15},{10,... | collective-permute-start | bytes 1204232 | tf_op jit(solution)/shard_map/ppermute | solution.py:216
  59.5 19.5 %collective-permute-start.9 = (f32[2,49,8,128]{3,2,1,0:T(8,128)}, f32[2,49,8,128]{3,2,1,0:T(8,128)S(1)}, u32[]{:S(2)}, u32[]{:S(2)}) collective-permute-start(f32[2,49,8,128]{3,2,1,0:T(8,128)} %get-tuple-element.63), channel_id=1, source_target_pairs={{0,4},{1,5},{2,6},{3,7},{4,0},{5,1},{6,2},{7,3},{8,12},{9,13},{10,... | collective-permute-start | bytes 1204232 | tf_op jit(solution)/shard_map/ppermute | solution.py:216
  61.7 24.8 %collective-permute-start = (f32[2,49,8,128]{3,2,1,0:T(8,128)}, f32[2,49,8,128]{3,2,1,0:T(8,128)S(1)}, u32[]{:S(2)}, u32[]{:S(2)}) collective-permute-start(f32[2,49,8,128]{3,2,1,0:T(8,128)} %get-tuple-element.53), channel_id=1, source_target_pairs={{0,2},{1,3},{2,4},{3,5},{4,6},{5,7},{6,0},{7,1},{8,10},{9,11},{10,... | collective-permute-start | bytes 1204232 | tf_op jit(solution)/shard_map/ppermute | solution.py:216
  64.7 29.1 %collective-permute-start.1 = (f32[2,49,8,128]{3,2,1,0:T(8,128)}, f32[2,49,8,128]{3,2,1,0:T(8,128)S(1)}, u32[]{:S(2)}, u32[]{:S(2)}) collective-permute-start(f32[2,49,8,128]{3,2,1,0:T(8,128)} %get-tuple-element.54), channel_id=1, source_target_pairs={{0,6},{1,7},{2,0},{3,1},{4,2},{5,3},{6,4},{7,5},{8,14},{9,15},{10,... | collective-permute-start | bytes 1204232 | tf_op jit(solution)/shard_map/ppermute | solution.py:216
  69.3 36.7 %collective-permute-start.2 = (f32[2,49,8,128]{3,2,1,0:T(8,128)}, f32[2,49,8,128]{3,2,1,0:T(8,128)S(1)}, u32[]{:S(2)}, u32[]{:S(2)}) collective-permute-start(f32[2,49,8,128]{3,2,1,0:T(8,128)} %get-tuple-element.55), channel_id=1, source_target_pairs={{0,4},{1,5},{2,6},{3,7},{4,0},{5,1},{6,2},{7,3},{8,12},{9,13},{10,... | collective-permute-start | bytes 1204232 | tf_op jit(solution)/shard_map/ppermute | solution.py:216
  76.7 29.3 %collective-permute-start.3 = (f32[2,49,8,128]{3,2,1,0:T(8,128)}, f32[2,49,8,128]{3,2,1,0:T(8,128)S(1)}, u32[]{:S(2)}, u32[]{:S(2)}) collective-permute-start(f32[2,49,8,128]{3,2,1,0:T(8,128)} %get-tuple-element.56), channel_id=1, source_target_pairs={{0,3},{1,2},{2,5},{3,4},{4,7},{5,6},{6,1},{7,0},{8,11},{9,10},{10,... | collective-permute-start | bytes 1204232 | tf_op jit(solution)/shard_map/ppermute | solution.py:216
  79.0 27.0 %collective-permute-start.4 = (f32[2,49,8,128]{3,2,1,0:T(8,128)}, f32[2,49,8,128]{3,2,1,0:T(8,128)S(1)}, u32[]{:S(2)}, u32[]{:S(2)}) collective-permute-start(f32[2,49,8,128]{3,2,1,0:T(8,128)} %get-tuple-element.57), channel_id=1, source_target_pairs={{0,7},{1,6},{2,1},{3,0},{4,3},{5,2},{6,5},{7,4},{8,15},{9,14},{10,... | collective-permute-start | bytes 1204232 | tf_op jit(solution)/shard_map/ppermute | solution.py:216
  86.5 26.9 %collective-permute-start.5 = (f32[2,49,8,128]{3,2,1,0:T(8,128)}, f32[2,49,8,128]{3,2,1,0:T(8,128)S(1)}, u32[]{:S(2)}, u32[]{:S(2)}) collective-permute-start(f32[2,49,8,128]{3,2,1,0:T(8,128)} %get-tuple-element.58), channel_id=1, source_target_pairs={{0,5},{1,4},{2,7},{3,6},{4,1},{5,0},{6,3},{7,2},{8,13},{9,12},{10,... | collective-permute-start | bytes 1204232 | tf_op jit(solution)/shard_map/ppermute | solution.py:216
  93.8 19.5 %collective-permute-start.6 = (f32[2,49,8,128]{3,2,1,0:T(8,128)}, f32[2,49,8,128]{3,2,1,0:T(8,128)S(1)}, u32[]{:S(2)}, u32[]{:S(2)}) collective-permute-start(f32[2,49,8,128]{3,2,1,0:T(8,128)} %get-tuple-element.59), channel_id=1, source_target_pairs={{0,1},{1,0},{2,3},{3,2},{4,5},{5,4},{6,7},{7,6},{8,9},{9,8},{10,11... | collective-permute-start | bytes 1204232 | tf_op jit(solution)/shard_map/ppermute | solution.py:216
  124.8 21.9 %collective-permute-start.21 = (f32[49,16,128]{2,1,0:T(8,128)S(1)}, f32[49,16,128]{2,1,0:T(8,128)S(1)}, u32[]{:S(2)}, u32[]{:S(2)}) collective-permute-start(f32[49,16,128]{2,1,0:T(8,128)S(1)} %get-tuple-element.83), channel_id=1, source_target_pairs={{0,2},{1,3},{2,4},{3,5},{4,6},{5,7},{6,0},{7,1},{8,10},{9,11},{10,... | collective-permute-start | bytes 1204232 | tf_op jit(solution)/shard_map/ppermute | solution.py:216
  125.7 21.1 %collective-permute-start.22 = (f32[49,16,128]{2,1,0:T(8,128)S(1)}, f32[49,16,128]{2,1,0:T(8,128)S(1)}, u32[]{:S(2)}, u32[]{:S(2)}) collective-permute-start(f32[49,16,128]{2,1,0:T(8,128)S(1)} %get-tuple-element.84), channel_id=1, source_target_pairs={{0,6},{1,7},{2,0},{3,1},{4,2},{5,3},{6,4},{7,5},{8,14},{9,15},{10,... | collective-permute-start | bytes 1204232 | tf_op jit(solution)/shard_map/ppermute | solution.py:216
  128.1 25.8 %collective-permute-start.24 = (f32[49,16,128]{2,1,0:T(8,128)}, f32[49,16,128]{2,1,0:T(8,128)S(1)}, u32[]{:S(2)}, u32[]{:S(2)}) collective-permute-start(f32[49,16,128]{2,1,0:T(8,128)} %get-tuple-element.86), channel_id=1, source_target_pairs={{0,3},{1,2},{2,5},{3,4},{4,7},{5,6},{6,1},{7,0},{8,11},{9,10},{10,... | collective-permute-start | bytes 1204232 | tf_op jit(solution)/shard_map/ppermute | solution.py:216
  128.1 34.4 %collective-permute-start.25 = (f32[49,16,128]{2,1,0:T(8,128)}, f32[49,16,128]{2,1,0:T(8,128)S(1)}, u32[]{:S(2)}, u32[]{:S(2)}) collective-permute-start(f32[49,16,128]{2,1,0:T(8,128)} %get-tuple-element.87), channel_id=1, source_target_pairs={{0,7},{1,6},{2,1},{3,0},{4,3},{5,2},{6,5},{7,4},{8,15},{9,14},{10,... | collective-permute-start | bytes 1204232 | tf_op jit(solution)/shard_map/ppermute | solution.py:216
  (26 other events, 512.0 us)

commit v4 on v3

--- a/solution.py
+++ b/solution.py
@@ -200,7 +200,7 @@
     return pltpu.CompilerParams(vmem_limit_bytes=limit_mib * MIB, dimension_semantics=semantics)
 
 
-STEPS = ((0, 0), (1, 0), (3, 0), (2, 0), (1, 1), (3, 1), (2, 1), (0, 1))
+STEPS = ((0, 0), (2, 0), (1, 0), (3, 0), (2, 1), (1, 1), (3, 1), (0, 1))
 
 
 PAIRS = tuple((STEPS.index((d, 0)), STEPS.index((d, 1))) for d in range(4))

time: 212 us -> 212 us (level)
  starting transfers between devices: 41.6 us -> 47 us
  waiting for transfers between devices: 97.7 us -> 92.4 us
    ppermute x28, starting transfers between devices: 31.4 us -> 36.8 us  [permute(): lax.ppermute(value, 'fourier', [(i, partner(i, d, flip)) for i in range(8)])]
    ppermute x28, waiting for transfers between devices: 95.9 us -> 90.6 us  [permute(): lax.ppermute(value, 'fourier', [(i, partner(i, d, flip)) for i in range(8)])]
  transfers between devices with their start and end apart: 32 -> 32, of which waited for: 19 -> 20; matrix products, arithmetic and copies ran while one was open for 0% -> 0% of each run, Pallas kernels for 13% -> 13%
where the time goes in v4:
time: 212 us; the launch traced here: 211 us
  waiting for transfers between devices  92.4 us (44%)
  Pallas kernels  53.2 us (25%)
  starting transfers between devices  47 us (22%)
  blocking collectives  17.1 us (8%)
    ppermute x28, waiting for transfers between devices, permute(): lax.ppermute(value, 'fourier', [(i, partner(i, d, flip)) for i in range(8)])  90.6 us
    pallas_call x8, Pallas kernels, call(): pl.pallas_call(kernel, in_specs=specs, out_specs=out_specs, out_shape=[ja...  42.4 us
    ppermute x28, starting transfers between devices, permute(): lax.ppermute(value, 'fourier', [(i, partner(i, d, flip)) for i in range(8)])  36.8 us
    all_to_all x1, blocking collectives, body(): dots = lax.all_to_all(dots, 'plane', 0, 0, tiled=True)  17.1 us
    pallas_call x3, Pallas kernels, pack(): pl.pallas_call(pack_kernel, grid=(2,), in_specs=[pl.BlockSpec(memory_spac...  10.9 us
    ppermute x4, starting transfers between devices, exchange(): return (lax.ppermute(east, 'plane', up), lax.ppermute(west, 'plane', down))  10.2 us
  transfers between devices with their start and end apart: 32, of which 20 were waited for; matrix products, arithmetic and copies ran while one was open for 0% of the time, Pallas kernels for 13%

profile of v4, /device:TPU:0, one launch (start us, length us, event | category | flops | bytes accessed | tf_op | source)
XLA Modules:
  0.0 211.1 jit_solution(6679722450449173109)
XLA Ops:
  0.6 3.6 %pack.4 = (f32[2,49,8,128]{3,2,1,0:T(8,128)}, f32[2,49,8,128]{3,2,1,0:T(8,128)}, f32[2,49,8,128]{3,2,1,0:T(8,128)}, f32[2,49,8,128]{3,2,1,0:T(8,128)}, f32[2,49,...) custom-call(s32[1]{0:T(128)} %bitcast.me_ref.refs_0_, ...), custom_call_target="tpu_custom_call" | custom-call | tf_op jit(solution)/shard_map/pack/pallas_call | solution.py:242
  10.6 3.6 %pack.5 = (f32[2,49,8,128]{3,2,1,0:T(8,128)}, f32[2,49,8,128]{3,2,1,0:T(8,128)}, f32[2,49,8,128]{3,2,1,0:T(8,128)}, f32[2,49,8,128]{3,2,1,0:T(8,128)}, f32[2,49,...) custom-call(s32[1]{0:T(128)} %bitcast.me_ref.refs_0_, ...), custom_call_target="tpu_custom_call" | custom-call | tf_op jit(solution)/shard_map/pack/pallas_call | solution.py:242
  19.3 7.0 %collective-permute-done.11.refs_6_ = f32[2,49,8,128]{3,2,1,0:T(8,128)S(1)} collective-permute-done((f32[2,49,8,128]{3,2,1,0:T(8,128)}, f32[2,49,8,128]{3,2,1,0:T(8,128)S(1)}, u32[]{:S(2)}, u32[]{:S(2)}) %collective-permute-start.11) | collective-permute-done | bytes 401440 | tf_op jit(solution)/shard_map/ppermute | solution.py:216
  29.8 5.3 %collective-permute-done.14.refs_10_ = f32[2,49,8,128]{3,2,1,0:T(8,128)S(1)} collective-permute-done((f32[2,49,8,128]{3,2,1,0:T(8,128)}, f32[2,49,8,128]{3,2,1,0:T(8,128)S(1)}, u32[]{:S(2)}, u32[]{:S(2)}) %collective-permute-start.14) | collective-permute-done | bytes 401440 | tf_op jit(solution)/shard_map/ppermute | solution.py:216
  37.6 6.1 %collective-permute-done.15.refs_11_ = f32[2,49,8,128]{3,2,1,0:T(8,128)S(1)} collective-permute-done((f32[2,49,8,128]{3,2,1,0:T(8,128)}, f32[2,49,8,128]{3,2,1,0:T(8,128)S(1)}, u32[]{:S(2)}, u32[]{:S(2)}) %collective-permute-start.15) | collective-permute-done | bytes 401440 | tf_op jit(solution)/shard_map/ppermute | solution.py:216
  43.8 3.7 %pack.3 = (f32[2,49,8,128]{3,2,1,0:T(8,128)}, f32[2,49,8,128]{3,2,1,0:T(8,128)}, f32[2,49,8,128]{3,2,1,0:T(8,128)}, f32[2,49,8,128]{3,2,1,0:T(8,128)}, f32[2,49,...) custom-call(s32[1]{0:T(128)} %bitcast.me_ref.refs_0_, ...), custom_call_target="tpu_custom_call" | custom-call | tf_op jit(solution)/shard_map/pack/pallas_call | solution.py:242
  53.7 6.8 %collective-permute-done.18.refs_14_ = f32[2,49,8,128]{3,2,1,0:T(8,128)S(1)} collective-permute-done((f32[2,49,8,128]{3,2,1,0:T(8,128)}, f32[2,49,8,128]{3,2,1,0:T(8,128)S(1)}, u32[]{:S(2)}, u32[]{:S(2)}) %collective-permute-start.18) | collective-permute-done | bytes 401440 | tf_op jit(solution)/shard_map/ppermute | solution.py:216
  61.1 3.4 %collective-permute-start = (f32[2,49,8,128]{3,2,1,0:T(8,128)}, f32[2,49,8,128]{3,2,1,0:T(8,128)S(1)}, u32[]{:S(2)}, u32[]{:S(2)}) collective-permute-start(f32[2,49,8,128]{3,2,1,0:T(8,128)} %get-tuple-element.53), channel_id=1, source_target_pairs={{0,4},{1,5},{2,6},{3,7},{4,0},{5,1},{6,2},{7,3},{8,12},{9,13},{10,... | collective-permute-start | bytes 1204232 | tf_op jit(solution)/shard_map/ppermute | solution.py:216
  64.5 5.1 %collective-permute-done.7.refs_2_ = f32[2,49,8,128]{3,2,1,0:T(8,128)S(1)} collective-permute-done((f32[2,49,8,128]{3,2,1,0:T(8,128)}, f32[2,49,8,128]{3,2,1,0:T(8,128)S(1)}, u32[]{:S(2)}, u32[]{:S(2)}) %collective-permute-start.7) | collective-permute-done | bytes 401440 | tf_op jit(solution)/shard_map/ppermute | solution.py:216
  72.5 5.6 %collective-permute-done.8.refs_3_ = f32[2,49,8,128]{3,2,1,0:T(8,128)S(1)} collective-permute-done((f32[2,49,8,128]{3,2,1,0:T(8,128)}, f32[2,49,8,128]{3,2,1,0:T(8,128)S(1)}, u32[]{:S(2)}, u32[]{:S(2)}) %collective-permute-start.8) | collective-permute-done | bytes 401440 | tf_op jit(solution)/shard_map/ppermute | solution.py:216
  80.0 6.9 %collective-permute-done.refs_2_ = f32[2,49,8,128]{3,2,1,0:T(8,128)S(1)} collective-permute-done((f32[2,49,8,128]{3,2,1,0:T(8,128)}, f32[2,49,8,128]{3,2,1,0:T(8,128)S(1)}, u32[]{:S(2)}, u32[]{:S(2)}) %collective-permute-start) | collective-permute-done | bytes 401440 | tf_op jit(solution)/shard_map/ppermute | solution.py:216
  89.3 5.8 %collective-permute-done.1.refs_3_ = f32[2,49,8,128]{3,2,1,0:T(8,128)S(1)} collective-permute-done((f32[2,49,8,128]{3,2,1,0:T(8,128)}, f32[2,49,8,128]{3,2,1,0:T(8,128)S(1)}, u32[]{:S(2)}, u32[]{:S(2)}) %collective-permute-start.1) | collective-permute-done | bytes 401440 | tf_op jit(solution)/shard_map/ppermute | solution.py:216
  95.3 12.1 %early.1 = (f32[7,128,896]{2,1,0:T(8,128)S(1)}, f32[7,128,896]{2,1,0:T(8,128)S(1)}, f32[7,128,896]{2,1,0:T(8,128)S(1)}, f32[7,128,896]{2,1,0:T(8,128)S(1)}, f32[...) custom-call(s32[1]{0:T(128)} %bitcast.me_ref.refs_0_, f32[2,49,8,128]{3,2,1,0:T(8,128)} %get-tuple-element.60.refs_1_, ...), custom_call_target="tpu_custom_call" | custom-call | bytes 41943040 | tf_op jit(solution)/shard_map/early/pallas_call | solution.py:706
  107.3 4.7 %collective-permute-done.4.refs_6_ = f32[2,49,8,128]{3,2,1,0:T(8,128)S(1)} collective-permute-done((f32[2,49,8,128]{3,2,1,0:T(8,128)}, f32[2,49,8,128]{3,2,1,0:T(8,128)S(1)}, u32[]{:S(2)}, u32[]{:S(2)}) %collective-permute-start.4) | collective-permute-done | bytes 401440 | tf_op jit(solution)/shard_map/ppermute | solution.py:216
  112.8 11.4 %late.1 = (f32[49,16,128]{2,1,0:T(8,128)S(1)}, f32[49,16,128]{2,1,0:T(8,128)S(1)}, f32[49,16,128]{2,1,0:T(8,128)S(1)}, f32[49,16,128]{2,1,0:T(8,128)}, f32[49,16...) custom-call(s32[1]{0:T(128)} %bitcast.me_ref.refs_0_, ...), custom_call_target="tpu_custom_call" | custom-call | bytes 41943040 | tf_op jit(solution)/shard_map/late/pallas_call | solution.py:706
  130.9 7.0 %collective-permute-done.21.refs_1_ = f32[49,16,128]{2,1,0:T(8,128)S(1)} collective-permute-done((f32[49,16,128]{2,1,0:T(8,128)S(1)}, f32[49,16,128]{2,1,0:T(8,128)S(1)}, u32[]{:S(2)}, u32[]{:S(2)}) %collective-permute-start.21) | collective-permute-done | bytes 401440 | tf_op jit(solution)/shard_map/ppermute | solution.py:216
  138.5 8.1 %collective-permute-done.22.refs_2_ = f32[49,16,128]{2,1,0:T(8,128)S(1)} collective-permute-done((f32[49,16,128]{2,1,0:T(8,128)S(1)}, f32[49,16,128]{2,1,0:T(8,128)S(1)}, u32[]{:S(2)}, u32[]{:S(2)}) %collective-permute-start.22) | collective-permute-done | bytes 401440 | tf_op jit(solution)/shard_map/ppermute | solution.py:216
  146.7 6.9 %collective-permute-done.24.refs_4_ = f32[49,16,128]{2,1,0:T(8,128)S(1)} collective-permute-done((f32[49,16,128]{2,1,0:T(8,128)}, f32[49,16,128]{2,1,0:T(8,128)S(1)}, u32[]{:S(2)}, u32[]{:S(2)}) %collective-permute-start.24) | collective-permute-done | bytes 401440 | tf_op jit(solution)/shard_map/ppermute | solution.py:216
  153.6 9.2 %collective-permute-done.25.refs_5_ = f32[49,16,128]{2,1,0:T(8,128)S(1)} collective-permute-done((f32[49,16,128]{2,1,0:T(8,128)}, f32[49,16,128]{2,1,0:T(8,128)S(1)}, u32[]{:S(2)}, u32[]{:S(2)}) %collective-permute-start.25) | collective-permute-done | bytes 401440 | tf_op jit(solution)/shard_map/ppermute | solution.py:216
  162.8 3.8 %first.1 = (f32[6272,128]{1,0:T(8,128)S(1)}, f32[6272,128]{1,0:T(8,128)S(1)}, f32[128,128]{1,0:T(8,128)S(1)}, f32[128,128]{1,0:T(8,128)S(1)}) custom-call(s32[1]{0:T(128)} %bitcast.me_ref.refs_0_, f32[16]{0:T(128)S(1)} %dynamic_slice.6.wave_ref, f32[49,16,128]{2,1,0:T(8,128)S(1)} %get-tuple-element.82.refs_0_, ...), custom_call_target="tpu_custom_call" | custom-call | tf_op jit(solution)/shard_map/first/pallas_call | solution.py:706
  166.6 3.8 %collective-permute-start.28 = (f32[128,128]{1,0:T(8,128)S(1)}, f32[128,128]{1,0:T(8,128)S(1)}, u32[]{:S(2)}, u32[]{:S(2)}) collective-permute-start(f32[128,128]{1,0:T(8,128)S(1)} %get-tuple-element.92), channel_id=1, source_target_pairs={{0,8},{8,16},{16,24},{24,32},{32,40},{40,48},{48,56},{56,64},{64,7... | collective-permute-start | bytes 196616 | tf_op jit(solution)/shard_map/ppermute | solution.py:780
  180.0 3.8 %collective-permute-start.30 = (f32[128,128]{1,0:T(8,128)S(1)}, f32[128,128]{1,0:T(8,128)S(1)}, u32[]{:S(2)}, u32[]{:S(2)}) collective-permute-start(f32[128,128]{1,0:T(8,128)S(1)} %get-tuple-element.98), channel_id=1, source_target_pairs={{0,8},{8,16},{16,24},{24,32},{32,40},{40,48},{48,56},{56,64},{64,7... | collective-permute-start | bytes 196616 | tf_op jit(solution)/shard_map/ppermute | solution.py:780
  185.1 4.5 %third.1 = (f32[6272,128]{1,0:T(8,128)S(1)}, f32[5,16,128]{2,1,0:T(8,128)S(1)}) custom-call(f32[16]{0:T(128)S(1)} %dynamic_slice.6.wave_ref, f32[6272,128]{1,0:T(8,128)S(1)} %get-tuple-element.90.r_ref, f32[6272,128]{1,0:T(8,128)S(1)} %get-tuple-element.94.q_ref, f32[6272,128]{1,0:T(8,128)S(1)} %get-tuple-element.95.s_ref, f32[2,8,128]{2,1,0:T(8,128)S(1)} %copy-done.3), custom_call_target="tpu_custom_call" | custom-call | bytes 12582912 | tf_op jit(solution)/shard_map/third/pallas_call | solution.py:706
  190.7 17.1 %all_to_all.5.dots_ref = f32[16,16,128]{2,1,0:T(8,128)S(1)} all-to-all(f32[16,16,128]{2,1,0:T(8,128)S(1)} %products.1), channel_id=1, replica_groups=mesh['plane'=16,'fourier'=8] {'plane'}, dimensions={0} | all-to-all | bytes 262144 | tf_op jit(solution)/shard_map/all_to_all | solution.py:825
  (90 shorter events, 54.7 us)
Async XLA Ops:
  6.9 19.3 %collective-permute-start.11 = (f32[2,49,8,128]{3,2,1,0:T(8,128)}, f32[2,49,8,128]{3,2,1,0:T(8,128)S(1)}, u32[]{:S(2)}, u32[]{:S(2)}) collective-permute-start(f32[2,49,8,128]{3,2,1,0:T(8,128)} %get-tuple-element.65), channel_id=1, source_target_pairs={{0,3},{1,2},{2,5},{3,4},{4,7},{5,6},{6,1},{7,0},{8,11},{9,10},{10,... | collective-permute-start | bytes 1204232 | tf_op jit(solution)/shard_map/ppermute | solution.py:216
  7.9 18.7 %collective-permute-start.12 = (f32[2,49,8,128]{3,2,1,0:T(8,128)}, f32[2,49,8,128]{3,2,1,0:T(8,128)S(1)}, u32[]{:S(2)}, u32[]{:S(2)}) collective-permute-start(f32[2,49,8,128]{3,2,1,0:T(8,128)} %get-tuple-element.66), channel_id=1, source_target_pairs={{0,7},{1,6},{2,1},{3,0},{4,3},{5,2},{6,5},{7,4},{8,15},{9,14},{10,... | collective-permute-start | bytes 1204232 | tf_op jit(solution)/shard_map/ppermute | solution.py:216
  9.9 19.6 %collective-permute-start.13 = (f32[2,49,8,128]{3,2,1,0:T(8,128)}, f32[2,49,8,128]{3,2,1,0:T(8,128)S(1)}, u32[]{:S(2)}, u32[]{:S(2)}) collective-permute-start(f32[2,49,8,128]{3,2,1,0:T(8,128)} %get-tuple-element.67), channel_id=1, source_target_pairs={{0,1},{1,0},{2,3},{3,2},{4,5},{5,4},{6,7},{7,6},{8,9},{9,8},{10,11... | collective-permute-start | bytes 1204232 | tf_op jit(solution)/shard_map/ppermute | solution.py:216
  14.2 20.9 %collective-permute-start.14 = (f32[2,49,8,128]{3,2,1,0:T(8,128)}, f32[2,49,8,128]{3,2,1,0:T(8,128)S(1)}, u32[]{:S(2)}, u32[]{:S(2)}) collective-permute-start(f32[2,49,8,128]{3,2,1,0:T(8,128)} %get-tuple-element.69), channel_id=1, source_target_pairs={{0,4},{1,5},{2,6},{3,7},{4,0},{5,1},{6,2},{7,3},{8,12},{9,13},{10,... | collective-permute-start | bytes 1204232 | tf_op jit(solution)/shard_map/ppermute | solution.py:216
  17.3 26.4 %collective-permute-start.15 = (f32[2,49,8,128]{3,2,1,0:T(8,128)}, f32[2,49,8,128]{3,2,1,0:T(8,128)S(1)}, u32[]{:S(2)}, u32[]{:S(2)}) collective-permute-start(f32[2,49,8,128]{3,2,1,0:T(8,128)} %get-tuple-element.70), channel_id=1, source_target_pairs={{0,2},{1,3},{2,4},{3,5},{4,6},{5,7},{6,0},{7,1},{8,10},{9,11},{10,... | collective-permute-start | bytes 1204232 | tf_op jit(solution)/shard_map/ppermute | solution.py:216
  26.2 21.3 %collective-permute-start.16 = (f32[2,49,8,128]{3,2,1,0:T(8,128)}, f32[2,49,8,128]{3,2,1,0:T(8,128)S(1)}, u32[]{:S(2)}, u32[]{:S(2)}) collective-permute-start(f32[2,49,8,128]{3,2,1,0:T(8,128)} %get-tuple-element.71), channel_id=1, source_target_pairs={{0,6},{1,7},{2,0},{3,1},{4,2},{5,3},{6,4},{7,5},{8,14},{9,15},{10,... | collective-permute-start | bytes 1204232 | tf_op jit(solution)/shard_map/ppermute | solution.py:216
  26.6 25.2 %collective-permute-start.17 = (f32[2,49,8,128]{3,2,1,0:T(8,128)}, f32[2,49,8,128]{3,2,1,0:T(8,128)S(1)}, u32[]{:S(2)}, u32[]{:S(2)}) collective-permute-start(f32[2,49,8,128]{3,2,1,0:T(8,128)} %get-tuple-element.72), channel_id=1, source_target_pairs={{0,5},{1,4},{2,7},{3,6},{4,1},{5,0},{6,3},{7,2},{8,13},{9,12},{10,... | collective-permute-start | bytes 1204232 | tf_op jit(solution)/shard_map/ppermute | solution.py:216
  29.5 31.1 %collective-permute-start.18 = (f32[2,49,8,128]{3,2,1,0:T(8,128)}, f32[2,49,8,128]{3,2,1,0:T(8,128)S(1)}, u32[]{:S(2)}, u32[]{:S(2)}) collective-permute-start(f32[2,49,8,128]{3,2,1,0:T(8,128)} %get-tuple-element.73), channel_id=1, source_target_pairs={{0,3},{1,2},{2,5},{3,4},{4,7},{5,6},{6,1},{7,0},{8,11},{9,10},{10,... | collective-permute-start | bytes 1204232 | tf_op jit(solution)/shard_map/ppermute | solution.py:216
  35.1 25.9 %collective-permute-start.19 = (f32[2,49,8,128]{3,2,1,0:T(8,128)}, f32[2,49,8,128]{3,2,1,0:T(8,128)S(1)}, u32[]{:S(2)}, u32[]{:S(2)}) collective-permute-start(f32[2,49,8,128]{3,2,1,0:T(8,128)} %get-tuple-element.74), channel_id=1, source_target_pairs={{0,7},{1,6},{2,1},{3,0},{4,3},{5,2},{6,5},{7,4},{8,15},{9,14},{10,... | collective-permute-start | bytes 1204232 | tf_op jit(solution)/shard_map/ppermute | solution.py:216
  43.7 20.8 %collective-permute-start.20 = (f32[2,49,8,128]{3,2,1,0:T(8,128)}, f32[2,49,8,128]{3,2,1,0:T(8,128)}, u32[]{:S(2)}, u32[]{:S(2)}) collective-permute-start(f32[2,49,8,128]{3,2,1,0:T(8,128)} %get-tuple-element.75), channel_id=1, source_target_pairs={{0,1},{1,0},{2,3},{3,2},{4,5},{5,4},{6,7},{7,6},{8,9},{9,8},{10,11... | collective-permute-start | bytes 1204232 | tf_op jit(solution)/shard_map/ppermute | solution.py:216
  47.5 22.1 %collective-permute-start.7 = (f32[2,49,8,128]{3,2,1,0:T(8,128)}, f32[2,49,8,128]{3,2,1,0:T(8,128)S(1)}, u32[]{:S(2)}, u32[]{:S(2)}) collective-permute-start(f32[2,49,8,128]{3,2,1,0:T(8,128)} %get-tuple-element.61), channel_id=1, source_target_pairs={{0,4},{1,5},{2,6},{3,7},{4,0},{5,1},{6,2},{7,3},{8,12},{9,13},{10,... | collective-permute-start | bytes 1204232 | tf_op jit(solution)/shard_map/ppermute | solution.py:216
  51.8 26.2 %collective-permute-start.8 = (f32[2,49,8,128]{3,2,1,0:T(8,128)}, f32[2,49,8,128]{3,2,1,0:T(8,128)S(1)}, u32[]{:S(2)}, u32[]{:S(2)}) collective-permute-start(f32[2,49,8,128]{3,2,1,0:T(8,128)} %get-tuple-element.62), channel_id=1, source_target_pairs={{0,2},{1,3},{2,4},{3,5},{4,6},{5,7},{6,0},{7,1},{8,10},{9,11},{10,... | collective-permute-start | bytes 1204232 | tf_op jit(solution)/shard_map/ppermute | solution.py:216
  60.5 19.4 %collective-permute-start.9 = (f32[2,49,8,128]{3,2,1,0:T(8,128)}, f32[2,49,8,128]{3,2,1,0:T(8,128)S(1)}, u32[]{:S(2)}, u32[]{:S(2)}) collective-permute-start(f32[2,49,8,128]{3,2,1,0:T(8,128)} %get-tuple-element.63), channel_id=1, source_target_pairs={{0,6},{1,7},{2,0},{3,1},{4,2},{5,3},{6,4},{7,5},{8,14},{9,15},{10,... | collective-permute-start | bytes 1204232 | tf_op jit(solution)/shard_map/ppermute | solution.py:216
  61.1 25.8 %collective-permute-start = (f32[2,49,8,128]{3,2,1,0:T(8,128)}, f32[2,49,8,128]{3,2,1,0:T(8,128)S(1)}, u32[]{:S(2)}, u32[]{:S(2)}) collective-permute-start(f32[2,49,8,128]{3,2,1,0:T(8,128)} %get-tuple-element.53), channel_id=1, source_target_pairs={{0,4},{1,5},{2,6},{3,7},{4,0},{5,1},{6,2},{7,3},{8,12},{9,13},{10,... | collective-permute-start | bytes 1204232 | tf_op jit(solution)/shard_map/ppermute | solution.py:216
  64.5 30.7 %collective-permute-start.1 = (f32[2,49,8,128]{3,2,1,0:T(8,128)}, f32[2,49,8,128]{3,2,1,0:T(8,128)S(1)}, u32[]{:S(2)}, u32[]{:S(2)}) collective-permute-start(f32[2,49,8,128]{3,2,1,0:T(8,128)} %get-tuple-element.54), channel_id=1, source_target_pairs={{0,2},{1,3},{2,4},{3,5},{4,6},{5,7},{6,0},{7,1},{8,10},{9,11},{10,... | collective-permute-start | bytes 1204232 | tf_op jit(solution)/shard_map/ppermute | solution.py:216
  69.6 37.7 %collective-permute-start.2 = (f32[2,49,8,128]{3,2,1,0:T(8,128)}, f32[2,49,8,128]{3,2,1,0:T(8,128)S(1)}, u32[]{:S(2)}, u32[]{:S(2)}) collective-permute-start(f32[2,49,8,128]{3,2,1,0:T(8,128)} %get-tuple-element.55), channel_id=1, source_target_pairs={{0,6},{1,7},{2,0},{3,1},{4,2},{5,3},{6,4},{7,5},{8,14},{9,15},{10,... | collective-permute-start | bytes 1204232 | tf_op jit(solution)/shard_map/ppermute | solution.py:216
  78.0 29.3 %collective-permute-start.3 = (f32[2,49,8,128]{3,2,1,0:T(8,128)}, f32[2,49,8,128]{3,2,1,0:T(8,128)S(1)}, u32[]{:S(2)}, u32[]{:S(2)}) collective-permute-start(f32[2,49,8,128]{3,2,1,0:T(8,128)} %get-tuple-element.56), channel_id=1, source_target_pairs={{0,5},{1,4},{2,7},{3,6},{4,1},{5,0},{6,3},{7,2},{8,13},{9,12},{10,... | collective-permute-start | bytes 1204232 | tf_op jit(solution)/shard_map/ppermute | solution.py:216
  79.9 32.1 %collective-permute-start.4 = (f32[2,49,8,128]{3,2,1,0:T(8,128)}, f32[2,49,8,128]{3,2,1,0:T(8,128)S(1)}, u32[]{:S(2)}, u32[]{:S(2)}) collective-permute-start(f32[2,49,8,128]{3,2,1,0:T(8,128)} %get-tuple-element.57), channel_id=1, source_target_pairs={{0,3},{1,2},{2,5},{3,4},{4,7},{5,6},{6,1},{7,0},{8,11},{9,10},{10,... | collective-permute-start | bytes 1204232 | tf_op jit(solution)/shard_map/ppermute | solution.py:216
  86.9 25.9 %collective-permute-start.5 = (f32[2,49,8,128]{3,2,1,0:T(8,128)}, f32[2,49,8,128]{3,2,1,0:T(8,128)S(1)}, u32[]{:S(2)}, u32[]{:S(2)}) collective-permute-start(f32[2,49,8,128]{3,2,1,0:T(8,128)} %get-tuple-element.58), channel_id=1, source_target_pairs={{0,7},{1,6},{2,1},{3,0},{4,3},{5,2},{6,5},{7,4},{8,15},{9,14},{10,... | collective-permute-start | bytes 1204232 | tf_op jit(solution)/shard_map/ppermute | solution.py:216
  126.1 20.5 %collective-permute-start.22 = (f32[49,16,128]{2,1,0:T(8,128)S(1)}, f32[49,16,128]{2,1,0:T(8,128)S(1)}, u32[]{:S(2)}, u32[]{:S(2)}) collective-permute-start(f32[49,16,128]{2,1,0:T(8,128)S(1)} %get-tuple-element.84), channel_id=1, source_target_pairs={{0,2},{1,3},{2,4},{3,5},{4,6},{5,7},{6,0},{7,1},{8,10},{9,11},{10,... | collective-permute-start | bytes 1204232 | tf_op jit(solution)/shard_map/ppermute | solution.py:216
  127.6 19.0 %collective-permute-start.23 = (f32[49,16,128]{2,1,0:T(8,128)}, f32[49,16,128]{2,1,0:T(8,128)S(1)}, u32[]{:S(2)}, u32[]{:S(2)}) collective-permute-start(f32[49,16,128]{2,1,0:T(8,128)} %get-tuple-element.85), channel_id=1, source_target_pairs={{0,6},{1,7},{2,0},{3,1},{4,2},{5,3},{6,4},{7,5},{8,14},{9,15},{10,... | collective-permute-start | bytes 1204232 | tf_op jit(solution)/shard_map/ppermute | solution.py:216
  129.3 24.3 %collective-permute-start.24 = (f32[49,16,128]{2,1,0:T(8,128)}, f32[49,16,128]{2,1,0:T(8,128)S(1)}, u32[]{:S(2)}, u32[]{:S(2)}) collective-permute-start(f32[49,16,128]{2,1,0:T(8,128)} %get-tuple-element.86), channel_id=1, source_target_pairs={{0,5},{1,4},{2,7},{3,6},{4,1},{5,0},{6,3},{7,2},{8,13},{9,12},{10,... | collective-permute-start | bytes 1204232 | tf_op jit(solution)/shard_map/ppermute | solution.py:216
  129.3 33.5 %collective-permute-start.25 = (f32[49,16,128]{2,1,0:T(8,128)}, f32[49,16,128]{2,1,0:T(8,128)S(1)}, u32[]{:S(2)}, u32[]{:S(2)}) collective-permute-start(f32[49,16,128]{2,1,0:T(8,128)} %get-tuple-element.87), channel_id=1, source_target_pairs={{0,3},{1,2},{2,5},{3,4},{4,7},{5,6},{6,1},{7,0},{8,11},{9,10},{10,... | collective-permute-start | bytes 1204232 | tf_op jit(solution)/shard_map/ppermute | solution.py:216
  137.9 24.8 %collective-permute-start.26 = (f32[49,16,128]{2,1,0:T(8,128)}, f32[49,16,128]{2,1,0:T(8,128)S(1)}, u32[]{:S(2)}, u32[]{:S(2)}) collective-permute-start(f32[49,16,128]{2,1,0:T(8,128)} %get-tuple-element.88), channel_id=1, source_target_pairs={{0,7},{1,6},{2,1},{3,0},{4,3},{5,2},{6,5},{7,4},{8,15},{9,14},{10,... | collective-permute-start | bytes 1204232 | tf_op jit(solution)/shard_map/ppermute | solution.py:216
  (26 other events, 513.6 us)

commit v5 on v3

--- a/solution.py
+++ b/solution.py
@@ -541,7 +541,7 @@
         store_rims(field, c, east_ref, west_ref)
         return carry
 
-    lax.fori_loop(0, 16, step, 0)
+    lax.fori_loop(0, 16, step, 0, unroll=2)
 
 
 def rim_fix(value, kind, c, b, edge_ref):
@@ -560,7 +560,7 @@
             q_ref[rows_of(c, n), :] = out[n]
         return carry
 
-    lax.fori_loop(0, 16, image, 0)
+    lax.fori_loop(0, 16, image, 0, unroll=2)
 
 
 def second_kernel(
@@ -585,7 +585,7 @@
         store_rims(field, c, east_ref, west_ref)
         return carry
 
-    lax.fori_loop(0, 16, search, 0)
+    lax.fori_loop(0, 16, search, 0, unroll=2)
 
 
 def third_kernel(wave_ref, r_ref, q_ref, s_ref, met_ref, t_ref, acc_ref):
@@ -604,7 +604,7 @@
             acc_ref[k, pl.ds(c, 1), :] = jnp.sum(sums[k], axis=0, keepdims=True)
         return carry
 
-    lax.fori_loop(0, 16, image, 0)
+    lax.fori_loop(0, 16, image, 0, unroll=2)
 
 
 def product_kernel(r_ref, q_ref, t_ref, acc_ref, west_in, east_in, dots_ref, add_ref, table_ref, sem):

time: 212 us -> 211 us (level)
  no operation moved by 1% of the time
where the time goes in v5:
time: 211 us
  waiting for transfers between devices  97.8 us (46%)
  Pallas kernels  53 us (25%)
  starting transfers between devices  41.6 us (20%)
  blocking collectives  17.1 us (8%)
    ppermute x28, waiting for transfers between devices, permute(): lax.ppermute(value, 'fourier', [(i, partner(i, d, flip)) for i in range(8)])  95.9 us
    pallas_call x8, Pallas kernels, call(): pl.pallas_call(kernel, in_specs=specs, out_specs=out_specs, out_shape=[ja...  42.1 us
    ppermute x28, starting transfers between devices, permute(): lax.ppermute(value, 'fourier', [(i, partner(i, d, flip)) for i in range(8)])  31.4 us
    all_to_all x1, blocking collectives, body(): dots = lax.all_to_all(dots, 'plane', 0, 0, tiled=True)  17.1 us
    pallas_call x3, Pallas kernels, pack(): pl.pallas_call(pack_kernel, grid=(2,), in_specs=[pl.BlockSpec(memory_spac...  10.9 us
    ppermute x4, starting transfers between devices, exchange(): return (lax.ppermute(east, 'plane', up), lax.ppermute(west, 'plane', down))  10.3 us
  transfers between devices with their start and end apart: 32, of which 19 were waited for; matrix products, arithmetic and copies ran while one was open for 0% of the time, Pallas kernels for 13%

profile of v5, /device:TPU:0, one launch (start us, length us, event | category | flops | bytes accessed | tf_op | source)
XLA Modules:
  0.0 210.8 jit_solution(13044261348209685604)
XLA Ops:
  0.6 3.6 %pack.4 = (f32[2,49,8,128]{3,2,1,0:T(8,128)}, f32[2,49,8,128]{3,2,1,0:T(8,128)}, f32[2,49,8,128]{3,2,1,0:T(8,128)}, f32[2,49,8,128]{3,2,1,0:T(8,128)}, f32[2,49,...) custom-call(s32[1]{0:T(128)} %bitcast.me_ref.refs_0_, ...), custom_call_target="tpu_custom_call" | custom-call | tf_op jit(solution)/shard_map/pack/pallas_call | solution.py:242
  9.3 3.6 %pack.5 = (f32[2,49,8,128]{3,2,1,0:T(8,128)}, f32[2,49,8,128]{3,2,1,0:T(8,128)}, f32[2,49,8,128]{3,2,1,0:T(8,128)}, f32[2,49,8,128]{3,2,1,0:T(8,128)}, f32[2,49,...) custom-call(s32[1]{0:T(128)} %bitcast.me_ref.refs_0_, ...), custom_call_target="tpu_custom_call" | custom-call | tf_op jit(solution)/shard_map/pack/pallas_call | solution.py:242
  19.1 6.1 %collective-permute-done.11.refs_6_ = f32[2,49,8,128]{3,2,1,0:T(8,128)S(1)} collective-permute-done((f32[2,49,8,128]{3,2,1,0:T(8,128)}, f32[2,49,8,128]{3,2,1,0:T(8,128)S(1)}, u32[]{:S(2)}, u32[]{:S(2)}) %collective-permute-start.11) | collective-permute-done | bytes 401440 | tf_op jit(solution)/shard_map/ppermute | solution.py:216
  30.2 5.0 %collective-permute-done.14.refs_10_ = f32[2,49,8,128]{3,2,1,0:T(8,128)S(1)} collective-permute-done((f32[2,49,8,128]{3,2,1,0:T(8,128)}, f32[2,49,8,128]{3,2,1,0:T(8,128)S(1)}, u32[]{:S(2)}, u32[]{:S(2)}) %collective-permute-start.14) | collective-permute-done | bytes 401440 | tf_op jit(solution)/shard_map/ppermute | solution.py:216
  36.2 6.1 %collective-permute-done.15.refs_11_ = f32[2,49,8,128]{3,2,1,0:T(8,128)S(1)} collective-permute-done((f32[2,49,8,128]{3,2,1,0:T(8,128)}, f32[2,49,8,128]{3,2,1,0:T(8,128)S(1)}, u32[]{:S(2)}, u32[]{:S(2)}) %collective-permute-start.15) | collective-permute-done | bytes 401440 | tf_op jit(solution)/shard_map/ppermute | solution.py:216
  42.5 3.7 %pack.3 = (f32[2,49,8,128]{3,2,1,0:T(8,128)}, f32[2,49,8,128]{3,2,1,0:T(8,128)}, f32[2,49,8,128]{3,2,1,0:T(8,128)}, f32[2,49,8,128]{3,2,1,0:T(8,128)}, f32[2,49,...) custom-call(s32[1]{0:T(128)} %bitcast.me_ref.refs_0_, ...), custom_call_target="tpu_custom_call" | custom-call | tf_op jit(solution)/shard_map/pack/pallas_call | solution.py:242
  53.6 5.9 %collective-permute-done.18.refs_14_ = f32[2,49,8,128]{3,2,1,0:T(8,128)S(1)} collective-permute-done((f32[2,49,8,128]{3,2,1,0:T(8,128)}, f32[2,49,8,128]{3,2,1,0:T(8,128)S(1)}, u32[]{:S(2)}, u32[]{:S(2)}) %collective-permute-start.18) | collective-permute-done | bytes 401440 | tf_op jit(solution)/shard_map/ppermute | solution.py:216
  65.0 4.3 %collective-permute-done.7.refs_2_ = f32[2,49,8,128]{3,2,1,0:T(8,128)S(1)} collective-permute-done((f32[2,49,8,128]{3,2,1,0:T(8,128)}, f32[2,49,8,128]{3,2,1,0:T(8,128)S(1)}, u32[]{:S(2)}, u32[]{:S(2)}) %collective-permute-start.7) | collective-permute-done | bytes 401440 | tf_op jit(solution)/shard_map/ppermute | solution.py:216
  70.9 5.7 %collective-permute-done.8.refs_3_ = f32[2,49,8,128]{3,2,1,0:T(8,128)S(1)} collective-permute-done((f32[2,49,8,128]{3,2,1,0:T(8,128)}, f32[2,49,8,128]{3,2,1,0:T(8,128)S(1)}, u32[]{:S(2)}, u32[]{:S(2)}) %collective-permute-start.8) | collective-permute-done | bytes 401440 | tf_op jit(solution)/shard_map/ppermute | solution.py:216
  80.4 6.0 %collective-permute-done.refs_2_ = f32[2,49,8,128]{3,2,1,0:T(8,128)S(1)} collective-permute-done((f32[2,49,8,128]{3,2,1,0:T(8,128)}, f32[2,49,8,128]{3,2,1,0:T(8,128)S(1)}, u32[]{:S(2)}, u32[]{:S(2)}) %collective-permute-start) | collective-permute-done | bytes 401440 | tf_op jit(solution)/shard_map/ppermute | solution.py:216
  87.8 6.0 %collective-permute-done.1.refs_3_ = f32[2,49,8,128]{3,2,1,0:T(8,128)S(1)} collective-permute-done((f32[2,49,8,128]{3,2,1,0:T(8,128)}, f32[2,49,8,128]{3,2,1,0:T(8,128)S(1)}, u32[]{:S(2)}, u32[]{:S(2)}) %collective-permute-start.1) | collective-permute-done | bytes 401440 | tf_op jit(solution)/shard_map/ppermute | solution.py:216
  93.9 12.1 %early.1 = (f32[7,128,896]{2,1,0:T(8,128)S(1)}, f32[7,128,896]{2,1,0:T(8,128)S(1)}, f32[7,128,896]{2,1,0:T(8,128)S(1)}, f32[7,128,896]{2,1,0:T(8,128)S(1)}, f32[...) custom-call(s32[1]{0:T(128)} %bitcast.me_ref.refs_0_, f32[2,49,8,128]{3,2,1,0:T(8,128)} %get-tuple-element.60.refs_1_, ...), custom_call_target="tpu_custom_call" | custom-call | bytes 41943040 | tf_op jit(solution)/shard_map/early/pallas_call | solution.py:706
  106.0 7.4 %collective-permute-done.5.refs_7_ = f32[2,49,8,128]{3,2,1,0:T(8,128)S(1)} collective-permute-done((f32[2,49,8,128]{3,2,1,0:T(8,128)}, f32[2,49,8,128]{3,2,1,0:T(8,128)S(1)}, u32[]{:S(2)}, u32[]{:S(2)}) %collective-permute-start.5) | collective-permute-done | bytes 401440 | tf_op jit(solution)/shard_map/ppermute | solution.py:216
  113.4 11.4 %late.1 = (f32[49,16,128]{2,1,0:T(8,128)S(1)}, f32[49,16,128]{2,1,0:T(8,128)S(1)}, f32[49,16,128]{2,1,0:T(8,128)S(1)}, f32[49,16,128]{2,1,0:T(8,128)}, f32[49,16...) custom-call(s32[1]{0:T(128)} %bitcast.me_ref.refs_0_, ...), custom_call_target="tpu_custom_call" | custom-call | bytes 41943040 | tf_op jit(solution)/shard_map/late/pallas_call | solution.py:706
  131.0 15.7 %collective-permute-done.21.refs_1_ = f32[49,16,128]{2,1,0:T(8,128)S(1)} collective-permute-done((f32[49,16,128]{2,1,0:T(8,128)S(1)}, f32[49,16,128]{2,1,0:T(8,128)S(1)}, u32[]{:S(2)}, u32[]{:S(2)}) %collective-permute-start.21) | collective-permute-done | bytes 401440 | tf_op jit(solution)/shard_map/ppermute | solution.py:216
  146.9 7.0 %collective-permute-done.24.refs_4_ = f32[49,16,128]{2,1,0:T(8,128)S(1)} collective-permute-done((f32[49,16,128]{2,1,0:T(8,128)}, f32[49,16,128]{2,1,0:T(8,128)S(1)}, u32[]{:S(2)}, u32[]{:S(2)}) %collective-permute-start.24) | collective-permute-done | bytes 401440 | tf_op jit(solution)/shard_map/ppermute | solution.py:216
  153.8 8.7 %collective-permute-done.25.refs_5_ = f32[49,16,128]{2,1,0:T(8,128)S(1)} collective-permute-done((f32[49,16,128]{2,1,0:T(8,128)}, f32[49,16,128]{2,1,0:T(8,128)S(1)}, u32[]{:S(2)}, u32[]{:S(2)}) %collective-permute-start.25) | collective-permute-done | bytes 401440 | tf_op jit(solution)/shard_map/ppermute | solution.py:216
  162.6 3.8 %first.1 = (f32[6272,128]{1,0:T(8,128)S(1)}, f32[6272,128]{1,0:T(8,128)S(1)}, f32[128,128]{1,0:T(8,128)S(1)}, f32[128,128]{1,0:T(8,128)S(1)}) custom-call(s32[1]{0:T(128)} %bitcast.me_ref.refs_0_, f32[16]{0:T(128)S(1)} %dynamic_slice.6.wave_ref, f32[49,16,128]{2,1,0:T(8,128)S(1)} %get-tuple-element.82.refs_0_, ...), custom_call_target="tpu_custom_call" | custom-call | tf_op jit(solution)/shard_map/first/pallas_call | solution.py:706
  166.4 3.9 %collective-permute-start.28 = (f32[128,128]{1,0:T(8,128)S(1)}, f32[128,128]{1,0:T(8,128)S(1)}, u32[]{:S(2)}, u32[]{:S(2)}) collective-permute-start(f32[128,128]{1,0:T(8,128)S(1)} %get-tuple-element.92), channel_id=1, source_target_pairs={{0,8},{8,16},{16,24},{24,32},{32,40},{40,48},{48,56},{56,64},{64,7... | collective-permute-start | bytes 196616 | tf_op jit(solution)/shard_map/ppermute | solution.py:780
  171.6 3.4 %local_image.1.local_ref = f32[6272,128]{1,0:T(8,128)S(1)} custom-call(f32[16]{0:T(128)S(1)} %dynamic_slice.6.wave_ref, f32[6272,128]{1,0:T(8,128)S(1)} %get-tuple-element.91.p_ref, f32[2,8,128]{2,1,0:T(8,128)S(1)} %copy-done.3), custom_call_target="tpu_custom_call" | custom-call | bytes 8388608 | tf_op jit(solution)/shard_map/local_image/pallas_call | solution.py:706
  176.5 3.3 %second.1 = (f32[6272,128]{1,0:T(8,128)S(1)}, f32[6272,128]{1,0:T(8,128)S(1)}, f32[128,128]{1,0:T(8,128)S(1)}, f32[128,128]{1,0:T(8,128)S(1)}) custom-call(f32[16]{0:T(128)S(1)} %dynamic_slice.6.wave_ref, f32[6272,128]{1,0:T(8,128)S(1)} %local_image.1.local_ref, f32[2,8,128]{2,1,0:T(8,128)S(1)} %copy-done.3, f32[128,128]{1,0:T(8,128)S(1)} %collective-permute-done.28.west_in, ...), custom_call_target="tpu_custom_call" | custom-call | tf_op jit(solution)/shard_map/second/pallas_call | solution.py:706
  179.8 3.8 %collective-permute-start.30 = (f32[128,128]{1,0:T(8,128)S(1)}, f32[128,128]{1,0:T(8,128)S(1)}, u32[]{:S(2)}, u32[]{:S(2)}) collective-permute-start(f32[128,128]{1,0:T(8,128)S(1)} %get-tuple-element.98), channel_id=1, source_target_pairs={{0,8},{8,16},{16,24},{24,32},{32,40},{40,48},{48,56},{56,64},{64,7... | collective-permute-start | bytes 196616 | tf_op jit(solution)/shard_map/ppermute | solution.py:780
  184.9 4.4 %third.1 = (f32[6272,128]{1,0:T(8,128)S(1)}, f32[5,16,128]{2,1,0:T(8,128)S(1)}) custom-call(f32[16]{0:T(128)S(1)} %dynamic_slice.6.wave_ref, f32[6272,128]{1,0:T(8,128)S(1)} %get-tuple-element.90.r_ref, f32[6272,128]{1,0:T(8,128)S(1)} %get-tuple-element.94.q_ref, f32[6272,128]{1,0:T(8,128)S(1)} %get-tuple-element.95.s_ref, f32[2,8,128]{2,1,0:T(8,128)S(1)} %copy-done.3), custom_call_target="tpu_custom_call" | custom-call | bytes 12582912 | tf_op jit(solution)/shard_map/third/pallas_call | solution.py:706
  190.5 17.1 %all_to_all.5.dots_ref = f32[16,16,128]{2,1,0:T(8,128)S(1)} all-to-all(f32[16,16,128]{2,1,0:T(8,128)S(1)} %products.1), channel_id=1, replica_groups=mesh['plane'=16,'fourier'=8] {'plane'}, dimensions={0} | all-to-all | bytes 262144 | tf_op jit(solution)/shard_map/all_to_all | solution.py:825
  (90 shorter events, 51.7 us)
Async XLA Ops:
  5.3 19.9 %collective-permute-start.11 = (f32[2,49,8,128]{3,2,1,0:T(8,128)}, f32[2,49,8,128]{3,2,1,0:T(8,128)S(1)}, u32[]{:S(2)}, u32[]{:S(2)}) collective-permute-start(f32[2,49,8,128]{3,2,1,0:T(8,128)} %get-tuple-element.65), channel_id=1, source_target_pairs={{0,7},{1,6},{2,1},{3,0},{4,3},{5,2},{6,5},{7,4},{8,15},{9,14},{10,... | collective-permute-start | bytes 1204232 | tf_op jit(solution)/shard_map/ppermute | solution.py:216
  7.2 20.1 %collective-permute-start.12 = (f32[2,49,8,128]{3,2,1,0:T(8,128)}, f32[2,49,8,128]{3,2,1,0:T(8,128)S(1)}, u32[]{:S(2)}, u32[]{:S(2)}) collective-permute-start(f32[2,49,8,128]{3,2,1,0:T(8,128)} %get-tuple-element.66), channel_id=1, source_target_pairs={{0,5},{1,4},{2,7},{3,6},{4,1},{5,0},{6,3},{7,2},{8,13},{9,12},{10,... | collective-permute-start | bytes 1204232 | tf_op jit(solution)/shard_map/ppermute | solution.py:216
  8.7 20.6 %collective-permute-start.13 = (f32[2,49,8,128]{3,2,1,0:T(8,128)}, f32[2,49,8,128]{3,2,1,0:T(8,128)S(1)}, u32[]{:S(2)}, u32[]{:S(2)}) collective-permute-start(f32[2,49,8,128]{3,2,1,0:T(8,128)} %get-tuple-element.67), channel_id=1, source_target_pairs={{0,1},{1,0},{2,3},{3,2},{4,5},{5,4},{6,7},{7,6},{8,9},{9,8},{10,11... | collective-permute-start | bytes 1204232 | tf_op jit(solution)/shard_map/ppermute | solution.py:216
  13.0 22.2 %collective-permute-start.14 = (f32[2,49,8,128]{3,2,1,0:T(8,128)}, f32[2,49,8,128]{3,2,1,0:T(8,128)S(1)}, u32[]{:S(2)}, u32[]{:S(2)}) collective-permute-start(f32[2,49,8,128]{3,2,1,0:T(8,128)} %get-tuple-element.69), channel_id=1, source_target_pairs={{0,2},{1,3},{2,4},{3,5},{4,6},{5,7},{6,0},{7,1},{8,10},{9,11},{10,... | collective-permute-start | bytes 1204232 | tf_op jit(solution)/shard_map/ppermute | solution.py:216
  16.9 25.5 %collective-permute-start.15 = (f32[2,49,8,128]{3,2,1,0:T(8,128)}, f32[2,49,8,128]{3,2,1,0:T(8,128)S(1)}, u32[]{:S(2)}, u32[]{:S(2)}) collective-permute-start(f32[2,49,8,128]{3,2,1,0:T(8,128)} %get-tuple-element.70), channel_id=1, source_target_pairs={{0,6},{1,7},{2,0},{3,1},{4,2},{5,3},{6,4},{7,5},{8,14},{9,15},{10,... | collective-permute-start | bytes 1204232 | tf_op jit(solution)/shard_map/ppermute | solution.py:216
  25.2 21.0 %collective-permute-start.16 = (f32[2,49,8,128]{3,2,1,0:T(8,128)}, f32[2,49,8,128]{3,2,1,0:T(8,128)S(1)}, u32[]{:S(2)}, u32[]{:S(2)}) collective-permute-start(f32[2,49,8,128]{3,2,1,0:T(8,128)} %get-tuple-element.71), channel_id=1, source_target_pairs={{0,4},{1,5},{2,6},{3,7},{4,0},{5,1},{6,2},{7,3},{8,12},{9,13},{10,... | collective-permute-start | bytes 1204232 | tf_op jit(solution)/shard_map/ppermute | solution.py:216
  27.2 23.6 %collective-permute-start.17 = (f32[2,49,8,128]{3,2,1,0:T(8,128)}, f32[2,49,8,128]{3,2,1,0:T(8,128)S(1)}, u32[]{:S(2)}, u32[]{:S(2)}) collective-permute-start(f32[2,49,8,128]{3,2,1,0:T(8,128)} %get-tuple-element.72), channel_id=1, source_target_pairs={{0,3},{1,2},{2,5},{3,4},{4,7},{5,6},{6,1},{7,0},{8,11},{9,10},{10,... | collective-permute-start | bytes 1204232 | tf_op jit(solution)/shard_map/ppermute | solution.py:216
  29.3 30.2 %collective-permute-start.18 = (f32[2,49,8,128]{3,2,1,0:T(8,128)}, f32[2,49,8,128]{3,2,1,0:T(8,128)S(1)}, u32[]{:S(2)}, u32[]{:S(2)}) collective-permute-start(f32[2,49,8,128]{3,2,1,0:T(8,128)} %get-tuple-element.73), channel_id=1, source_target_pairs={{0,7},{1,6},{2,1},{3,0},{4,3},{5,2},{6,5},{7,4},{8,15},{9,14},{10,... | collective-permute-start | bytes 1204232 | tf_op jit(solution)/shard_map/ppermute | solution.py:216
  35.2 26.5 %collective-permute-start.19 = (f32[2,49,8,128]{3,2,1,0:T(8,128)}, f32[2,49,8,128]{3,2,1,0:T(8,128)S(1)}, u32[]{:S(2)}, u32[]{:S(2)}) collective-permute-start(f32[2,49,8,128]{3,2,1,0:T(8,128)} %get-tuple-element.74), channel_id=1, source_target_pairs={{0,5},{1,4},{2,7},{3,6},{4,1},{5,0},{6,3},{7,2},{8,13},{9,12},{10,... | collective-permute-start | bytes 1204232 | tf_op jit(solution)/shard_map/ppermute | solution.py:216
  42.4 22.3 %collective-permute-start.20 = (f32[2,49,8,128]{3,2,1,0:T(8,128)}, f32[2,49,8,128]{3,2,1,0:T(8,128)}, u32[]{:S(2)}, u32[]{:S(2)}) collective-permute-start(f32[2,49,8,128]{3,2,1,0:T(8,128)} %get-tuple-element.75), channel_id=1, source_target_pairs={{0,1},{1,0},{2,3},{3,2},{4,5},{5,4},{6,7},{7,6},{8,9},{9,8},{10,11... | collective-permute-start | bytes 1204232 | tf_op jit(solution)/shard_map/ppermute | solution.py:216
  46.2 23.1 %collective-permute-start.7 = (f32[2,49,8,128]{3,2,1,0:T(8,128)}, f32[2,49,8,128]{3,2,1,0:T(8,128)S(1)}, u32[]{:S(2)}, u32[]{:S(2)}) collective-permute-start(f32[2,49,8,128]{3,2,1,0:T(8,128)} %get-tuple-element.61), channel_id=1, source_target_pairs={{0,2},{1,3},{2,4},{3,5},{4,6},{5,7},{6,0},{7,1},{8,10},{9,11},{10,... | collective-permute-start | bytes 1204232 | tf_op jit(solution)/shard_map/ppermute | solution.py:216
  50.9 25.8 %collective-permute-start.8 = (f32[2,49,8,128]{3,2,1,0:T(8,128)}, f32[2,49,8,128]{3,2,1,0:T(8,128)S(1)}, u32[]{:S(2)}, u32[]{:S(2)}) collective-permute-start(f32[2,49,8,128]{3,2,1,0:T(8,128)} %get-tuple-element.62), channel_id=1, source_target_pairs={{0,6},{1,7},{2,0},{3,1},{4,2},{5,3},{6,4},{7,5},{8,14},{9,15},{10,... | collective-permute-start | bytes 1204232 | tf_op jit(solution)/shard_map/ppermute | solution.py:216
  59.5 19.5 %collective-permute-start.9 = (f32[2,49,8,128]{3,2,1,0:T(8,128)}, f32[2,49,8,128]{3,2,1,0:T(8,128)S(1)}, u32[]{:S(2)}, u32[]{:S(2)}) collective-permute-start(f32[2,49,8,128]{3,2,1,0:T(8,128)} %get-tuple-element.63), channel_id=1, source_target_pairs={{0,4},{1,5},{2,6},{3,7},{4,0},{5,1},{6,2},{7,3},{8,12},{9,13},{10,... | collective-permute-start | bytes 1204232 | tf_op jit(solution)/shard_map/ppermute | solution.py:216
  61.7 24.8 %collective-permute-start = (f32[2,49,8,128]{3,2,1,0:T(8,128)}, f32[2,49,8,128]{3,2,1,0:T(8,128)S(1)}, u32[]{:S(2)}, u32[]{:S(2)}) collective-permute-start(f32[2,49,8,128]{3,2,1,0:T(8,128)} %get-tuple-element.53), channel_id=1, source_target_pairs={{0,2},{1,3},{2,4},{3,5},{4,6},{5,7},{6,0},{7,1},{8,10},{9,11},{10,... | collective-permute-start | bytes 1204232 | tf_op jit(solution)/shard_map/ppermute | solution.py:216
  64.7 29.1 %collective-permute-start.1 = (f32[2,49,8,128]{3,2,1,0:T(8,128)}, f32[2,49,8,128]{3,2,1,0:T(8,128)S(1)}, u32[]{:S(2)}, u32[]{:S(2)}) collective-permute-start(f32[2,49,8,128]{3,2,1,0:T(8,128)} %get-tuple-element.54), channel_id=1, source_target_pairs={{0,6},{1,7},{2,0},{3,1},{4,2},{5,3},{6,4},{7,5},{8,14},{9,15},{10,... | collective-permute-start | bytes 1204232 | tf_op jit(solution)/shard_map/ppermute | solution.py:216
  69.3 36.7 %collective-permute-start.2 = (f32[2,49,8,128]{3,2,1,0:T(8,128)}, f32[2,49,8,128]{3,2,1,0:T(8,128)S(1)}, u32[]{:S(2)}, u32[]{:S(2)}) collective-permute-start(f32[2,49,8,128]{3,2,1,0:T(8,128)} %get-tuple-element.55), channel_id=1, source_target_pairs={{0,4},{1,5},{2,6},{3,7},{4,0},{5,1},{6,2},{7,3},{8,12},{9,13},{10,... | collective-permute-start | bytes 1204232 | tf_op jit(solution)/shard_map/ppermute | solution.py:216
  76.7 29.3 %collective-permute-start.3 = (f32[2,49,8,128]{3,2,1,0:T(8,128)}, f32[2,49,8,128]{3,2,1,0:T(8,128)S(1)}, u32[]{:S(2)}, u32[]{:S(2)}) collective-permute-start(f32[2,49,8,128]{3,2,1,0:T(8,128)} %get-tuple-element.56), channel_id=1, source_target_pairs={{0,3},{1,2},{2,5},{3,4},{4,7},{5,6},{6,1},{7,0},{8,11},{9,10},{10,... | collective-permute-start | bytes 1204232 | tf_op jit(solution)/shard_map/ppermute | solution.py:216
  79.0 27.0 %collective-permute-start.4 = (f32[2,49,8,128]{3,2,1,0:T(8,128)}, f32[2,49,8,128]{3,2,1,0:T(8,128)S(1)}, u32[]{:S(2)}, u32[]{:S(2)}) collective-permute-start(f32[2,49,8,128]{3,2,1,0:T(8,128)} %get-tuple-element.57), channel_id=1, source_target_pairs={{0,7},{1,6},{2,1},{3,0},{4,3},{5,2},{6,5},{7,4},{8,15},{9,14},{10,... | collective-permute-start | bytes 1204232 | tf_op jit(solution)/shard_map/ppermute | solution.py:216
  86.5 26.9 %collective-permute-start.5 = (f32[2,49,8,128]{3,2,1,0:T(8,128)}, f32[2,49,8,128]{3,2,1,0:T(8,128)S(1)}, u32[]{:S(2)}, u32[]{:S(2)}) collective-permute-start(f32[2,49,8,128]{3,2,1,0:T(8,128)} %get-tuple-element.58), channel_id=1, source_target_pairs={{0,5},{1,4},{2,7},{3,6},{4,1},{5,0},{6,3},{7,2},{8,13},{9,12},{10,... | collective-permute-start | bytes 1204232 | tf_op jit(solution)/shard_map/ppermute | solution.py:216
  93.8 19.5 %collective-permute-start.6 = (f32[2,49,8,128]{3,2,1,0:T(8,128)}, f32[2,49,8,128]{3,2,1,0:T(8,128)S(1)}, u32[]{:S(2)}, u32[]{:S(2)}) collective-permute-start(f32[2,49,8,128]{3,2,1,0:T(8,128)} %get-tuple-element.59), channel_id=1, source_target_pairs={{0,1},{1,0},{2,3},{3,2},{4,5},{5,4},{6,7},{7,6},{8,9},{9,8},{10,11... | collective-permute-start | bytes 1204232 | tf_op jit(solution)/shard_map/ppermute | solution.py:216
  124.8 21.9 %collective-permute-start.21 = (f32[49,16,128]{2,1,0:T(8,128)S(1)}, f32[49,16,128]{2,1,0:T(8,128)S(1)}, u32[]{:S(2)}, u32[]{:S(2)}) collective-permute-start(f32[49,16,128]{2,1,0:T(8,128)S(1)} %get-tuple-element.83), channel_id=1, source_target_pairs={{0,2},{1,3},{2,4},{3,5},{4,6},{5,7},{6,0},{7,1},{8,10},{9,11},{10,... | collective-permute-start | bytes 1204232 | tf_op jit(solution)/shard_map/ppermute | solution.py:216
  125.7 21.1 %collective-permute-start.22 = (f32[49,16,128]{2,1,0:T(8,128)S(1)}, f32[49,16,128]{2,1,0:T(8,128)S(1)}, u32[]{:S(2)}, u32[]{:S(2)}) collective-permute-start(f32[49,16,128]{2,1,0:T(8,128)S(1)} %get-tuple-element.84), channel_id=1, source_target_pairs={{0,6},{1,7},{2,0},{3,1},{4,2},{5,3},{6,4},{7,5},{8,14},{9,15},{10,... | collective-permute-start | bytes 1204232 | tf_op jit(solution)/shard_map/ppermute | solution.py:216
  128.1 25.8 %collective-permute-start.24 = (f32[49,16,128]{2,1,0:T(8,128)}, f32[49,16,128]{2,1,0:T(8,128)S(1)}, u32[]{:S(2)}, u32[]{:S(2)}) collective-permute-start(f32[49,16,128]{2,1,0:T(8,128)} %get-tuple-element.86), channel_id=1, source_target_pairs={{0,3},{1,2},{2,5},{3,4},{4,7},{5,6},{6,1},{7,0},{8,11},{9,10},{10,... | collective-permute-start | bytes 1204232 | tf_op jit(solution)/shard_map/ppermute | solution.py:216
  128.1 34.4 %collective-permute-start.25 = (f32[49,16,128]{2,1,0:T(8,128)}, f32[49,16,128]{2,1,0:T(8,128)S(1)}, u32[]{:S(2)}, u32[]{:S(2)}) collective-permute-start(f32[49,16,128]{2,1,0:T(8,128)} %get-tuple-element.87), channel_id=1, source_target_pairs={{0,7},{1,6},{2,1},{3,0},{4,3},{5,2},{6,5},{7,4},{8,15},{9,14},{10,... | collective-permute-start | bytes 1204232 | tf_op jit(solution)/shard_map/ppermute | solution.py:216
  (26 other events, 511.8 us)
